TPU v7x, 32 devices: a whole 2x2x4 slice. The times are simulated.
32 devices in a mesh: energy: 2 (over x), row: 4 (over z), col: 4 (over y, core).
Axes of the slice: x: 2, y: 2, z: 4, core: 2. Of those that a mesh axis runs over, the one named last changes fastest.
Arguments:
- object_field: float32 [2, 32, 1024, 1024], P(None, 'energy', 'row', 'col'), may hold values from -6 to 6
- probe_field: float32 [2, 32, 256, 256], P(None, 'energy'), may hold values from -5 to 5
- amplitudes: float32 [32, 4, 4, 4, 256, 256], P('energy', 'row', 'col'), may hold values from 0 to 3
- kk_kernel: float32 [2, 2, 32, 32], replicated, may hold values from -0.75 to 0.75
- offsets: int32 [4, 4, 4, 2], P('row', 'col'), may hold values from 0 to 128, as said below
Outputs:
- blended: float32 [2, 32, 1024, 1024], P(None, 'energy', 'row', 'col')
- new_probe: float32 [2, 32, 256, 256], P(None, 'energy')
Inputs may be any that keep to these rules, and one draw needn't show every extreme that they name: `offsets`: position k of every tile starts within 32 of 0 for k = 0, 1 and within 32 below 128 for k = 2, 3 in rows; in columns likewise, near 0 for even k and near the top for odd k.
All inputs are finite; a program needn't handle non-finite values.
Results may differ from a plain program's by a relative error of at most 0.0001.
Values sent between devices are 32-bit elements; how exact they have to be, the bound alone decides.
No kernel may reach another device: no remote copies, remote signals or barrier semaphores. Data moves between devices by JAX's collectives and lax.ppermute only.
A program may use at most 320 MiB of HBM per device.

v0:
```python
import math

import jax
import jax.numpy as jnp
from jax import lax
from jax.sharding import PartitionSpec as P

HALO = 64


PRECISE = lax.Precision.HIGHEST
STEP = 0.25
PROBE_STEP = 0.5
FLOOR = 0.25


def padded(cells, sides, width):
    for axis, dim in sides:
        count = lax.axis_size(axis)
        ends = count - 1
        head = lax.slice_in_dim(cells, 0, width, axis=dim)
        tail = lax.slice_in_dim(cells, cells.shape[dim] - width, cells.shape[dim], axis=dim)
        cells = jnp.concatenate(
            [
                lax.ppermute(tail, axis, [(i, (i + 1) % count) for i in range(ends)]),
                cells,
                lax.ppermute(head, axis, [((i + 1) % count, i) for i in range(ends)]),
            ],
            axis=dim,
        )
    return cells


def shifted(block, axis, distance):
    devices = range(lax.axis_size(axis))
    route = [(i - distance, i) for i in devices if i - distance in devices]
    return lax.ppermute(block, axis, route)


def dft_tables(length):
    counter = jnp.arange(length, dtype=jnp.int32)
    phases = counter[:, None] * counter[None, :] % length
    angles = phases.astype(jnp.float32) * (2.0 * math.pi / length)
    factor = 1.0 / math.sqrt(length)
    return (jnp.cos(angles) * factor, -jnp.sin(angles) * factor)


def left_product(cos_table, sin_table, real_part, imag_part):

    def multiply(matrix, field):
        return jnp.einsum("uv,evw->euw", matrix, field, precision=PRECISE)

    return (
        multiply(cos_table, real_part) - multiply(sin_table, imag_part),
        multiply(cos_table, imag_part) + multiply(sin_table, real_part),
    )


def right_product(cos_table, sin_table, real_part, imag_part):

    def multiply(field, matrix):
        return jnp.einsum("euv,vw->euw", field, matrix, precision=PRECISE)

    return (
        multiply(real_part, cos_table) - multiply(imag_part, sin_table),
        multiply(real_part, sin_table) + multiply(imag_part, cos_table),
    )


def transform(cos_table, sin_table, real_part, imag_part):
    real_part, imag_part = left_product(cos_table, sin_table, real_part, imag_part)
    return right_product(cos_table, sin_table, real_part, imag_part)


def position_update(window, probe_field, measured, cos_table, sin_table):
    probe_real, probe_imag = (probe_field[0], probe_field[1])
    window_real, window_imag = (window[0], window[1])
    exit_real = probe_real * window_real - probe_imag * window_imag
    exit_imag = probe_real * window_imag + probe_imag * window_real
    far_real, far_imag = transform(cos_table, sin_table, exit_real, exit_imag)
    modulus = jnp.sqrt(far_real * far_real + far_imag * far_imag)
    rescale = measured / jnp.maximum(modulus, FLOOR)
    back_real, back_imag = transform(cos_table, -sin_table, far_real * rescale, far_imag * rescale)
    diff_real = exit_real - back_real
    diff_imag = exit_imag - back_imag
    object_step = jnp.stack(
        [
            probe_real * diff_real + probe_imag * diff_imag,
            probe_real * diff_imag - probe_imag * diff_real,
        ]
    )
    probe_step = jnp.stack(
        [
            window_real * diff_real + window_imag * diff_imag,
            window_real * diff_imag - window_imag * diff_real,
        ]
    )
    return (object_step, probe_step)


def couple(kk_kernel, columns):
    return columns + jnp.einsum("abef,bfrc->aerc", kk_kernel, columns, precision=PRECISE)


def local(object_field, probe_field, amplitudes, kk_kernel, offsets):
    length = probe_field.shape[2]
    cos_table, sin_table = dft_tables(length)
    extended = padded(object_field, (("row", 2), ("col", 3)), HALO)
    gradient = jnp.zeros_like(extended)
    probe_grad = jnp.zeros_like(probe_field)
    anchor = jnp.zeros((), jnp.int32)
    for position in range(4):
        corner = (anchor, anchor, offsets[0, 0, position, 0], offsets[0, 0, position, 1])
        window = lax.dynamic_slice(extended, corner, probe_field.shape)
        object_step, probe_step = position_update(
            window, probe_field, amplitudes[:, 0, 0, position], cos_table, sin_table
        )
        current = lax.dynamic_slice(gradient, corner, probe_field.shape)
        gradient = lax.dynamic_update_slice(gradient, current + object_step, corner)
        probe_grad = probe_grad + probe_step
    edge = HALO
    top_rim = gradient[:, :, :edge, :]
    bottom_rim = gradient[:, :, -edge:, :]
    from_below = shifted(top_rim, "row", -1)
    from_above = shifted(bottom_rim, "row", 1)
    middle = gradient[:, :, edge:-edge, :]
    middle = jnp.concatenate(
        [
            middle[:, :, :edge] + from_above,
            middle[:, :, edge:-edge],
            middle[:, :, -edge:] + from_below,
        ],
        axis=2,
    )
    left_rim = middle[:, :, :, :edge]
    right_rim = middle[:, :, :, -edge:]
    from_right = shifted(left_rim, "col", -1)
    from_left = shifted(right_rim, "col", 1)
    interior = middle[:, :, :, edge:-edge]
    summed = jnp.concatenate(
        [
            interior[:, :, :, :edge] + from_left,
            interior[:, :, :, edge:-edge],
            interior[:, :, :, -edge:] + from_right,
        ],
        axis=3,
    )
    tiles = lax.axis_size("row") * lax.axis_size("col")
    probe_rate = PROBE_STEP / (4 * tiles)
    probe_total = lax.psum(probe_grad, ("row", "col"))
    new_probe = probe_field - probe_rate * probe_total
    stepped = object_field - STEP * summed
    blended = lax.all_to_all(
        couple(
            kk_kernel, lax.all_to_all(stepped, "energy", split_axis=2, concat_axis=1, tiled=True)
        ),
        "energy",
        split_axis=1,
        concat_axis=2,
        tiled=True,
    )
    return (blended, new_probe)


def solution(mesh):
    return jax.shard_map(
        local,
        mesh=mesh,
        in_specs=(
            P(None, "energy", "row", "col"),
            P(None, "energy", None, None),
            P("energy", "row", "col", None, None, None),
            P(),
            P("row", "col", None, None),
        ),
        out_specs=(P(None, "energy", "row", "col"), P(None, "energy", None, None)),
        check_vma=False,
    )
```

profile of v0, /device:TPU:0, one launch (start us, length us, event | category | flops | bytes accessed | tf_op | source)
XLA Modules:
  0.0 1732.8 jit_solution(3207014383232034888)
XLA Ops:
  16.5 43.4 %collective-permute-done = f32[2,16,64,256]{3,2,1,0:T(8,128)S(1)} collective-permute-done((f32[2,16,64,256]{3,2,1,0:T(8,128)S(1)}, f32[2,16,64,256]{3,2,1,0:T(8,128)S(1)}, u32[]{:S(2)}, u32[]{:S(2)}) %collective-permute-start) | collective-permute-done | bytes 2097184 | tf_op jit(solution)/shard_map/ppermute | solution.py:25
  66.8 11.2 fusion.547
  122.0 20.2 %pad_maximum_fusion = f32[2,16,384,384]{3,2,1,0:T(8,128)} fusion(f32[2,16,384,64]{3,2,1,0:T(8,128)} %copy.80, f32[2,16,384,256]{3,2,1,0:T(8,128)} %constant_dynamic-update-slice_fusion, f32[2,16,384,64]{3,2,1,0:T(8,128)} %copy.79), kind=kLoop, calls=%fused_computation | loop fusion | flops 9437184 | bytes 37748736 | tf_op jit(solution)/shard_map/concatenate | solution.py:23
  142.2 24.6 %fusion.85 = (f32[16,256,256]{2,1,0:T(8,128)S(1)}, f32[16,256,256]{2,1,0:T(8,128)}, f32[16,256,256]{2,1,0:T(8,128)}, f32[16,256,256]{2,1,0:T(8,128)}) fusion(f32[2,16,384,384]{3,2,1,0:T(8,128)} %pad_maximum_fusion, s32[]{:T(128)S(6)} %select_n.178, s32[]{:T(128)S(6)} %select_n.179, s32[]{:T(128)S(6)} %add.385, f32[2,16,256,256]{3,2,1,0:T(8,128)} %param.6, ...), kind=kLoop, calls=%fused_computation.125 | loop fusion | flops 12582912 | bytes 58720292 | tf_op jit(solution)/shard_map/sub | solution.py:78
  166.8 22.5 %fusion.86 = (f32[16,256,256]{2,1,0:T(8,128)S(1)}, f32[16,256,256]{2,1,0:T(8,128)}, f32[16,256,256]{2,1,0:T(8,128)}, f32[16,256,256]{2,1,0:T(8,128)}) fusion(f32[2,16,384,384]{3,2,1,0:T(8,128)} %pad_maximum_fusion, s32[]{:T(128)S(6)} %select_n.178, s32[]{:T(128)S(6)} %select_n.179, s32[]{:T(128)S(6)} %add.385, f32[2,16,256,256]{3,2,1,0:T(8,128)S(1)} %bitcast.568, ...), kind=kLoop, calls=%fused_computation.126 | loop fusion | flops 12582912 | bytes 58720292 | tf_op jit(solution)/shard_map/add | solution.py:79
  189.4 12.0 fusion.150
  240.7 10.5 fusion.11
  258.8 10.8 fusion.146
  306.1 10.6 fusion.45
  316.7 10.4 fusion.164
  337.4 10.7 convolution_add_fusion.7
  348.1 10.4 fusion.59
  368.8 10.5 fusion.152
  386.9 10.5 convolution_subtract_fusion.7
  397.4 10.9 convolution_subtract_fusion.1
  408.3 13.4 fusion.105
  421.7 10.5 fusion.108
  442.4 10.7 fusion.102
  460.6 10.5 fusion.114
  481.3 10.4 fusion.117
  491.8 31.6 %fusion.91 = (f32[16,256,256]{2,1,0:T(8,128)}, f32[16,256,256]{2,1,0:T(8,128)}, f32[16,256,256]{2,1,0:T(8,128)}, f32[16,256,256]{2,1,0:T(8,128)}, f32[16,256,256...) fusion(f32[16,256,256]{2,1,0:T(8,128)} %fusion.117, ...), kind=kOutput, calls=%fused_computation.157 | convolution fusion | flops 3252682752 | bytes 88080384 | tf_op jit(solution)/shard_map/euv,vw->euw/dot_general | solution.py:62
  523.4 12.2 fusion.167
  594.6 10.4 fusion.51
  635.8 10.7 convolution_add_fusion.4
  656.8 10.7 fusion.37
  688.0 10.5 convolution_add_fusion.2
  698.5 10.4 fusion.19
  709.0 10.6 fusion.21
  745.1 10.7 fusion.55
  766.0 10.9 fusion.39
  785.1 10.4 fusion.23
  795.6 22.0 %add_bitcast_fusion.3 = (f32[1,16,256,256]{3,2,1,0:T(8,128)}, f32[1,16,256,256]{3,2,1,0:T(8,128)}, f32[1,16,256,256]{3,2,1,0:T(8,128)}, f32[1,16,256,256]{3,2,1,0:T(8,128)}) fusion(f32[16,256,256]{2,1,0:T(8,128)S(1)} %copy-done.9, f32[16,256,256]{2,1,0:T(8,128)} %fusion.55, f32[16,256,256]{2,1,0:T(8,128)} %fusion.51, f32[16,256,256]{2,1,0:T(8,128)S(1)} %copy-done.11, ...), kind=kOutput, calls=%fused_computation.154 | convolution fusion | flops 3238985728 | bytes 58720268 | tf_op jit(solution)/shard_map/euv,vw->euw/dot_general | solution.py:62
  834.0 75.2 %dynamic_update_slice.12 = f32[2,16,384,384]{3,2,1,0:T(8,128)} dynamic-update-slice(f32[2,16,384,384]{3,2,1,0:T(8,128)} %broadcast_in_dim.2, f32[2,16,256,256]{3,2,1,0:T(8,128)} %pad_maximum_fusion.2, s32[]{:T(128)} %constant.10.clone.1, s32[]{:T(128)} %constant.10.clone.1, s32[]{:T(128)S(6)} %select_n.171, s32[]{:T(128)S(6)} %select_n.172) | dynamic-update-slice | bytes 16777220 | tf_op jit(solution)/shard_map/dynamic_update_slice | solution.py:119
  909.2 22.3 %add_bitcast_fusion.2 = (f32[1,16,256,256]{3,2,1,0:T(8,128)}, f32[1,16,256,256]{3,2,1,0:T(8,128)}, f32[1,16,256,256]{3,2,1,0:T(8,128)S(1)}, f32[1,16,256,256]{3,2,1,0:T(8,128)S(1)}) fusion(f32[16,256,256]{2,1,0:T(8,128)} %get-tuple-element.19, f32[16,256,256]{2,1,0:T(8,128)} %fusion.39, f32[16,256,256]{2,1,0:T(8,128)} %fusion.35, ...), kind=kOutput, calls=%fused_computation.152 | convolution fusion | flops 3238985728 | bytes 58720268 | tf_op jit(solution)/shard_map/euv,vw->euw/dot_general | solution.py:62
  939.5 85.4 %dynamic_update_slice.13 = f32[2,16,384,384]{3,2,1,0:T(8,128)} dynamic-update-slice(f32[2,16,384,384]{3,2,1,0:T(8,128)} %dynamic_update_slice.12, f32[2,16,256,256]{3,2,1,0:T(8,128)} %maximum_add_fusion, s32[]{:T(128)} %constant.10.clone.1, s32[]{:T(128)} %constant.10.clone.1, s32[]{:T(128)S(6)} %select_n.174, s32[]{:T(128)S(6)} %select_n.175) | dynamic-update-slice | bytes 16777220 | tf_op jit(solution)/shard_map/dynamic_update_slice | solution.py:119
  1025.0 22.1 %add_bitcast_fusion.1 = (f32[1,16,256,256]{3,2,1,0:T(8,128)}, f32[1,16,256,256]{3,2,1,0:T(8,128)}, f32[1,16,256,256]{3,2,1,0:T(8,128)S(1)}, f32[1,16,256,256]{3,2,1,0:T(8,128)S(1)}) fusion(f32[16,256,256]{2,1,0:T(8,128)} %get-tuple-element.25, f32[16,256,256]{2,1,0:T(8,128)} %fusion.23, f32[16,256,256]{2,1,0:T(8,128)} %fusion.19, ...), kind=kOutput, calls=%fused_computation.150 | convolution fusion | flops 3238985728 | bytes 58720268 | tf_op jit(solution)/shard_map/euv,vw->euw/dot_general | solution.py:62
  1055.1 80.1 %dynamic_update_slice.14 = f32[2,16,384,384]{3,2,1,0:T(8,128)} dynamic-update-slice(f32[2,16,384,384]{3,2,1,0:T(8,128)} %dynamic_update_slice.13, f32[2,16,256,256]{3,2,1,0:T(8,128)} %maximum_add_fusion.1, s32[]{:T(128)} %constant.10.clone.1, s32[]{:T(128)} %constant.10.clone.1, s32[]{:T(128)S(6)} %select_n.176, s32[]{:T(128)S(6)} %select_n.177) | dynamic-update-slice | bytes 16777220 | tf_op jit(solution)/shard_map/dynamic_update_slice | solution.py:119
  1135.2 21.8 %add_bitcast_fusion = (f32[1,16,256,256]{3,2,1,0:T(8,128)}, f32[1,16,256,256]{3,2,1,0:T(8,128)}, f32[1,16,256,256]{3,2,1,0:T(8,128)S(1)}, f32[1,16,256,256]{3,2,1,0:T(8,128)S(1)}) fusion(f32[16,256,256]{2,1,0:T(8,128)} %copy-done.4, f32[16,256,256]{2,1,0:T(8,128)} %fusion.7, f32[16,256,256]{2,1,0:T(8,128)} %fusion.3, f32[16,256,256]{2,1,0:T(8,128)} %copy-done.3, ...), kind=kOutput, calls=%fused_computation.148 | convolution fusion | flops 3238985728 | bytes 58720268 | tf_op jit(solution)/shard_map/euv,vw->euw/dot_general | solution.py:62
  1164.0 64.1 %dynamic_update_slice.15 = f32[2,16,384,384]{3,2,1,0:T(8,128)} dynamic-update-slice(f32[2,16,384,384]{3,2,1,0:T(8,128)} %dynamic_update_slice.14, f32[2,16,256,256]{3,2,1,0:T(8,128)} %maximum_add_fusion.2, s32[]{:T(128)} %constant.10.clone.1, s32[]{:T(128)} %constant.10.clone.1, s32[]{:T(128)S(6)} %select_n.178, s32[]{:T(128)S(6)} %select_n.179) | dynamic-update-slice | bytes 16777220 | tf_op jit(solution)/shard_map/dynamic_update_slice | solution.py:119
  1230.4 35.5 %collective-permute-start.4 = (f32[2,16,64,384]{3,2,1,0:T(8,128)S(1)}, f32[2,16,64,384]{3,2,1,0:T(8,128)S(1)}, u32[]{:S(2)}, u32[]{:S(2)}) collective-permute-start(f32[2,16,64,384]{3,2,1,0:T(8,128)S(1)} %slice.161), channel_id=1, source_target_pairs={{0,4},{4,8},{8,12},{1,5},{5,9},{9,13},{2,6},{6,10},{10,14},{3,7},{... | collective-permute-start | bytes 9437192 | tf_op jit(solution)/shard_map/ppermute | solution.py:37
  1265.8 57.2 %collective-permute-done.4 = f32[2,16,64,384]{3,2,1,0:T(8,128)S(1)} collective-permute-done((f32[2,16,64,384]{3,2,1,0:T(8,128)S(1)}, f32[2,16,64,384]{3,2,1,0:T(8,128)S(1)}, u32[]{:S(2)}, u32[]{:S(2)}) %collective-permute-start.4) | collective-permute-done | bytes 3145760 | tf_op jit(solution)/shard_map/ppermute | solution.py:37
  1331.4 61.1 %collective-permute-done.5 = f32[2,16,64,384]{3,2,1,0:T(8,128)S(1)} collective-permute-done((f32[2,16,64,384]{3,2,1,0:T(8,128)}, f32[2,16,64,384]{3,2,1,0:T(8,128)S(1)}, u32[]{:S(2)}, u32[]{:S(2)}) %collective-permute-start.5) | collective-permute-done | bytes 3145760 | tf_op jit(solution)/shard_map/ppermute | solution.py:37
  1409.2 13.5 collective-permute-start.6
  1443.2 23.5 %collective-permute-done.7 = f32[2,16,256,64]{2,3,1,0:T(8,128)} collective-permute-done((f32[2,16,256,64]{2,3,1,0:T(8,128)S(1)}, f32[2,16,256,64]{2,3,1,0:T(8,128)}, u32[]{:S(2)}, u32[]{:S(2)}) %collective-permute-start.7) | collective-permute-done | bytes 2097184 | tf_op jit(solution)/shard_map/ppermute | solution.py:37
  1498.4 15.7 fusion.2
  1514.1 56.3 %all-to-all-done = f32[2,16,256,256]{3,1,0,2:T(8,128)} async-done(((f32[2,16,256,256]{3,1,0,2:T(8,128)}), f32[2,16,256,256]{3,1,0,2:T(8,128)}, u32[]{:S(2)}, u32[]{:S(2)}) %all-to-all-start) | async-done | bytes 8388640 | tf_op jit(solution)/shard_map/all_to_all | solution.py:155
  1601.0 106.0 %all-reduce.2.cloned.1.call-done = f32[2,16,256,256]{3,2,1,0:T(8,128)} async-done(((f32[2,16,256,256]{3,2,1,0:T(8,128)}), f32[2,16,256,256]{3,2,1,0:T(8,128)}) %all-reduce.2.cloned.1.call-update) | async-done | bytes 8388624 | tf_op jit(solution)/shard_map/psum | solution.py:150
  1707.0 10.7 multiply_subtract_fusion
  (165 shorter events, 506.2 us)
Async XLA Ops:
  7.2 1567.7 %copy-start = (f32[2,2,32,32]{3,2,1,0:T(8,128)S(1)}, f32[2,2,32,32]{3,2,1,0:T(8,128)}, u32[]{:S(2)}) copy-start(f32[2,2,32,32]{3,2,1,0:T(8,128)} %param.8) | copy-start | bytes 49156
  7.2 54.3 %copy-start.12 = (f32[2,16,256,256]{3,2,1,0:T(8,128)S(1)}, f32[2,16,256,256]{3,2,1,0:T(8,128)}, u32[]{:S(2)}) copy-start(f32[2,16,256,256]{3,2,1,0:T(8,128)} %param.5) | copy-start | bytes 25165828
  9.9 50.1 %collective-permute-start = (f32[2,16,64,256]{3,2,1,0:T(8,128)S(1)}, f32[2,16,64,256]{3,2,1,0:T(8,128)S(1)}, u32[]{:S(2)}, u32[]{:S(2)}) collective-permute-start(f32[2,16,64,256]{3,2,1,0:T(8,128)S(1)} %get-tuple-element.55), channel_id=1, source_target_pairs={{0,4},{4,8},{8,12},{1,5},{5,9},{9,13},{2,6},{6,10},{10,14},{3,7},{... | collective-permute-start | bytes 6291464 | tf_op jit(solution)/shard_map/ppermute | solution.py:25
  15.2 50.1 %collective-permute-start.1 = (f32[2,16,64,256]{3,2,1,0:T(8,128)S(1)}, f32[2,16,64,256]{3,2,1,0:T(8,128)S(1)}, u32[]{:S(2)}, u32[]{:S(2)}) collective-permute-start(f32[2,16,64,256]{3,2,1,0:T(8,128)S(1)} %get-tuple-element.54), channel_id=1, source_target_pairs={{4,0},{8,4},{12,8},{5,1},{9,5},{13,9},{6,2},{10,6},{14,10},{7,3},{... | collective-permute-start | bytes 6291464 | tf_op jit(solution)/shard_map/ppermute | solution.py:27
  82.3 27.9 %collective-permute-start.3 = (f32[2,16,384,64]{2,3,1,0:T(8,128)S(1)}, f32[2,16,384,64]{2,3,1,0:T(8,128)}, u32[]{:S(2)}, u32[]{:S(2)}) collective-permute-start(f32[2,16,384,64]{2,3,1,0:T(8,128)S(1)} %copy.78), channel_id=1, source_target_pairs={{1,0},{2,1},{3,2},{5,4},{6,5},{7,6},{9,8},{10,9},{11,10},{13,12},{... | collective-permute-start | bytes 9437192 | tf_op jit(solution)/shard_map/ppermute | solution.py:27
  83.6 10.8 copy-start.35
  89.7 26.4 %collective-permute-start.2 = (f32[2,16,384,64]{2,3,1,0:T(8,128)}, f32[2,16,384,64]{2,3,1,0:T(8,128)}, u32[]{:S(2)}, u32[]{:S(2)}) collective-permute-start(f32[2,16,384,64]{2,3,1,0:T(8,128)} %copy.77), channel_id=1, source_target_pairs={{0,1},{1,2},{2,3},{4,5},{5,6},{6,7},{8,9},{9,10},{10,11},{12,13},{... | collective-permute-start | bytes 9437192 | tf_op jit(solution)/shard_map/ppermute | solution.py:25
  122.0 44.8 %slice-start = ((s8[8388608]{0:T(1024)(128)(4,1)}), s8[4194304]{0:T(1024)(128)(4,1)S(1)}, s32[]{:S(2)}) async-start(s8[8388608]{0:T(1024)(128)(4,1)} %bitcast.567), calls=%async_computation.3 | async-start | bytes 8388608
  142.2 24.6 %slice-start.1 = ((s8[8388608]{0:T(1024)(128)(4,1)}), s8[4194304]{0:T(1024)(128)(4,1)S(1)}, s32[]{:S(2)}) async-start(s8[8388608]{0:T(1024)(128)(4,1)} %bitcast.567), calls=%async_computation.4 | async-start | bytes 8388608
  166.8 230.6 %copy-start.3 = (f32[16,256,256]{2,1,0:T(8,128)}, f32[16,256,256]{2,1,0:T(8,128)S(1)}, u32[]{:S(2)}) copy-start(f32[16,256,256]{2,1,0:T(8,128)S(1)} %get-tuple-element.18) | copy-start | bytes 12582916
  189.3 69.5 %copy-start.4 = (f32[16,256,256]{2,1,0:T(8,128)}, f32[16,256,256]{2,1,0:T(8,128)S(1)}, u32[]{:S(2)}) copy-start(f32[16,256,256]{2,1,0:T(8,128)S(1)} %get-tuple-element.22) | copy-start | bytes 12582916
  189.3 12.0 copy-start.6
  258.8 10.9 copy-start.7
  269.7 10.3 copy-start.8
  306.1 10.6 copy-start.9
  316.7 10.4 copy-start.10
  368.8 10.5 copy-start.31
  408.3 73.1 %copy-start.17 = (f32[16,256,256]{2,1,0:T(8,128)}, f32[16,256,256]{2,1,0:T(8,128)S(1)}, u32[]{:S(2)}) copy-start(f32[16,256,256]{2,1,0:T(8,128)S(1)} %convolution_subtract_fusion.1) | copy-start | bytes 12582916
  408.3 13.4 copy-start.29
  421.7 10.5 copy-start.34
  432.2 10.2 copy-start.32
  442.4 10.7 copy-start.5
  442.4 10.7 copy-start.33
  523.4 154.3 %copy-start.19 = (f32[16,256,256]{2,1,0:T(8,128)}, f32[16,256,256]{2,1,0:T(8,128)S(1)}, u32[]{:S(2)}) copy-start(f32[16,256,256]{2,1,0:T(8,128)S(1)} %get-tuple-element.49) | copy-start | bytes 12582916
  523.4 12.2 copy-start.30
  561.1 10.4 copy-start.26
  571.5 7.6 copy-start.22
  605.0 10.2 copy-start.25
  615.3 10.4 copy-start.21
  656.8 10.8 copy-start.24
  709.0 10.6 copy-start.23
  727.1 10.4 copy-start.13
  745.1 10.7 copy-start.16
  745.1 10.7 copy-start.27
  755.8 21.1 %copy-start.28 = (f32[16,256,256]{2,1,0:T(8,128)S(1)}, f32[16,256,256]{2,1,0:T(8,128)}, u32[]{:S(2)}) copy-start(f32[16,256,256]{2,1,0:T(8,128)} %fusion.180) | copy-start | bytes 12582916
  766.0 11.0 copy-start.20
  766.0 29.6 %slice-start.2 = ((s8[8388608]{0:T(1024)(128)(4,1)}), s8[4194304]{0:T(1024)(128)(4,1)S(1)}, s32[]{:S(2)}) async-start(s8[8388608]{0:T(1024)(128)(4,1)} %bitcast.569), calls=%async_computation.5 | async-start | bytes 8388608
  777.0 18.6 %slice-start.3 = ((s8[8388608]{0:T(1024)(128)(4,1)}), s8[4194304]{0:T(1024)(128)(4,1)S(1)}, s32[]{:S(2)}) async-start(s8[8388608]{0:T(1024)(128)(4,1)} %bitcast.569), calls=%async_computation.6 | async-start | bytes 8388608
  785.1 10.4 copy-start.14
  785.1 10.4 copy-start.11
  1228.1 102.7 %copy-start.1 = (f32[2,16,384,384]{3,2,1,0:T(8,128)S(1)}, f32[2,16,384,384]{3,2,1,0:T(8,128)}, u32[]{:S(2)}) copy-start(f32[2,16,384,384]{3,2,1,0:T(8,128)} %dynamic_update_slice.15) | copy-start | bytes 56623108
  1230.4 92.7 %collective-permute-start.4 = (f32[2,16,64,384]{3,2,1,0:T(8,128)S(1)}, f32[2,16,64,384]{3,2,1,0:T(8,128)S(1)}, u32[]{:S(2)}, u32[]{:S(2)}) collective-permute-start(f32[2,16,64,384]{3,2,1,0:T(8,128)S(1)} %slice.161), channel_id=1, source_target_pairs={{0,4},{4,8},{8,12},{1,5},{5,9},{9,13},{2,6},{6,10},{10,14},{3,7},{... | collective-permute-start | bytes 9437192 | tf_op jit(solution)/shard_map/ppermute | solution.py:37
  1329.5 63.1 %collective-permute-start.5 = (f32[2,16,64,384]{3,2,1,0:T(8,128)}, f32[2,16,64,384]{3,2,1,0:T(8,128)S(1)}, u32[]{:S(2)}, u32[]{:S(2)}) collective-permute-start(f32[2,16,64,384]{3,2,1,0:T(8,128)} %get-tuple-element.43), channel_id=1, source_target_pairs={{4,0},{8,4},{12,8},{5,1},{9,5},{13,9},{6,2},{10,6},{14,10},{7,3},{... | collective-permute-start | bytes 9437192 | tf_op jit(solution)/shard_map/ppermute | solution.py:37
  1409.2 16.1 collective-permute-start.6
  1441.9 24.8 %collective-permute-start.7 = (f32[2,16,256,64]{2,3,1,0:T(8,128)S(1)}, f32[2,16,256,64]{2,3,1,0:T(8,128)}, u32[]{:S(2)}, u32[]{:S(2)}) collective-permute-start(f32[2,16,256,64]{2,3,1,0:T(8,128)S(1)} %copy.151), channel_id=1, source_target_pairs={{1,0},{2,1},{3,2},{5,4},{6,5},{7,6},{9,8},{10,9},{11,10},{13,12},{... | collective-permute-start | bytes 6291464 | tf_op jit(solution)/shard_map/ppermute | solution.py:37
  1491.2 79.1 %all-to-all-start = ((f32[2,16,256,256]{3,1,0,2:T(8,128)}), f32[2,16,256,256]{3,1,0,2:T(8,128)}, u32[]{:S(2)}, u32[]{:S(2)}) async-start(f32[2,16,256,256]{3,1,0,2:T(8,128)} %copy.153), calls=%async_computation | async-start | bytes 16777216 | tf_op jit(solution)/shard_map/all_to_all | solution.py:155
  1498.3 208.7 %all-reduce.2.cloned.1.call-start = ((), (), s32[]{:S(2)}) async-start(), calls=%async_computation.2 | async-start | bytes 16777216 | tf_op jit(solution)/shard_map/psum | solution.py:150
  1593.8 123.9 %all-to-all-start.1 = ((f32[2,32,128,256]{3,0,2,1:T(2,128)}), f32[2,32,128,256]{3,0,2,1:T(2,128)}, u32[]{:S(2)}, u32[]{:S(2)}) async-start(f32[2,32,128,256]{3,0,2,1:T(2,128)} %copy.155), calls=%async_computation.1 | async-start | bytes 16777216 | tf_op jit(solution)/shard_map/all_to_all | solution.py:153
  (4 other events, 18.4 us)
Sparse Core Ops, SparseCore 0:
  1514.2 192.7 all-reduce.1
where the time goes:
time: 1750 us; the launch traced here: 1730 us
  matrix products  701 us (40%)
  local copies, waits for them, and re-layouts  416 us (24%)
  waiting for transfers between devices  350 us (20%)
  other arithmetic  157 us (9%)
  starting transfers between devices  78.3 us (4%)
  between operations  30.1 us (2%)
    dot_general x32, matrix products, multiply(): return jnp.einsum('euv,vw->euw', field, matrix, precision=PRECISE)  397 us
    dynamic_update_slice x4, local copies, waits for them, and re-layouts, local(): gradient = lax.dynamic_update_slice(gradient, current + object_step, corner)  305 us
    dot_general x32, matrix products, multiply(): return jnp.einsum('uv,evw->euw', matrix, field, precision=PRECISE)  295 us
    ppermute x4, waiting for transfers between devices, shifted(): return lax.ppermute(block, axis, route)  144 us
    psum x1, waiting for transfers between devices, local(): probe_total = lax.psum(probe_grad, ('row', 'col'))  106 us
    all_to_all x1, waiting for transfers between devices, local(): lax.all_to_all(stepped, 'energy', split_axis=2, concat_axis=1, tiled=True)  56.3 us
    ppermute x4, starting transfers between devices, shifted(): return lax.ppermute(block, axis, route)  51.5 us
    ppermute x2, waiting for transfers between devices, padded(): lax.ppermute(tail, axis, [(i, (i + 1) % count) for i in range(ends)])  43.4 us
  transfers between devices with their start and end apart: 11, of which 7 were waited for; matrix products, arithmetic and copies ran while one was open for 4% of the time, Pallas kernels for 0%

commit v1 on v0

v1 whole, which is shorter than its diff:
```python
import math

import jax
import jax.numpy as jnp
import ml_dtypes
import numpy as np
from jax import lax
from jax.experimental import pallas as pl
from jax.experimental.pallas import tpu as pltpu
from jax.sharding import PartitionSpec as P

HALO = 64
LANES = 128
SUB = 8
STEP = 0.25
PROBE_STEP = 0.5
FLOOR = 0.25
PARTS = (2, 4, 5, 5)
VMEM = 56 * 2**20


def chunks_of(energies):
    if energies == sum(PARTS):
        sizes = PARTS
    else:
        sizes = (1,) * energies
    return [(sum(sizes[:i]), size) for i, size in enumerate(sizes)]


def split(x):
    hi = x.astype(jnp.bfloat16)
    return hi, (x - hi.astype(jnp.float32)).astype(jnp.bfloat16)


def dft_parts(length):
    half = length // 2
    pixel = np.arange(half)
    even = pixel - pixel % 2 + half * (pixel % 2)
    out = []
    for freqs in (even, even + 1):
        angle = (freqs[:, None] * pixel[None, :] % length) * (2.0 * math.pi / length)
        c, s = np.cos(angle) / math.sqrt(length), np.sin(angle) / math.sqrt(length)
        m = np.block([[c, s], [-s, c]])
        hi = m.astype(np.float32).astype(ml_dtypes.bfloat16)
        lo = (m - hi.astype(np.float64)).astype(np.float32).astype(ml_dtypes.bfloat16)
        out.append((hi, lo))
    even, odd = out
    wide = lambda m: np.concatenate([m[0], m[0], m[1]], axis=1)
    tall = lambda m: np.concatenate([m[0], m[0], m[1]], axis=0)
    t = lambda m: (m[0].T, m[1].T)
    left = np.stack([wide(even), wide(odd), wide(t(even)), wide(t(odd))])
    right = np.stack([tall(t(even)), tall(t(odd)), tall(even), tall(odd)])
    return left, right


def dot(a, b):
    return jnp.dot(a, b, preferred_element_type=jnp.float32)


def gradient_kernel(
    offs, obj, top, bot, lft, rgt, probe, amp, left, right, gout, gl, gr, pg, ext, grad
):
    win = probe.shape[2]
    tile = obj.shape[2]
    half = win // 2
    rows = tile + 2 * HALO
    mid = rows // 2
    lane = lax.broadcasted_iota(jnp.int32, (win, LANES), 1)
    for p in range(2):
        for j in range(tile // LANES):
            cols = slice(j * LANES, (j + 1) * LANES)
            ext[p, 1 + j, 0:HALO] = top[p, 0, :, cols]
            ext[p, 1 + j, HALO : HALO + tile] = obj[p, 0, :, cols]
            ext[p, 1 + j, HALO + tile : rows] = bot[p, 0, :, cols]
        packed = lft[p, 0]
        ext[p, 0, 0:mid] = pltpu.roll(packed, HALO, 1)
        ext[p, 0, mid:rows] = packed
        packed = rgt[p, 0]
        ext[p, 3, 0:mid] = packed
        ext[p, 3, mid:rows] = pltpu.roll(packed, HALO, 1)
    grad[...] = jnp.zeros_like(grad)
    pg[...] = jnp.zeros_like(pg)

    def window_of(k):
        a = offs[2 * k]
        b = offs[2 * k + 1] + HALO
        base = b // LANES
        r = b % LANES
        back = (LANES - r) % LANES
        return a, base, r, back

    def position(k):
        a, base, r, back = window_of(k)
        keep = lane < LANES - r
        def load(p):
            v = [pltpu.roll(ext[p, base + j, pl.ds(a, win), :], back, 1) for j in range(3)]
            return jnp.concatenate([jnp.where(keep, v[0], v[1]), jnp.where(keep, v[1], v[2])], axis=1)
        wr, wi = load(0), load(1)
        pr, pi = probe[0, 0], probe[1, 0]
        er = pr * wr - pi * wi
        ei = pr * wi + pi * wr

        def lmul(which, top_, bottom_):
            hi, lo = split(jnp.concatenate([top_, bottom_], axis=0))
            return dot(left[which], jnp.concatenate([hi, lo, hi], axis=0))

        def rmul(which, l_, r_):
            hi, lo = split(jnp.concatenate([l_, r_], axis=1))
            return dot(jnp.concatenate([hi, lo, hi], axis=1), right[which])

        ze = lmul(0, er[:half] + er[half:], ei[:half] + ei[half:])
        zo = lmul(1, er[:half] - er[half:], ei[:half] - ei[half:])
        zr = jnp.concatenate([ze[:half], zo[:half]], axis=0)
        zi = jnp.concatenate([ze[half:], zo[half:]], axis=0)
        ye = rmul(0, zr[:, :half] + zr[:, half:], zi[:, :half] + zi[:, half:])
        yo = rmul(1, zr[:, :half] - zr[:, half:], zi[:, :half] - zi[:, half:])
        meas = amp[0, 0, 0, k]
        groups = (half // 8, 8, win)
        mt, mb = meas[:half].reshape(groups), meas[half:].reshape(groups)
        odd_row = lax.broadcasted_iota(jnp.int32, groups, 1) % 2 == 1
        meas = jnp.concatenate(
            [
                jnp.where(odd_row, pltpu.roll(mb, 1, 1), mt).reshape(half, win),
                jnp.where(odd_row, mb, pltpu.roll(mt, 7, 1)).reshape(half, win),
            ],
            axis=0,
        )
        odd = lane % 2 == 1
        ml, mr = meas[:, :half], meas[:, half:]
        me = jnp.where(odd, pltpu.roll(mr, 1, 1), ml)
        mo = jnp.where(odd, mr, pltpu.roll(ml, LANES - 1, 1))

        def fix(y, m_):
            fr, fi = y[:, :half], y[:, half:]
            s = m_ * lax.rsqrt(jnp.maximum(fr * fr + fi * fi, FLOOR * FLOOR))
            return fr * s, fi * s

        te = rmul(2, *fix(ye, me))
        to = rmul(3, *fix(yo, mo))
        sr, dr = te[:, :half] + to[:, :half], te[:, :half] - to[:, :half]
        si, di = te[:, half:] + to[:, half:], te[:, half:] - to[:, half:]
        xr = jnp.concatenate([sr, dr], axis=1)
        xi = jnp.concatenate([si, di], axis=1)
        be = lmul(2, xr[:half], xi[:half])
        bo = lmul(3, xr[half:], xi[half:])
        br = jnp.concatenate([be[:half] + bo[:half], be[:half] - bo[:half]], axis=0)
        bi = jnp.concatenate([be[half:] + bo[half:], be[half:] - bo[half:]], axis=0)
        dr, di = er - br, ei - bi
        pg[0, 0] += wr * dr + wi * di
        pg[1, 0] += wr * di - wi * dr
        steps = (pr * dr + pi * di, pr * di - pi * dr)
        below = lane < r
        for p in range(2):
            u = pltpu.roll(steps[p][:, :LANES], r, 1)
            v = pltpu.roll(steps[p][:, LANES:], r, 1)
            grad[p, base, pl.ds(a, win), :] += jnp.where(below, 0.0, u)
            grad[p, base + 1, pl.ds(a, win), :] += jnp.where(below, u, v)
            grad[p, base + 2, pl.ds(a, win), :] += jnp.where(below, v, 0.0)

    for k in range(amp.shape[3]):
        position(k)
    first = lax.broadcasted_iota(jnp.int32, (mid, LANES), 1) < HALO
    for p in range(2):
        for j in range(tile // LANES):
            gout[p, 0, :, j * LANES : (j + 1) * LANES] = grad[p, 1 + j]
        edge = grad.at[p, 0]
        gl[p, 0] = jnp.where(first, pltpu.roll(edge[0:mid], HALO, 1), edge[mid:rows])
        edge = grad.at[p, 3]
        gr[p, 0] = jnp.where(first, edge[0:mid], pltpu.roll(edge[mid:rows], HALO, 1))


def params():
    return pltpu.CompilerParams(vmem_limit_bytes=VMEM)


def cost(flops, moved):
    return pl.CostEstimate(flops=int(flops), bytes_accessed=int(moved), transcendentals=0)


def plane(*shape):
    return pl.BlockSpec((2, 1) + shape, lambda e, *_: (0, e, 0, 0))


def later(first, *shape):
    return pl.BlockSpec((2, 1) + shape, lambda e, *_: (0, first + e, 0, 0))


def struct(*shape):
    return jax.ShapeDtypeStruct(shape, jnp.float32)


def gradient_call(offs, obj, top, bot, lft, rgt, probe, amp, left, right, first, count):
    win, tile = probe.shape[2], obj.shape[2]
    rows = tile + 2 * HALO
    side = (rows // 2, LANES)
    frame = pltpu.VMEM((2, tile // LANES + 2, rows, LANES), jnp.float32)
    whole = lambda m: pl.BlockSpec(m.shape, lambda e, *_: (0, 0, 0))
    return pl.pallas_call(
        gradient_kernel,
        grid_spec=pltpu.PrefetchScalarGridSpec(
            num_scalar_prefetch=1,
            grid=(count,),
            in_specs=[
                later(first, tile, tile),
                plane(HALO, tile),
                plane(HALO, tile),
                plane(*side),
                plane(*side),
                later(first, win, win),
                pl.BlockSpec((1, 1, 1) + amp.shape[3:], lambda e, *_: (first + e, 0, 0, 0, 0, 0)),
                whole(left),
                whole(right),
            ],
            out_specs=[plane(rows, tile), plane(*side), plane(*side), plane(win, win)],
            scratch_shapes=[frame, frame],
        ),
        out_shape=[
            struct(2, count, rows, tile),
            struct(2, count, *side),
            struct(2, count, *side),
            struct(2, count, win, win),
        ],
        compiler_params=params(),
        cost_estimate=cost(count * 7e9, count * 5e6),
    )(offs, obj, top, bot, lft, rgt, probe, amp, left, right)


def pack_kernel(near, far, top_near, top_far, bot_near, bot_far, left, right):
    tile = near.shape[2]
    mid = tile // 2
    for p in range(2):
        for refs, out, low in (
            ((top_near, near, bot_near), left, True),
            ((top_far, far, bot_far), right, False),
        ):
            body = refs[1][p, 0]
            upper = jnp.concatenate([refs[0][p, 0], body[:mid]], axis=0)
            lower = jnp.concatenate([body[mid:], refs[2][p, 0]], axis=0)
            lane = lax.broadcasted_iota(jnp.int32, upper.shape, 1)
            if low:
                out[p, 0] = jnp.where(lane < HALO, upper, pltpu.roll(lower, HALO, 1))
            else:
                out[p, 0] = jnp.where(lane < HALO, pltpu.roll(upper, HALO, 1), lower)


def pack_call(obj, top, bot, first, count):
    tile = obj.shape[2]
    last = tile // LANES - 1
    side = (tile // 2 + HALO, LANES)

    def lanes(rows, base, block):
        return pl.BlockSpec((2, 1, rows, LANES), lambda e: (0, base + e, 0, block))

    return pl.pallas_call(
        pack_kernel,
        grid=(count,),
        in_specs=[
            lanes(tile, first, 0),
            lanes(tile, first, last),
            lanes(HALO, 0, 0),
            lanes(HALO, 0, last),
            lanes(HALO, 0, 0),
            lanes(HALO, 0, last),
        ],
        out_specs=[plane(*side), plane(*side)],
        out_shape=[struct(2, count, *side)] * 2,
        compiler_params=params(),
        cost_estimate=cost(0, count * 12e5),
    )(obj, obj, top, top, bot, bot)


def from_left(packed, upper):
    lane = lax.broadcasted_iota(jnp.int32, packed.shape, 1)
    return jnp.where(lane < HALO, packed if upper else pltpu.roll(packed, HALO, 1), 0.0)


def from_right(packed, upper):
    lane = lax.broadcasted_iota(jnp.int32, packed.shape, 1)
    return jnp.where(lane < HALO, 0.0, pltpu.roll(packed, HALO, 1) if upper else packed)


def rim_kernel(g_top, g_bot, l_top, l_bot, r_top, r_bot, top, bot):
    for p in range(2):
        for g, l, r, out, upper in (
            (g_top, l_top, r_top, top, True),
            (g_bot, l_bot, r_bot, bot, False),
        ):
            out[p, 0] = g[p, 0]
            out[p, 0, :, :LANES] += from_left(l[p, 0], upper)
            out[p, 0, :, -LANES:] += from_right(r[p, 0], upper)


def rim_call(g, lft, rgt):
    count, rows, tile = g.shape[1:]

    def strip(block, width):
        return pl.BlockSpec((2, 1, HALO, width), lambda e: (0, e, block, 0))

    last = rows // HALO - 1
    packed_last = lft.shape[2] // HALO - 1
    return pl.pallas_call(
        rim_kernel,
        grid=(count,),
        in_specs=[
            strip(0, tile),
            strip(last, tile),
            strip(0, LANES),
            strip(packed_last, LANES),
            strip(0, LANES),
            strip(packed_last, LANES),
        ],
        out_specs=[plane(HALO, tile), plane(HALO, tile)],
        out_shape=[struct(2, count, HALO, tile)] * 2,
        compiler_params=params(),
        cost_estimate=cost(0, count * 8e5),
    )(g, g, lft, lft, rgt, rgt)


def step_kernel(obj, g, lft, rgt, above, below, out):
    tile = obj.shape[2]
    mid = tile // 2
    for p in range(2):
        l, r = lft[p, 0], rgt[p, 0]
        cols = (
            jnp.concatenate([from_left(l, True)[HALO:], from_left(l, False)[:mid]], axis=0),
            jnp.concatenate([from_right(r, True)[HALO:], from_right(r, False)[:mid]], axis=0),
        )
        for j, start in enumerate((0, tile - LANES)):
            span = slice(start, start + LANES)
            total = g[p, 0, HALO : HALO + tile, span] + cols[j]
            total = jnp.concatenate(
                [
                    total[:HALO] + above[p, 0, :, span],
                    total[HALO:-HALO],
                    total[-HALO:] + below[p, 0, :, span],
                ],
                axis=0,
            )
            out[p, 0, :, span] = obj[p, 0, :, span] - STEP * total


def step_call(obj, g, lft, rgt, above, below, first):
    tile = obj.shape[2]
    count, rows = g.shape[1:3]
    side = lft.shape[2:]
    return pl.pallas_call(
        step_kernel,
        grid=(count,),
        in_specs=[
            later(first, tile, tile),
            plane(rows, tile),
            plane(*side),
            plane(*side),
            plane(HALO, tile),
            plane(HALO, tile),
        ],
        out_specs=plane(tile, tile),
        out_shape=struct(2, count, tile, tile),
        compiler_params=params(),
        cost_estimate=cost(0, count * 25e5),
    )(obj, g, lft, rgt, above, below)


def probe_kernel(rate, probe, total, *rest):
    rest[-1][...] = probe[...] - rate * total[...]


def probe_call(probe, total, rate, first, running):
    win = probe.shape[2]
    count = total.shape[1]
    extra = [] if running is None else [running]
    return pl.pallas_call(
        lambda *refs: probe_kernel(rate, *refs),
        grid=(count,),
        in_specs=[later(first, win, win), plane(win, win)]
        + [pl.BlockSpec(memory_space=pl.ANY)] * len(extra),
        out_specs=later(first, win, win),
        out_shape=struct(*probe.shape),
        input_output_aliases={2: 0} if extra else {},
        compiler_params=params(),
        cost_estimate=cost(0, count * 16e5),
    )(probe, total, *extra)


def couple_kernel(weights, *refs):
    parts, out = refs[:-1], refs[-1]
    energies = out.shape[1]
    spans = chunks_of(energies)
    for g in range(out.shape[2] // SUB):
        rows = slice(g * SUB, (g + 1) * SUB)

        def flat(ref, q):
            x = ref[q, :, rows, :]
            return x.reshape(x.shape[0] * SUB, x.shape[2])

        own = [[flat(ref, q) for q in range(2)] for ref in parts[: len(spans)]]
        other = [[flat(ref, q) for q in range(2)] for ref in parts[len(spans) :]]
        hi, lo = split(jnp.concatenate([x for pair in own + other for x in pair], axis=0))
        mixed = dot(weights[...], jnp.concatenate([hi, lo, hi], axis=0))
        for (first, count), pair in zip(spans, own):
            for p in range(2):
                start = (p * energies + first) * SUB
                value = pair[p] + mixed[start : start + count * SUB]
                out[p, first : first + count, rows, :] = value.reshape(count, SUB, value.shape[1])


def couple_call(weights, parts, energies):
    tile = parts[0].shape[2]
    rows = 2 * SUB

    def block(count):
        return pl.BlockSpec((2, count, rows, tile), lambda i: (0, 0, i, 0))

    return pl.pallas_call(
        couple_kernel,
        grid=(tile // rows,),
        in_specs=[pl.BlockSpec(weights.shape, lambda i: (0, 0))]
        + [block(part.shape[1]) for part in parts],
        out_specs=block(energies),
        out_shape=struct(2, energies, tile, tile),
        compiler_params=params(),
        cost_estimate=cost(10e9, 26e6),
    )(weights, *parts)


def coupling_weights(kk_kernel, energies):
    count = lax.axis_size("energy")
    me = lax.axis_index("energy")
    mine = lax.dynamic_slice_in_dim(kk_kernel, me * energies, energies, axis=2)
    pieces = []
    for shift in range(count):
        source = (me - shift) % count
        block = lax.dynamic_slice_in_dim(mine, source * energies, energies, axis=3)
        block = block.transpose(0, 2, 1, 3)
        for first, size in chunks_of(energies):
            pieces.append(block[..., first : first + size].reshape(2 * energies, 2 * size))
    matrix = jnp.concatenate(pieces, axis=1)
    hi = lax.reduce_precision(matrix, 8, 7)
    matrix = jnp.concatenate([hi, hi, matrix - hi], axis=1)
    grown = matrix[:, None, :, None] * jnp.eye(SUB, dtype=jnp.float32)[None, :, None, :]
    return grown.reshape(matrix.shape[0] * SUB, matrix.shape[1] * SUB).astype(jnp.bfloat16)


def toward(block, axis, distance):
    count = lax.axis_size(axis)
    route = [(i, i + distance) for i in range(count) if 0 <= i + distance < count]
    return lax.ppermute(block, axis, route)


def local(object_field, probe_field, amplitudes, kk_kernel, offsets):
    energies = object_field.shape[1]
    ring = lax.axis_size("energy")
    tables = [jnp.asarray(m) for m in dft_parts(probe_field.shape[2])]
    offs = offsets.reshape(-1)
    weights = coupling_weights(kk_kernel, energies)
    rate = PROBE_STEP / (offsets.shape[2] * lax.axis_size("row") * lax.axis_size("col"))
    spans = chunks_of(energies)
    halos = []
    for first, count in spans:
        part = object_field[:, first : first + count]
        top = toward(part[:, :, -HALO:], "row", 1)
        bot = toward(part[:, :, :HALO], "row", -1)
        left, right = pack_call(object_field, top, bot, first, count)
        halos.append((top, bot, toward(right, "col", 1), toward(left, "col", -1)))
    own, other = [], [[] for _ in range(ring - 1)]
    new_probe = None
    totals = []
    for (first, count), halo in zip(spans, halos):
        g, g_left, g_right, probe_grad = gradient_call(
            offs, object_field, *halo, probe_field, amplitudes, *tables, first, count
        )
        totals.append(lax.psum(probe_grad, ("row", "col")))
        lft = toward(g_right, "col", 1)
        rgt = toward(g_left, "col", -1)
        top, bot = rim_call(g, lft, rgt)
        above = toward(bot, "row", 1)
        below = toward(top, "row", -1)
        stepped = step_call(object_field, g, lft, rgt, above, below, first)
        own.append(stepped)
        for shift in range(1, ring):
            route = [(i, (i + shift) % ring) for i in range(ring)]
            other[shift - 1].append(lax.ppermute(stepped, "energy", route))
    for (first, count), total in zip(spans, totals):
        new_probe = probe_call(probe_field, total, rate, first, new_probe)
    blended = couple_call(weights, own + [x for group in other for x in group], energies)
    return (blended, new_probe)


def solution(mesh):
    return jax.shard_map(
        local,
        mesh=mesh,
        in_specs=(
            P(None, "energy", "row", "col"),
            P(None, "energy", None, None),
            P("energy", "row", "col", None, None, None),
            P(),
            P("row", "col", None, None),
        ),
        out_specs=(P(None, "energy", "row", "col"), P(None, "energy", None, None)),
        check_vma=False,
    )
```

time: 1750 us -> 494 us (0.28)
  matrix products: 701 us -> 0 us
  local copies, waits for them, and re-layouts: 416 us -> 35.1 us
  waiting for transfers between devices: 350 us -> 136 us
  Pallas kernels: 0 us -> 209 us
  other arithmetic: 157 us -> 7.99 us
    dot_general x65 -> x0, matrix products: 701 us -> none  [the longest x32 397 us: multiply(): return jnp.einsum('euv,vw->euw', field, matrix, precision=PRECISE)]
    dynamic_update_slice x4 -> x0, local copies, waits for them, and re-layouts: 305 us -> none  [local(): gradient = lax.dynamic_update_slice(gradient, current + object_step, corner)]
    pallas_call x0 -> x21, Pallas kernels: none -> 209 us  [the longest x4 121 us: gradient_call(): pl.pallas_call(gradient_kernel, grid_spec=pltpu.PrefetchScalarGridSpec(nu...]
    ppermute x8 -> x36, waiting for transfers between devices: 188 us -> 80.7 us  [the longest x32 77.3 us: toward(): return lax.ppermute(block, axis, route)]
    add x9 -> x0, other arithmetic: 83.8 us -> none  [the longest x3 23 us: local(): gradient = lax.dynamic_update_slice(gradient, current + object_step, corner)]
    all_to_all x2 -> x0, waiting for transfers between devices: 56.3 us -> none  [the longest x1 56.3 us: local(): lax.all_to_all(stepped, 'energy', split_axis=2, concat_axis=1, tiled=True)]
    psum x1, waiting for transfers between devices: 106 us -> 55.3 us  [local(): totals.append(lax.psum(probe_grad, ('row', 'col')))]
    sub x3 -> x0, other arithmetic: 41.6 us -> none  [the longest x1 24.6 us: position_update(): exit_real = probe_real * window_real - probe_imag * window_imag]
  transfers between devices with their start and end apart: 11 -> 37, of which waited for: 7 -> 15; matrix products, arithmetic and copies ran while one was open for 4% -> 7% of each run, Pallas kernels for 0% -> 39%
where the time goes in v1:
time: 494 us; the launch traced here: 491 us
  Pallas kernels  209 us (42%)
  waiting for transfers between devices  136 us (28%)
  starting transfers between devices  88 us (18%)
  local copies, waits for them, and re-layouts  35.1 us (7%)
  between operations  14.8 us (3%)
  other arithmetic  7.99 us (2%)
    pallas_call x4, Pallas kernels, gradient_call(): pl.pallas_call(gradient_kernel, grid_spec=pltpu.PrefetchScalarGridSpec(nu...  121 us
    ppermute x32, starting transfers between devices, toward(): return lax.ppermute(block, axis, route)  81.7 us
    ppermute x32, waiting for transfers between devices, toward(): return lax.ppermute(block, axis, route)  77.3 us
    psum x1, waiting for transfers between devices, local(): totals.append(lax.psum(probe_grad, ('row', 'col')))  55.3 us
    pallas_call x4, Pallas kernels, step_call(): pl.pallas_call(step_kernel, grid=(count,), in_specs=[later(first, tile, t...  21.7 us
    convert_element_type x1, local copies, waits for them, and re-layouts, coupling_weights(): grown.reshape(matrix.shape[0] * SUB, matrix.shape[1] * SUB)  18.1 us
    pallas_call x1, Pallas kernels, couple_call(): pl.pallas_call(couple_kernel, grid=(tile // rows,), in_specs=[pl.BlockSpe...  18.1 us
    pallas_call x4, Pallas kernels, probe_call(): pl.pallas_call(lambda *refs: probe_kernel(rate, *refs), grid=(count,), in...  17.5 us
  transfers between devices with their start and end apart: 37, of which 15 were waited for; matrix products, arithmetic and copies ran while one was open for 7% of the time, Pallas kernels for 39%

profile of v1, /device:TPU:0, one launch (start us, length us, event | category | flops | bytes accessed | tf_op | source)
XLA Modules:
  0.0 491.3 jit_solution(11914999203391090124)
XLA Ops:
  8.5 5.0 %collective-permute-start.8 = (f32[2,4,64,256]{3,2,1,0:T(8,128)S(1)}, f32[2,4,64,256]{3,2,1,0:T(8,128)S(1)}, u32[]{:S(2)}, u32[]{:S(2)}) collective-permute-start(f32[2,4,64,256]{3,2,1,0:T(8,128)S(1)} %get-tuple-element.75), channel_id=1, source_target_pairs={{0,4},{4,8},{8,12},{1,5},{5,9},{9,13},{2,6},{6,10},{10,14},{3,7},{... | collective-permute-start | bytes 1572872 | tf_op jit(solution)/shard_map/ppermute | solution.py:447
  13.5 3.0 fusion.1
  16.5 3.5 collective-permute-start.16
  21.1 3.5 collective-permute-start
  27.1 17.1 %collective-permute-done.top_near.top_far.top = f32[2,2,64,256]{3,2,1,0:T(8,128)S(1)} collective-permute-done((f32[2,2,64,256]{3,2,1,0:T(8,128)S(1)}, f32[2,2,64,256]{3,2,1,0:T(8,128)S(1)}, u32[]{:S(2)}, u32[]{:S(2)}) %collective-permute-start) | collective-permute-done | bytes 262176 | tf_op jit(solution)/shard_map/ppermute | solution.py:447
  45.6 5.1 %collective-permute-start.24 = (f32[2,5,64,256]{3,2,1,0:T(8,128)}, f32[2,5,64,256]{3,2,1,0:T(8,128)S(1)}, u32[]{:S(2)}, u32[]{:S(2)}) collective-permute-start(f32[2,5,64,256]{3,2,1,0:T(8,128)} %get-tuple-element.71), channel_id=1, source_target_pairs={{0,4},{4,8},{8,12},{1,5},{5,9},{9,13},{2,6},{6,10},{10,14},{3,7},{... | collective-permute-start | bytes 1966088 | tf_op jit(solution)/shard_map/ppermute | solution.py:447
  57.8 4.1 shard_map.90
  61.9 2.6 collective-permute-done.17.bot_near.bot_far.bot
  64.5 3.1 collective-permute-start.10
  67.6 5.0 %shard_map.94 = (f32[2,5,192,128]{3,2,1,0:T(8,128)}, f32[2,5,192,128]{3,2,1,0:T(8,128)}) custom-call(f32[2,16,256,256]{3,2,1,0:T(8,128)} %obj.15, f32[2,16,256,256]{3,2,1,0:T(8,128)} %obj.15, f32[2,5,64,256]{3,2,1,0:T(8,128)} %copy-done.7, f32[2,5,64,256]{3,2,1,0:T(8,128)} %copy-done.7, f32[2,5,64,256]{3,2,1,0:T(8,128)} %copy-done.10, ...), custom_call_target="tpu_custom_call" | custom-call | bytes 6000000 | tf_op jit(solution)/shard_map/pallas_call | solution.py:254
  73.9 2.9 collective-permute-done.25.bot_near.bot_far.bot
  78.3 5.0 %shard_map.98 = (f32[2,5,192,128]{3,2,1,0:T(8,128)}, f32[2,5,192,128]{3,2,1,0:T(8,128)}) custom-call(f32[2,16,256,256]{3,2,1,0:T(8,128)} %obj.15, f32[2,16,256,256]{3,2,1,0:T(8,128)} %obj.15, f32[2,5,64,256]{3,2,1,0:T(8,128)} %copy-done.8, f32[2,5,64,256]{3,2,1,0:T(8,128)} %copy-done.8, f32[2,5,64,256]{3,2,1,0:T(8,128)} %copy-done.9, f32[2,5,64,256]{3,2,1,0:T(8,128)} %copy-done.9), custom_call_target="tpu_custom_call" | custom-call | bytes 6000000 | tf_op jit(solution)/shard_map/pallas_call | solution.py:254
  84.6 4.9 %collective-permute-start.26 = (f32[2,5,192,128]{3,2,1,0:T(8,128)}, f32[2,5,192,128]{3,2,1,0:T(8,128)S(1)}, u32[]{:S(2)}, u32[]{:S(2)}) collective-permute-start(f32[2,5,192,128]{3,2,1,0:T(8,128)} %get-tuple-element.55), channel_id=1, source_target_pairs={{0,1},{1,2},{2,3},{4,5},{5,6},{6,7},{8,9},{9,10},{10,11},{12,13},{... | collective-permute-start | bytes 2949128 | tf_op jit(solution)/shard_map/ppermute | solution.py:447
  89.6 17.3 %shard_map.87 = (f32[2,2,384,256]{3,2,1,0:T(8,128)}, f32[2,2,192,128]{3,2,1,0:T(8,128)}, f32[2,2,192,128]{3,2,1,0:T(8,128)}, f32[2,2,256,256]{3,2,1,0:T(8,128)}) custom-call(s32[8]{0:T(128)} %reshape.53.offs, f32[2,16,256,256]{3,2,1,0:T(8,128)} %obj.15, f32[2,2,64,256]{3,2,1,0:T(8,128)} %copy-done.13, f32[2,2,64,256]{3,2,1,0:T(8,128)} %copy-done.14, ...), custom_call_target="tpu_custom_call" | custom-call | flops 14000000000 | bytes 10000000 | tf_op jit(solution)/shard_map/pallas_call | solution.py:198
  109.4 36.5 %shard_map.95 = (f32[2,5,384,256]{3,2,1,0:T(8,128)}, f32[2,5,192,128]{3,2,1,0:T(8,128)}, f32[2,5,192,128]{3,2,1,0:T(8,128)}, f32[2,5,256,256]{3,2,1,0:T(8,128)}) custom-call(s32[8]{0:T(128)} %reshape.53.offs, f32[2,16,256,256]{3,2,1,0:T(8,128)} %obj.15, f32[2,5,64,256]{3,2,1,0:T(8,128)} %copy-done.7, f32[2,5,64,256]{3,2,1,0:T(8,128)} %copy-done.10, ...), custom_call_target="tpu_custom_call" | custom-call | flops 35000000512 | bytes 25000000 | tf_op jit(solution)/shard_map/pallas_call | solution.py:198
  145.9 4.8 collective-permute-start.20
  152.1 36.6 %shard_map.99 = (f32[2,5,384,256]{3,2,1,0:T(8,128)}, f32[2,5,192,128]{3,2,1,0:T(8,128)}, f32[2,5,192,128]{3,2,1,0:T(8,128)}, f32[2,5,256,256]{3,2,1,0:T(8,128)}) custom-call(s32[8]{0:T(128)} %reshape.53.offs, f32[2,16,256,256]{3,2,1,0:T(8,128)} %obj.15, f32[2,5,64,256]{3,2,1,0:T(8,128)} %copy-done.8, f32[2,5,64,256]{3,2,1,0:T(8,128)} %copy-done.9, ...), custom_call_target="tpu_custom_call" | custom-call | flops 35000000512 | bytes 25000000 | tf_op jit(solution)/shard_map/pallas_call | solution.py:198
  188.7 4.9 collective-permute-start.28
  195.1 30.3 %shard_map.91 = (f32[2,4,384,256]{3,2,1,0:T(8,128)}, f32[2,4,192,128]{3,2,1,0:T(8,128)}, f32[2,4,192,128]{3,2,1,0:T(8,128)}, f32[2,4,256,256]{3,2,1,0:T(8,128)}) custom-call(s32[8]{0:T(128)} %reshape.53.offs, f32[2,16,256,256]{3,2,1,0:T(8,128)} %obj.15, f32[2,4,64,256]{3,2,1,0:T(8,128)} %copy-done.11, f32[2,4,64,256]{3,2,1,0:T(8,128)} %copy-done.12, ...), custom_call_target="tpu_custom_call" | custom-call | flops 28000000000 | bytes 20000000 | tf_op jit(solution)/shard_map/pallas_call | solution.py:198
  225.4 4.8 collective-permute-start.12
  232.5 4.7 shard_map.96
  237.3 2.8 collective-permute-start.22
  241.4 4.6 shard_map.100
  246.0 4.6 collective-permute-start.30
  252.8 3.7 shard_map.92
  256.5 4.6 collective-permute-start.14
  261.1 8.0 %collective-permute-done.22.above = f32[2,5,64,256]{3,2,1,0:T(8,128)S(1)} collective-permute-done((f32[2,5,64,256]{3,2,1,0:T(8,128)}, f32[2,5,64,256]{3,2,1,0:T(8,128)S(1)}, u32[]{:S(2)}, u32[]{:S(2)}) %collective-permute-start.22) | collective-permute-done | bytes 655392 | tf_op jit(solution)/shard_map/ppermute | solution.py:447
  270.4 3.4 collective-permute-done.23.below
  274.7 6.7 %shard_map.97.refs_2_ = f32[2,5,256,256]{3,2,1,0:T(8,128)} custom-call(f32[2,16,256,256]{3,2,1,0:T(8,128)} %obj.15, f32[2,5,384,256]{3,2,1,0:T(8,128)} %get-tuple-element.50.g_top.g_bot.g, f32[2,5,192,128]{3,2,1,0:T(8,128)} %copy-done, f32[2,5,192,128]{3,2,1,0:T(8,128)} %copy-done.1, f32[2,5,64,256]{3,2,1,0:T(8,128)} %copy-done.15, f32[2,5,64,256]{3,2,1,0:T(8,128)} %copy-done.17), custom_call_target="tpu_custom_call" | custom-call | bytes 12500000 | tf_op jit(solution)/shard_map/pallas_call | solution.py:346
  282.8 14.4 %collective-permute-done.30.above = f32[2,5,64,256]{3,2,1,0:T(8,128)S(1)} collective-permute-done((f32[2,5,64,256]{3,2,1,0:T(8,128)}, f32[2,5,64,256]{3,2,1,0:T(8,128)S(1)}, u32[]{:S(2)}, u32[]{:S(2)}) %collective-permute-start.30) | collective-permute-done | bytes 655392 | tf_op jit(solution)/shard_map/ppermute | solution.py:447
  297.2 4.7 collective-permute-done.31.below
  302.8 6.7 %shard_map.101.refs_3_ = f32[2,5,256,256]{3,2,1,0:T(8,128)} custom-call(f32[2,16,256,256]{3,2,1,0:T(8,128)} %obj.15, f32[2,5,384,256]{3,2,1,0:T(8,128)} %get-tuple-element.57.g_top.g_bot.g, f32[2,5,192,128]{3,2,1,0:T(8,128)} %copy-done.2, f32[2,5,192,128]{3,2,1,0:T(8,128)} %collective-permute-done.29.r_top.r_bot.rgt, f32[2,5,64,256]{3,2,1,0:T(8,128)} %copy-done.16, ...), custom_call_target="tpu_custom_call" | custom-call | bytes 12500000 | tf_op jit(solution)/shard_map/pallas_call | solution.py:346
  311.0 8.7 %collective-permute-done.14.above = f32[2,4,64,256]{3,2,1,0:T(8,128)S(1)} collective-permute-done((f32[2,4,64,256]{3,2,1,0:T(8,128)}, f32[2,4,64,256]{3,2,1,0:T(8,128)S(1)}, u32[]{:S(2)}, u32[]{:S(2)}) %collective-permute-start.14) | collective-permute-done | bytes 524320 | tf_op jit(solution)/shard_map/ppermute | solution.py:447
  319.7 4.7 collective-permute-done.15.below
  325.2 5.2 %shard_map.93.refs_1_ = f32[2,4,256,256]{3,2,1,0:T(8,128)} custom-call(f32[2,16,256,256]{3,2,1,0:T(8,128)} %obj.15, f32[2,4,384,256]{3,2,1,0:T(8,128)} %get-tuple-element.43.g_top.g_bot.g, f32[2,4,192,128]{3,2,1,0:T(8,128)} %copy-done.3, f32[2,4,192,128]{3,2,1,0:T(8,128)} %copy-done.4, f32[2,4,64,256]{3,2,1,0:T(8,128)} %copy-done.19, ...), custom_call_target="tpu_custom_call" | custom-call | bytes 10000000 | tf_op jit(solution)/shard_map/pallas_call | solution.py:346
  331.9 2.5 collective-permute-start.4
  335.9 4.6 collective-permute-done.5.r_top.r_bot.rgt
  343.3 3.5 collective-permute-start.6
  351.0 4.0 collective-permute-done.6.above
  357.7 3.1 shard_map.89.refs_0_
  362.6 7.9 %multiply_convert_fusion = bf16[32,8,192,8]{3,2,1,0:T(8,128)(2,1)} fusion(f32[8,8]{1,0:T(8,128)S(1)} %fusion, f32[32,192]{1,0:T(8,128)S(1)} %pad_maximum_fusion), kind=kLoop, calls=%fused_computation | loop fusion | flops 786432 | bytes 811264 | tf_op jit(solution)/shard_map/convert_element_type | solution.py:441
  370.5 18.1 %convert_element_type.14.weights = bf16[256,1536]{1,0:T(8,128)(2,1)} reshape(bf16[32,8,192,8]{3,2,1,0:T(8,128)(2,1)} %multiply_convert_fusion) | data formatting | bytes 1572864 | tf_op jit(solution)/shard_map/convert_element_type | solution.py:441
  388.7 55.3 %all-reduce.3.cloned.1.call-done = (f32[2,5,256,256]{3,2,1,0:T(8,128)}, f32[2,5,256,256]{3,2,1,0:T(8,128)}, f32[2,4,256,256]{3,2,1,0:T(8,128)}, f32[2,2,256,256]{3,2,1,0:T(8,128)}) async-done(((f32[2,5,256,256]{3,2,1,0:T(8,128)}, f32[2,5,256,256]{3,2,1,0:T(8,128)}, f32[2,4,256,256]{3,2,1,0:T(8,128)}, f32[2,2,256,256]{3,2,1,0:T(8,128)}), (f32[2,5,256,256]{3,2,1,0:T(8,128)}, f32[2,5,256,256]{3,2,1,0:T(8,128)}, ...) | async-done | bytes 8388624 | tf_op jit(solution)/shard_map/psum | solution.py:472
  446.4 4.2 shard_map.104.refs_2_
  450.5 5.5 %shard_map.105.refs_2_ = f32[2,16,256,256]{3,2,1,0:T(8,128)} custom-call(f32[2,16,256,256]{3,2,1,0:T(8,128)} %refs_0_.7, f32[2,5,256,256]{3,2,1,0:T(8,128)} %get-tuple-element.67.refs_1_, f32[2,16,256,256]{3,2,1,0:T(8,128)} %shard_map.104.refs_2_), custom_call_target="tpu_custom_call", output_to_operand_aliasing={{}: (2, {})} | custom-call | bytes 8000000 | tf_op jit(solution)/shard_map/pallas_call | solution.py:372
  456.0 5.5 %shard_map.106 = f32[2,16,256,256]{3,2,1,0:T(8,128)} custom-call(f32[2,16,256,256]{3,2,1,0:T(8,128)} %refs_0_.7, f32[2,5,256,256]{3,2,1,0:T(8,128)} %get-tuple-element.66.refs_1_, f32[2,16,256,256]{3,2,1,0:T(8,128)} %shard_map.105.refs_2_), custom_call_target="tpu_custom_call", output_to_operand_aliasing={{}: (2, {})} | custom-call | bytes 8000000 | tf_op jit(solution)/shard_map/pallas_call | solution.py:372
  461.5 3.4 collective-permute-done.32.refs_4_
  466.4 18.1 %shard_map.102 = f32[2,16,256,256]{3,2,1,0:T(8,128)} custom-call(bf16[256,1536]{1,0:T(8,128)(2,1)} %convert_element_type.14.weights, f32[2,2,256,256]{3,2,1,0:T(8,128)} %shard_map.89.refs_0_, f32[2,4,256,256]{3,2,1,0:T(8,128)} %shard_map.93.refs_1_, f32[2,5,256,256]{3,2,1,0:T(8,128)} %shard_map.97.refs_2_, f32[2,5,256,256]{3,2,1,0:T(8,128)} %shard_map.101.refs_3_, ...), custom_call_target="tpu_custom_call" | custom-call | flops 10000000000 | bytes 26000000 | tf_op jit(solution)/shard_map/pallas_call | solution.py:414
  (151 shorter events, 53.5 us)
Async XLA Ops:
  7.2 436.8 %all-reduce.3.cloned.1.call-start = ((), (), s32[]{:S(2)}) async-start(), calls=%async_computation | async-start | bytes 16777216 | tf_op jit(solution)/shard_map/psum | solution.py:472
  8.5 42.1 %collective-permute-start.8 = (f32[2,4,64,256]{3,2,1,0:T(8,128)S(1)}, f32[2,4,64,256]{3,2,1,0:T(8,128)S(1)}, u32[]{:S(2)}, u32[]{:S(2)}) collective-permute-start(f32[2,4,64,256]{3,2,1,0:T(8,128)S(1)} %get-tuple-element.75), channel_id=1, source_target_pairs={{0,4},{4,8},{8,12},{1,5},{5,9},{9,13},{2,6},{6,10},{10,14},{3,7},{... | collective-permute-start | bytes 1572872 | tf_op jit(solution)/shard_map/ppermute | solution.py:447
  16.5 39.3 %collective-permute-start.16 = (f32[2,5,64,256]{3,2,1,0:T(8,128)S(1)}, f32[2,5,64,256]{3,2,1,0:T(8,128)S(1)}, u32[]{:S(2)}, u32[]{:S(2)}) collective-permute-start(f32[2,5,64,256]{3,2,1,0:T(8,128)S(1)} %get-tuple-element.73), channel_id=1, source_target_pairs={{0,4},{4,8},{8,12},{1,5},{5,9},{9,13},{2,6},{6,10},{10,14},{3,7},{... | collective-permute-start | bytes 1966088 | tf_op jit(solution)/shard_map/ppermute | solution.py:447
  21.1 23.2 %collective-permute-start = (f32[2,2,64,256]{3,2,1,0:T(8,128)S(1)}, f32[2,2,64,256]{3,2,1,0:T(8,128)S(1)}, u32[]{:S(2)}, u32[]{:S(2)}) collective-permute-start(f32[2,2,64,256]{3,2,1,0:T(8,128)S(1)} %get-tuple-element.77), channel_id=1, source_target_pairs={{0,4},{4,8},{8,12},{1,5},{5,9},{9,13},{2,6},{6,10},{10,14},{3,7},{... | collective-permute-start | bytes 786440 | tf_op jit(solution)/shard_map/ppermute | solution.py:447
  24.5 21.0 %collective-permute-start.1 = (f32[2,2,64,256]{3,2,1,0:T(8,128)S(1)}, f32[2,2,64,256]{3,2,1,0:T(8,128)S(1)}, u32[]{:S(2)}, u32[]{:S(2)}) collective-permute-start(f32[2,2,64,256]{3,2,1,0:T(8,128)S(1)} %get-tuple-element.76), channel_id=1, source_target_pairs={{4,0},{8,4},{12,8},{5,1},{9,5},{13,9},{6,2},{10,6},{14,10},{7,3},{... | collective-permute-start | bytes 786440 | tf_op jit(solution)/shard_map/ppermute | solution.py:447
  25.8 28.6 %collective-permute-start.9 = (f32[2,4,64,256]{3,2,1,0:T(8,128)S(1)}, f32[2,4,64,256]{3,2,1,0:T(8,128)S(1)}, u32[]{:S(2)}, u32[]{:S(2)}) collective-permute-start(f32[2,4,64,256]{3,2,1,0:T(8,128)S(1)} %get-tuple-element.74), channel_id=1, source_target_pairs={{4,0},{8,4},{12,8},{5,1},{9,5},{13,9},{6,2},{10,6},{14,10},{7,3},{... | collective-permute-start | bytes 1572872 | tf_op jit(solution)/shard_map/ppermute | solution.py:447
  44.3 7.8 %copy-start.13 = (f32[2,2,64,256]{3,2,1,0:T(8,128)}, f32[2,2,64,256]{3,2,1,0:T(8,128)S(1)}, u32[]{:S(2)}) copy-start(f32[2,2,64,256]{3,2,1,0:T(8,128)S(1)} %collective-permute-done.top_near.top_far.top) | copy-start | bytes 786436
  44.3 20.2 %collective-permute-start.17 = (f32[2,5,64,256]{3,2,1,0:T(8,128)}, f32[2,5,64,256]{3,2,1,0:T(8,128)S(1)}, u32[]{:S(2)}, u32[]{:S(2)}) collective-permute-start(f32[2,5,64,256]{3,2,1,0:T(8,128)} %get-tuple-element.72), channel_id=1, source_target_pairs={{4,0},{8,4},{12,8},{5,1},{9,5},{13,9},{6,2},{10,6},{14,10},{7,3},{... | collective-permute-start | bytes 1966088 | tf_op jit(solution)/shard_map/ppermute | solution.py:447
  45.6 6.5 %copy-start.14 = (f32[2,2,64,256]{3,2,1,0:T(8,128)}, f32[2,2,64,256]{3,2,1,0:T(8,128)S(1)}, u32[]{:S(2)}) copy-start(f32[2,2,64,256]{3,2,1,0:T(8,128)S(1)} %collective-permute-done.1.bot_near.bot_far.bot) | copy-start | bytes 786436
  45.6 27.0 %collective-permute-start.24 = (f32[2,5,64,256]{3,2,1,0:T(8,128)}, f32[2,5,64,256]{3,2,1,0:T(8,128)S(1)}, u32[]{:S(2)}, u32[]{:S(2)}) collective-permute-start(f32[2,5,64,256]{3,2,1,0:T(8,128)} %get-tuple-element.71), channel_id=1, source_target_pairs={{0,4},{4,8},{8,12},{1,5},{5,9},{9,13},{2,6},{6,10},{10,14},{3,7},{... | collective-permute-start | bytes 1966088 | tf_op jit(solution)/shard_map/ppermute | solution.py:447
  50.7 6.4 %copy-start.24 = (s32[1,1,4,2]{2,3,1,0:T(2,128)S(1)}, s32[1,1,4,2]{2,3,1,0:T(2,128)}, u32[]{:S(2)}) copy-start(s32[1,1,4,2]{2,3,1,0:T(2,128)} %param.11) | copy-start | bytes 100
  50.7 26.1 %collective-permute-start.25 = (f32[2,5,64,256]{3,2,1,0:T(8,128)}, f32[2,5,64,256]{3,2,1,0:T(8,128)S(1)}, u32[]{:S(2)}, u32[]{:S(2)}) collective-permute-start(f32[2,5,64,256]{3,2,1,0:T(8,128)} %get-tuple-element.70), channel_id=1, source_target_pairs={{4,0},{8,4},{12,8},{5,1},{9,5},{13,9},{6,2},{10,6},{14,10},{7,3},{... | collective-permute-start | bytes 1966088 | tf_op jit(solution)/shard_map/ppermute | solution.py:447
  54.4 28.8 %collective-permute-start.2 = (f32[2,2,192,128]{3,2,1,0:T(8,128)}, f32[2,2,192,128]{3,2,1,0:T(8,128)S(1)}, u32[]{:S(2)}, u32[]{:S(2)}) collective-permute-start(f32[2,2,192,128]{3,2,1,0:T(8,128)} %get-tuple-element.34), channel_id=1, source_target_pairs={{0,1},{1,2},{2,3},{4,5},{5,6},{6,7},{8,9},{9,10},{10,11},{12,13},{... | collective-permute-start | bytes 1179656 | tf_op jit(solution)/shard_map/ppermute | solution.py:447
  55.8 6.1 %copy-start.7 = (f32[2,5,64,256]{3,2,1,0:T(8,128)}, f32[2,5,64,256]{3,2,1,0:T(8,128)S(1)}, u32[]{:S(2)}) copy-start(f32[2,5,64,256]{3,2,1,0:T(8,128)S(1)} %collective-permute-done.16.top_near.top_far.top) | copy-start | bytes 1966084
  55.8 28.8 %collective-permute-start.3 = (f32[2,2,192,128]{3,2,1,0:T(8,128)}, f32[2,2,192,128]{3,2,1,0:T(8,128)}, u32[]{:S(2)}, u32[]{:S(2)}) collective-permute-start(f32[2,2,192,128]{3,2,1,0:T(8,128)} %get-tuple-element.35), channel_id=1, source_target_pairs={{1,0},{2,1},{3,2},{5,4},{6,5},{7,6},{9,8},{10,9},{11,10},{13,12},{... | collective-permute-start | bytes 1179656 | tf_op jit(solution)/shard_map/ppermute | solution.py:447
  64.5 129.1 %collective-permute-start.10 = (f32[2,4,192,128]{3,2,1,0:T(8,128)}, f32[2,4,192,128]{3,2,1,0:T(8,128)}, u32[]{:S(2)}, u32[]{:S(2)}) collective-permute-start(f32[2,4,192,128]{3,2,1,0:T(8,128)} %get-tuple-element.41), channel_id=1, source_target_pairs={{0,1},{1,2},{2,3},{4,5},{5,6},{6,7},{8,9},{9,10},{10,11},{12,13},{... | collective-permute-start | bytes 2359304 | tf_op jit(solution)/shard_map/ppermute | solution.py:447
  72.6 5.7 %copy-start.8 = (f32[2,5,64,256]{3,2,1,0:T(8,128)}, f32[2,5,64,256]{3,2,1,0:T(8,128)S(1)}, u32[]{:S(2)}) copy-start(f32[2,5,64,256]{3,2,1,0:T(8,128)S(1)} %collective-permute-done.24.top_near.top_far.top) | copy-start | bytes 1966084
  72.6 122.5 %collective-permute-start.11 = (f32[2,4,192,128]{3,2,1,0:T(8,128)}, f32[2,4,192,128]{3,2,1,0:T(8,128)}, u32[]{:S(2)}, u32[]{:S(2)}) collective-permute-start(f32[2,4,192,128]{3,2,1,0:T(8,128)} %get-tuple-element.42), channel_id=1, source_target_pairs={{1,0},{2,1},{3,2},{5,4},{6,5},{7,6},{9,8},{10,9},{11,10},{13,12},{... | collective-permute-start | bytes 2359304 | tf_op jit(solution)/shard_map/ppermute | solution.py:447
  76.8 6.5 %copy-start.27 = (f32[2,5,192,128]{3,2,1,0:T(8,128)S(1)}, f32[2,5,192,128]{3,2,1,0:T(8,128)}, u32[]{:S(2)}) copy-start(f32[2,5,192,128]{3,2,1,0:T(8,128)} %get-tuple-element.49) | copy-start | bytes 2949124
  76.8 30.1 %collective-permute-start.18 = (f32[2,5,192,128]{3,2,1,0:T(8,128)}, f32[2,5,192,128]{3,2,1,0:T(8,128)S(1)}, u32[]{:S(2)}, u32[]{:S(2)}) collective-permute-start(f32[2,5,192,128]{3,2,1,0:T(8,128)} %get-tuple-element.48), channel_id=1, source_target_pairs={{0,1},{1,2},{2,3},{4,5},{5,6},{6,7},{8,9},{9,10},{10,11},{12,13},{... | collective-permute-start | bytes 2949128 | tf_op jit(solution)/shard_map/ppermute | solution.py:447
  83.3 6.3 %copy-start.31 = (f32[2,2,192,128]{3,2,1,0:T(8,128)}, f32[2,2,192,128]{3,2,1,0:T(8,128)S(1)}, u32[]{:S(2)}) copy-start(f32[2,2,192,128]{3,2,1,0:T(8,128)S(1)} %collective-permute-done.2.lft) | copy-start | bytes 1179652
  83.3 25.1 %collective-permute-start.19 = (f32[2,5,192,128]{3,2,1,0:T(8,128)S(1)}, f32[2,5,192,128]{3,2,1,0:T(8,128)S(1)}, u32[]{:S(2)}, u32[]{:S(2)}) collective-permute-start(f32[2,5,192,128]{3,2,1,0:T(8,128)S(1)} %copy-done.27), channel_id=1, source_target_pairs={{1,0},{2,1},{3,2},{5,4},{6,5},{7,6},{9,8},{10,9},{11,10},{13,12},{... | collective-permute-start | bytes 2949128 | tf_op jit(solution)/shard_map/ppermute | solution.py:447
  84.6 22.3 %copy-start.26 = (f32[2,5,192,128]{3,2,1,0:T(8,128)S(1)}, f32[2,5,192,128]{3,2,1,0:T(8,128)}, u32[]{:S(2)}) copy-start(f32[2,5,192,128]{3,2,1,0:T(8,128)} %get-tuple-element.56) | copy-start | bytes 2949124
  84.6 66.1 %collective-permute-start.26 = (f32[2,5,192,128]{3,2,1,0:T(8,128)}, f32[2,5,192,128]{3,2,1,0:T(8,128)S(1)}, u32[]{:S(2)}, u32[]{:S(2)}) collective-permute-start(f32[2,5,192,128]{3,2,1,0:T(8,128)} %get-tuple-element.55), channel_id=1, source_target_pairs={{0,1},{1,2},{2,3},{4,5},{5,6},{6,7},{8,9},{9,10},{10,11},{12,13},{... | collective-permute-start | bytes 2949128 | tf_op jit(solution)/shard_map/ppermute | solution.py:447
  106.9 45.2 %collective-permute-start.27 = (f32[2,5,192,128]{3,2,1,0:T(8,128)S(1)}, f32[2,5,192,128]{3,2,1,0:T(8,128)}, u32[]{:S(2)}, u32[]{:S(2)}) collective-permute-start(f32[2,5,192,128]{3,2,1,0:T(8,128)S(1)} %copy-done.26), channel_id=1, source_target_pairs={{1,0},{2,1},{3,2},{5,4},{6,5},{7,6},{9,8},{10,9},{11,10},{13,12},{... | collective-permute-start | bytes 2949128 | tf_op jit(solution)/shard_map/ppermute | solution.py:447
  145.9 84.3 %collective-permute-start.20 = (f32[2,5,192,128]{3,2,1,0:T(8,128)}, f32[2,5,192,128]{3,2,1,0:T(8,128)S(1)}, u32[]{:S(2)}, u32[]{:S(2)}) collective-permute-start(f32[2,5,192,128]{3,2,1,0:T(8,128)} %get-tuple-element.51), channel_id=1, source_target_pairs={{0,1},{1,2},{2,3},{4,5},{5,6},{6,7},{8,9},{9,10},{10,11},{12,13},{... | collective-permute-start | bytes 2949128 | tf_op jit(solution)/shard_map/ppermute | solution.py:447
  150.8 80.8 %collective-permute-start.21 = (f32[2,5,192,128]{3,2,1,0:T(8,128)}, f32[2,5,192,128]{3,2,1,0:T(8,128)S(1)}, u32[]{:S(2)}, u32[]{:S(2)}) collective-permute-start(f32[2,5,192,128]{3,2,1,0:T(8,128)} %get-tuple-element.52), channel_id=1, source_target_pairs={{1,0},{2,1},{3,2},{5,4},{6,5},{7,6},{9,8},{10,9},{11,10},{13,12},{... | collective-permute-start | bytes 2949128 | tf_op jit(solution)/shard_map/ppermute | solution.py:447
  188.7 51.4 %collective-permute-start.28 = (f32[2,5,192,128]{3,2,1,0:T(8,128)}, f32[2,5,192,128]{3,2,1,0:T(8,128)S(1)}, u32[]{:S(2)}, u32[]{:S(2)}) collective-permute-start(f32[2,5,192,128]{3,2,1,0:T(8,128)} %get-tuple-element.58), channel_id=1, source_target_pairs={{0,1},{1,2},{2,3},{4,5},{5,6},{6,7},{8,9},{9,10},{10,11},{12,13},{... | collective-permute-start | bytes 2949128 | tf_op jit(solution)/shard_map/ppermute | solution.py:447
  193.6 47.8 %collective-permute-start.29 = (f32[2,5,192,128]{3,2,1,0:T(8,128)}, f32[2,5,192,128]{3,2,1,0:T(8,128)}, u32[]{:S(2)}, u32[]{:S(2)}) collective-permute-start(f32[2,5,192,128]{3,2,1,0:T(8,128)} %get-tuple-element.59), channel_id=1, source_target_pairs={{1,0},{2,1},{3,2},{5,4},{6,5},{7,6},{9,8},{10,9},{11,10},{13,12},{... | collective-permute-start | bytes 2949128 | tf_op jit(solution)/shard_map/ppermute | solution.py:447
  225.4 25.2 %collective-permute-start.12 = (f32[2,4,192,128]{3,2,1,0:T(8,128)}, f32[2,4,192,128]{3,2,1,0:T(8,128)S(1)}, u32[]{:S(2)}, u32[]{:S(2)}) collective-permute-start(f32[2,4,192,128]{3,2,1,0:T(8,128)} %get-tuple-element.44), channel_id=1, source_target_pairs={{0,1},{1,2},{2,3},{4,5},{5,6},{6,7},{8,9},{9,10},{10,11},{12,13},{... | collective-permute-start | bytes 2359304 | tf_op jit(solution)/shard_map/ppermute | solution.py:447
  230.3 21.6 %collective-permute-start.13 = (f32[2,4,192,128]{3,2,1,0:T(8,128)}, f32[2,4,192,128]{3,2,1,0:T(8,128)S(1)}, u32[]{:S(2)}, u32[]{:S(2)}) collective-permute-start(f32[2,4,192,128]{3,2,1,0:T(8,128)} %get-tuple-element.45), channel_id=1, source_target_pairs={{1,0},{2,1},{3,2},{5,4},{6,5},{7,6},{9,8},{10,9},{11,10},{13,12},{... | collective-permute-start | bytes 2359304 | tf_op jit(solution)/shard_map/ppermute | solution.py:447
  237.3 31.9 %collective-permute-start.22 = (f32[2,5,64,256]{3,2,1,0:T(8,128)}, f32[2,5,64,256]{3,2,1,0:T(8,128)S(1)}, u32[]{:S(2)}, u32[]{:S(2)}) collective-permute-start(f32[2,5,64,256]{3,2,1,0:T(8,128)} %get-tuple-element.53), channel_id=1, source_target_pairs={{0,4},{4,8},{8,12},{1,5},{5,9},{9,13},{2,6},{6,10},{10,14},{3,7},{... | collective-permute-start | bytes 1966088 | tf_op jit(solution)/shard_map/ppermute | solution.py:447
  240.1 33.7 %collective-permute-start.23 = (f32[2,5,64,256]{3,2,1,0:T(8,128)}, f32[2,5,64,256]{3,2,1,0:T(8,128)S(1)}, u32[]{:S(2)}, u32[]{:S(2)}) collective-permute-start(f32[2,5,64,256]{3,2,1,0:T(8,128)} %get-tuple-element.54), channel_id=1, source_target_pairs={{4,0},{8,4},{12,8},{5,1},{9,5},{13,9},{6,2},{10,6},{14,10},{7,3},{... | collective-permute-start | bytes 1966088 | tf_op jit(solution)/shard_map/ppermute | solution.py:447
  246.0 51.2 %collective-permute-start.30 = (f32[2,5,64,256]{3,2,1,0:T(8,128)}, f32[2,5,64,256]{3,2,1,0:T(8,128)S(1)}, u32[]{:S(2)}, u32[]{:S(2)}) collective-permute-start(f32[2,5,64,256]{3,2,1,0:T(8,128)} %get-tuple-element.60), channel_id=1, source_target_pairs={{0,4},{4,8},{8,12},{1,5},{5,9},{9,13},{2,6},{6,10},{10,14},{3,7},{... | collective-permute-start | bytes 1966088 | tf_op jit(solution)/shard_map/ppermute | solution.py:447
  250.6 51.3 %collective-permute-start.31 = (f32[2,5,64,256]{3,2,1,0:T(8,128)}, f32[2,5,64,256]{3,2,1,0:T(8,128)S(1)}, u32[]{:S(2)}, u32[]{:S(2)}) collective-permute-start(f32[2,5,64,256]{3,2,1,0:T(8,128)} %get-tuple-element.61), channel_id=1, source_target_pairs={{4,0},{8,4},{12,8},{5,1},{9,5},{13,9},{6,2},{10,6},{14,10},{7,3},{... | collective-permute-start | bytes 1966088 | tf_op jit(solution)/shard_map/ppermute | solution.py:447
  256.5 63.1 %collective-permute-start.14 = (f32[2,4,64,256]{3,2,1,0:T(8,128)}, f32[2,4,64,256]{3,2,1,0:T(8,128)S(1)}, u32[]{:S(2)}, u32[]{:S(2)}) collective-permute-start(f32[2,4,64,256]{3,2,1,0:T(8,128)} %get-tuple-element.46), channel_id=1, source_target_pairs={{0,4},{4,8},{8,12},{1,5},{5,9},{9,13},{2,6},{6,10},{10,14},{3,7},{... | collective-permute-start | bytes 1572872 | tf_op jit(solution)/shard_map/ppermute | solution.py:447
  269.1 4.7 copy-start.15
  269.1 55.3 %collective-permute-start.15 = (f32[2,4,64,256]{3,2,1,0:T(8,128)}, f32[2,4,64,256]{3,2,1,0:T(8,128)S(1)}, u32[]{:S(2)}, u32[]{:S(2)}) collective-permute-start(f32[2,4,64,256]{3,2,1,0:T(8,128)} %get-tuple-element.47), channel_id=1, source_target_pairs={{4,0},{8,4},{12,8},{5,1},{9,5},{13,9},{6,2},{10,6},{14,10},{7,3},{... | collective-permute-start | bytes 1572872 | tf_op jit(solution)/shard_map/ppermute | solution.py:447
  281.4 183.5 %collective-permute-start.34 = (f32[2,5,256,256]{3,2,1,0:T(8,128)}, f32[2,5,256,256]{3,2,1,0:T(8,128)S(1)}, u32[]{:S(2)}, u32[]{:S(2)}) collective-permute-start(f32[2,5,256,256]{3,2,1,0:T(8,128)} %shard_map.97.refs_2_), channel_id=1, source_target_pairs={{0,16},{16,0},{1,17},{17,1},{2,18},{18,2},{3,19},{19,3},{4,20},{20... | collective-permute-start | bytes 7864328 | tf_op jit(solution)/shard_map/ppermute | solution.py:482
  297.2 4.7 copy-start.16
  309.5 155.4 %collective-permute-start.35 = (f32[2,5,256,256]{3,2,1,0:T(8,128)}, f32[2,5,256,256]{3,2,1,0:T(8,128)}, u32[]{:S(2)}, u32[]{:S(2)}) collective-permute-start(f32[2,5,256,256]{3,2,1,0:T(8,128)} %shard_map.101.refs_3_), channel_id=1, source_target_pairs={{0,16},{16,0},{1,17},{17,1},{2,18},{18,2},{3,19},{19,3},{4,20},{20... | collective-permute-start | bytes 7864328 | tf_op jit(solution)/shard_map/ppermute | solution.py:482
  330.4 18.0 %copy-start.23 = (f32[2,2,32,32]{3,2,1,0:T(8,128)S(1)}, f32[2,2,32,32]{3,2,1,0:T(8,128)}, u32[]{:S(2)}) copy-start(f32[2,2,32,32]{3,2,1,0:T(8,128)} %param.10) | copy-start | bytes 49156
  330.4 134.5 %collective-permute-start.33 = (f32[2,4,256,256]{3,2,1,0:T(8,128)}, f32[2,4,256,256]{3,2,1,0:T(8,128)}, u32[]{:S(2)}, u32[]{:S(2)}) collective-permute-start(f32[2,4,256,256]{3,2,1,0:T(8,128)} %shard_map.93.refs_1_), channel_id=1, source_target_pairs={{0,16},{16,0},{1,17},{17,1},{2,18},{18,2},{3,19},{19,3},{4,20},{20... | collective-permute-start | bytes 6291464 | tf_op jit(solution)/shard_map/ppermute | solution.py:482
  331.9 4.0 collective-permute-start.4
  334.4 6.1 %collective-permute-start.5 = (f32[2,2,192,128]{3,2,1,0:T(8,128)}, f32[2,2,192,128]{3,2,1,0:T(8,128)S(1)}, u32[]{:S(2)}, u32[]{:S(2)}) collective-permute-start(f32[2,2,192,128]{3,2,1,0:T(8,128)} %get-tuple-element.38), channel_id=1, source_target_pairs={{1,0},{2,1},{3,2},{5,4},{6,5},{7,6},{9,8},{10,9},{11,10},{13,12},{... | collective-permute-start | bytes 1179656 | tf_op jit(solution)/shard_map/ppermute | solution.py:447
  343.3 11.6 %collective-permute-start.6 = (f32[2,2,64,256]{3,2,1,0:T(8,128)}, f32[2,2,64,256]{3,2,1,0:T(8,128)S(1)}, u32[]{:S(2)}, u32[]{:S(2)}) collective-permute-start(f32[2,2,64,256]{3,2,1,0:T(8,128)} %get-tuple-element.39), channel_id=1, source_target_pairs={{0,4},{4,8},{8,12},{1,5},{5,9},{9,13},{2,6},{6,10},{10,14},{3,7},{... | collective-permute-start | bytes 786440 | tf_op jit(solution)/shard_map/ppermute | solution.py:447
  346.8 10.1 %collective-permute-start.7 = (f32[2,2,64,256]{3,2,1,0:T(8,128)}, f32[2,2,64,256]{3,2,1,0:T(8,128)S(1)}, u32[]{:S(2)}, u32[]{:S(2)}) collective-permute-start(f32[2,2,64,256]{3,2,1,0:T(8,128)} %get-tuple-element.40), channel_id=1, source_target_pairs={{4,0},{8,4},{12,8},{5,1},{9,5},{13,9},{6,2},{10,6},{14,10},{7,3},{... | collective-permute-start | bytes 786440 | tf_op jit(solution)/shard_map/ppermute | solution.py:447
  360.7 104.2 %collective-permute-start.32 = (f32[2,2,256,256]{3,2,1,0:T(8,128)}, f32[2,2,256,256]{3,2,1,0:T(8,128)}, u32[]{:S(2)}, u32[]{:S(2)}) collective-permute-start(f32[2,2,256,256]{3,2,1,0:T(8,128)} %shard_map.89.refs_0_), channel_id=1, source_target_pairs={{0,16},{16,0},{1,17},{17,1},{2,18},{18,2},{3,19},{19,3},{4,20},{20... | collective-permute-start | bytes 3145736 | tf_op jit(solution)/shard_map/ppermute | solution.py:482
  (21 other events, 36.0 us)
Sparse Core Ops, SparseCore 0:
  225.5 218.4 all-reduce.2

commit v2 on v1

--- a/solution.py
+++ b/solution.py
@@ -15,7 +15,7 @@
 STEP = 0.25
 PROBE_STEP = 0.5
 FLOOR = 0.25
-PARTS = (2, 4, 5, 5)
+PARTS = (3, 7, 6)
 VMEM = 56 * 2**20
 
 
@@ -58,7 +58,7 @@
 
 
 def gradient_kernel(
-    offs, obj, top, bot, lft, rgt, probe, amp, left, right, gout, gl, gr, pg, ext, grad
+    tiles, rate, offs, obj, top, bot, lft, rgt, probe, amp, left, right, gout, gl, gr, pg, ext, grad
 ):
     win = probe.shape[2]
     tile = obj.shape[2]
@@ -159,6 +159,7 @@
 
     for k in range(amp.shape[3]):
         position(k)
+    pg[...] = probe[...] * (1.0 / tiles) - rate * pg[...]
     first = lax.broadcasted_iota(jnp.int32, (mid, LANES), 1) < HALO
     for p in range(2):
         for j in range(tile // LANES):
@@ -177,6 +178,17 @@
     return pl.CostEstimate(flops=int(flops), bytes_accessed=int(moved), transcendentals=0)
 
 
+def anywhere(arrays):
+    return [pl.BlockSpec(memory_space=pl.ANY)] * len(arrays)
+
+
+def ordered(kernel, inputs, after):
+    def body(*refs):
+        return kernel(*refs[:inputs], *refs[inputs + len(after) :])
+
+    return body
+
+
 def plane(*shape):
     return pl.BlockSpec((2, 1) + shape, lambda e, *_: (0, e, 0, 0))
 
@@ -189,14 +201,16 @@
     return jax.ShapeDtypeStruct(shape, jnp.float32)
 
 
-def gradient_call(offs, obj, top, bot, lft, rgt, probe, amp, left, right, first, count):
+def gradient_call(
+    scales, offs, obj, top, bot, lft, rgt, probe, amp, left, right, first, count, running, after
+):
     win, tile = probe.shape[2], obj.shape[2]
     rows = tile + 2 * HALO
     side = (rows // 2, LANES)
     frame = pltpu.VMEM((2, tile // LANES + 2, rows, LANES), jnp.float32)
     whole = lambda m: pl.BlockSpec(m.shape, lambda e, *_: (0, 0, 0))
     return pl.pallas_call(
-        gradient_kernel,
+        ordered(lambda *refs: gradient_kernel(*scales, *refs), 10, running + after),
         grid_spec=pltpu.PrefetchScalarGridSpec(
             num_scalar_prefetch=1,
             grid=(count,),
@@ -210,19 +224,21 @@
                 pl.BlockSpec((1, 1, 1) + amp.shape[3:], lambda e, *_: (first + e, 0, 0, 0, 0, 0)),
                 whole(left),
                 whole(right),
-            ],
-            out_specs=[plane(rows, tile), plane(*side), plane(*side), plane(win, win)],
+            ]
+            + anywhere(running + after),
+            out_specs=[plane(rows, tile), plane(*side), plane(*side), later(first, win, win)],
             scratch_shapes=[frame, frame],
         ),
         out_shape=[
             struct(2, count, rows, tile),
             struct(2, count, *side),
             struct(2, count, *side),
-            struct(2, count, win, win),
+            struct(*probe.shape),
         ],
+        input_output_aliases={10: 3} if running else {},
         compiler_params=params(),
         cost_estimate=cost(count * 7e9, count * 5e6),
-    )(offs, obj, top, bot, lft, rgt, probe, amp, left, right)
+    )(offs, obj, top, bot, lft, rgt, probe, amp, left, right, *running, *after)
 
 
 def pack_kernel(near, far, top_near, top_far, bot_near, bot_far, left, right):
@@ -243,7 +259,7 @@
                 out[p, 0] = jnp.where(lane < HALO, pltpu.roll(upper, HALO, 1), lower)
 
 
-def pack_call(obj, top, bot, first, count):
+def pack_call(obj, top, bot, first, count, after):
     tile = obj.shape[2]
     last = tile // LANES - 1
     side = (tile // 2 + HALO, LANES)
@@ -252,7 +268,7 @@
         return pl.BlockSpec((2, 1, rows, LANES), lambda e: (0, base + e, 0, block))
 
     return pl.pallas_call(
-        pack_kernel,
+        ordered(pack_kernel, 6, after),
         grid=(count,),
         in_specs=[
             lanes(tile, first, 0),
@@ -261,12 +277,13 @@
             lanes(HALO, 0, last),
             lanes(HALO, 0, 0),
             lanes(HALO, 0, last),
-        ],
+        ]
+        + anywhere(after),
         out_specs=[plane(*side), plane(*side)],
         out_shape=[struct(2, count, *side)] * 2,
         compiler_params=params(),
         cost_estimate=cost(0, count * 12e5),
-    )(obj, obj, top, top, bot, bot)
+    )(obj, obj, top, top, bot, bot, *after)
 
 
 def from_left(packed, upper):
@@ -290,7 +307,7 @@
             out[p, 0, :, -LANES:] += from_right(r[p, 0], upper)
 
 
-def rim_call(g, lft, rgt):
+def rim_call(g, lft, rgt, after):
     count, rows, tile = g.shape[1:]
 
     def strip(block, width):
@@ -299,7 +316,7 @@
     last = rows // HALO - 1
     packed_last = lft.shape[2] // HALO - 1
     return pl.pallas_call(
-        rim_kernel,
+        ordered(rim_kernel, 6, after),
         grid=(count,),
         in_specs=[
             strip(0, tile),
@@ -308,12 +325,13 @@
             strip(packed_last, LANES),
             strip(0, LANES),
             strip(packed_last, LANES),
-        ],
+        ]
+        + anywhere(after),
         out_specs=[plane(HALO, tile), plane(HALO, tile)],
         out_shape=[struct(2, count, HALO, tile)] * 2,
         compiler_params=params(),
-        cost_estimate=cost(0, count * 8e5),
-    )(g, g, lft, lft, rgt, rgt)
+        cost_estimate=cost(1e3, 1e3),
+    )(g, g, lft, lft, rgt, rgt, *after)
 
 
 def step_kernel(obj, g, lft, rgt, above, below, out):
@@ -339,12 +357,12 @@
             out[p, 0, :, span] = obj[p, 0, :, span] - STEP * total
 
 
-def step_call(obj, g, lft, rgt, above, below, first):
+def step_call(obj, g, lft, rgt, above, below, first, after):
     tile = obj.shape[2]
     count, rows = g.shape[1:3]
     side = lft.shape[2:]
     return pl.pallas_call(
-        step_kernel,
+        ordered(step_kernel, 6, after),
         grid=(count,),
         in_specs=[
             later(first, tile, tile),
@@ -353,39 +371,35 @@
             plane(*side),
             plane(HALO, tile),
             plane(HALO, tile),
-        ],
+        ]
+        + anywhere(after),
         out_specs=plane(tile, tile),
         out_shape=struct(2, count, tile, tile),
         compiler_params=params(),
-        cost_estimate=cost(0, count * 25e5),
-    )(obj, g, lft, rgt, above, below)
-
-
-def probe_kernel(rate, probe, total, *rest):
-    rest[-1][...] = probe[...] - rate * total[...]
-
-
-def probe_call(probe, total, rate, first, running):
-    win = probe.shape[2]
-    count = total.shape[1]
-    extra = [] if running is None else [running]
-    return pl.pallas_call(
-        lambda *refs: probe_kernel(rate, *refs),
-        grid=(count,),
-        in_specs=[later(first, win, win), plane(win, win)]
-        + [pl.BlockSpec(memory_space=pl.ANY)] * len(extra),
-        out_specs=later(first, win, win),
-        out_shape=struct(*probe.shape),
-        input_output_aliases={2: 0} if extra else {},
-        compiler_params=params(),
-        cost_estimate=cost(0, count * 16e5),
-    )(probe, total, *extra)
-
-
-def couple_kernel(weights, *refs):
-    parts, out = refs[:-1], refs[-1]
+        cost_estimate=cost(1e3, 1e3),
+    )(obj, g, lft, rgt, above, below, *after)
+
+
+def couple_kernel(table, choose, *refs):
+    parts, out, weights = refs[:-2], refs[-2], refs[-1]
     energies = out.shape[1]
     spans = chunks_of(energies)
+    width = choose.shape[1]
+
+    @pl.when(pl.program_id(0) == 0)
+    def _():
+        rows = lax.broadcasted_iota(jnp.int32, (weights.shape[0], table.shape[0]), 0)
+        source = lax.broadcasted_iota(jnp.int32, rows.shape, 1)
+        spread = (rows // SUB == source).astype(jnp.bfloat16)
+        wide = (weights.shape[0], width)
+        lane = lax.broadcasted_iota(jnp.int32, wide, 1)
+        same = lax.broadcasted_iota(jnp.int32, wide, 0) % SUB == lane % SUB
+        for part, spots in zip(split(table[...]), ((0, 1), (2,))):
+            picked = dot(part, choose[...]).astype(jnp.bfloat16)
+            grown = jnp.where(same, dot(spread, picked), 0.0).astype(jnp.bfloat16)
+            for spot in spots:
+                weights[:, spot * width : (spot + 1) * width] = grown
+
     for g in range(out.shape[2] // SUB):
         rows = slice(g * SUB, (g + 1) * SUB)
 
@@ -404,7 +418,7 @@
                 out[p, first : first + count, rows, :] = value.reshape(count, SUB, value.shape[1])
 
 
-def couple_call(weights, parts, energies):
+def couple_call(table, choose, parts, energies, after):
     tile = parts[0].shape[2]
     rows = 2 * SUB
 
@@ -412,33 +426,40 @@
         return pl.BlockSpec((2, count, rows, tile), lambda i: (0, 0, i, 0))
 
     return pl.pallas_call(
-        couple_kernel,
+        ordered(couple_kernel, 2 + len(parts), after),
         grid=(tile // rows,),
-        in_specs=[pl.BlockSpec(weights.shape, lambda i: (0, 0))]
-        + [block(part.shape[1]) for part in parts],
+        in_specs=[
+            pl.BlockSpec(table.shape, lambda i: (0, 0)),
+            pl.BlockSpec(choose.shape, lambda i: (0, 0)),
+        ]
+        + [block(part.shape[1]) for part in parts]
+        + anywhere(after),
         out_specs=block(energies),
         out_shape=struct(2, energies, tile, tile),
+        scratch_shapes=[pltpu.VMEM((2 * energies * SUB, 3 * choose.shape[1]), jnp.bfloat16)],
         compiler_params=params(),
-        cost_estimate=cost(10e9, 26e6),
-    )(weights, *parts)
-
-
-def coupling_weights(kk_kernel, energies):
+        cost_estimate=cost(1e3, 1e3),
+    )(table, choose, *parts, *after)
+
+
+def coupling(kk_kernel, energies):
     count = lax.axis_size("energy")
     me = lax.axis_index("energy")
+    total = kk_kernel.shape[3]
     mine = lax.dynamic_slice_in_dim(kk_kernel, me * energies, energies, axis=2)
-    pieces = []
-    for shift in range(count):
-        source = (me - shift) % count
-        block = lax.dynamic_slice_in_dim(mine, source * energies, energies, axis=3)
-        block = block.transpose(0, 2, 1, 3)
+    table = mine.transpose(0, 2, 1, 3).reshape(2 * energies, 2 * total)
+    shift, within, base = [], [], []
+    for step in range(count):
         for first, size in chunks_of(energies):
-            pieces.append(block[..., first : first + size].reshape(2 * energies, 2 * size))
-    matrix = jnp.concatenate(pieces, axis=1)
-    hi = lax.reduce_precision(matrix, 8, 7)
-    matrix = jnp.concatenate([hi, hi, matrix - hi], axis=1)
-    grown = matrix[:, None, :, None] * jnp.eye(SUB, dtype=jnp.float32)[None, :, None, :]
-    return grown.reshape(matrix.shape[0] * SUB, matrix.shape[1] * SUB).astype(jnp.bfloat16)
+            for q in range(2):
+                for f in range(first, first + size):
+                    shift += [step] * SUB
+                    within += [f] * SUB
+                    base += [q * total] * SUB
+    source = (me - jnp.asarray(shift, jnp.int32)) % count
+    column = jnp.asarray(base, jnp.int32) + source * energies + jnp.asarray(within, jnp.int32)
+    row = lax.broadcasted_iota(jnp.int32, (2 * total, len(shift)), 0)
+    return table, (row == column[None]).astype(jnp.bfloat16)
 
 
 def toward(block, axis, distance):
@@ -452,37 +473,50 @@
     ring = lax.axis_size("energy")
     tables = [jnp.asarray(m) for m in dft_parts(probe_field.shape[2])]
     offs = offsets.reshape(-1)
-    weights = coupling_weights(kk_kernel, energies)
-    rate = PROBE_STEP / (offsets.shape[2] * lax.axis_size("row") * lax.axis_size("col"))
+    table, choose = coupling(kk_kernel, energies)
+    tiles = lax.axis_size("row") * lax.axis_size("col")
+    scales = (tiles, PROBE_STEP / (offsets.shape[2] * tiles))
     spans = chunks_of(energies)
-    halos = []
+    energy_route = lambda shift: [(i, (i + shift) % ring) for i in range(ring)]
+    halos, grads, own = [], [], []
+    other = [[] for _ in range(ring - 1)]
     for first, count in spans:
         part = object_field[:, first : first + count]
-        top = toward(part[:, :, -HALO:], "row", 1)
-        bot = toward(part[:, :, :HALO], "row", -1)
-        left, right = pack_call(object_field, top, bot, first, count)
+        top, bot = toward(part[:, :, -HALO:], "row", 1), toward(part[:, :, :HALO], "row", -1)
+        left, right = pack_call(object_field, top, bot, first, count, [])
         halos.append((top, bot, toward(right, "col", 1), toward(left, "col", -1)))
-    own, other = [], [[] for _ in range(ring - 1)]
-    new_probe = None
-    totals = []
-    for (first, count), halo in zip(spans, halos):
-        g, g_left, g_right, probe_grad = gradient_call(
-            offs, object_field, *halo, probe_field, amplitudes, *tables, first, count
-        )
-        totals.append(lax.psum(probe_grad, ("row", "col")))
+    rims = []
+
+    def trim(i):
+        g, g_left, g_right = grads[i]
         lft = toward(g_right, "col", 1)
         rgt = toward(g_left, "col", -1)
-        top, bot = rim_call(g, lft, rgt)
-        above = toward(bot, "row", 1)
-        below = toward(top, "row", -1)
-        stepped = step_call(object_field, g, lft, rgt, above, below, first)
-        own.append(stepped)
+        top, bot = rim_call(g, lft, rgt, [])
+        rims.append((g, lft, rgt, toward(bot, "row", 1), toward(top, "row", -1)))
+        return top
+
+    running, after = [], []
+    for i, ((first, count), halo) in enumerate(zip(spans, halos)):
+        *grad, share = gradient_call(
+            scales, offs, object_field, *halo, probe_field, amplitudes, *tables,
+            first, count, running, after,
+        )
+        grads.append(grad)
+        running, after = [share], []
+        if i == len(spans) - 2:
+            after = [trim(len(rims))]
+    new_probe = lax.psum(share, ("row", "col"))
+    for i, (first, count) in enumerate(spans):
+        if i >= len(rims):
+            trim(i)
+        after = own[-1:]
+        if i == len(spans) - 1:
+            after = after + [group[0] for group in other]
+        own.append(step_call(object_field, *rims[i], first, after))
         for shift in range(1, ring):
-            route = [(i, (i + shift) % ring) for i in range(ring)]
-            other[shift - 1].append(lax.ppermute(stepped, "energy", route))
-    for (first, count), total in zip(spans, totals):
-        new_probe = probe_call(probe_field, total, rate, first, new_probe)
-    blended = couple_call(weights, own + [x for group in other for x in group], energies)
+            other[shift - 1].append(lax.ppermute(own[-1], "energy", energy_route(shift)))
+    other = [x for group in other for x in group]
+    blended = couple_call(table, choose, own + other, energies, [])
     return (blended, new_probe)
 
 

time: 494 us -> 477 us (0.966)
  waiting for transfers between devices: 136 us -> 182 us
  Pallas kernels: 209 us -> 185 us
  starting transfers between devices: 88 us -> 66.1 us
  local copies, waits for them, and re-layouts: 35.1 us -> 26.2 us
  other arithmetic: 7.99 us -> 0.65 us
    ppermute x4 -> x3, waiting for transfers between devices: 3.39 us -> 111 us  [local(): lax.ppermute(own[-1], 'energy', energy_route(shift))]
    psum x1, waiting for transfers between devices: 55.3 us -> 0.01 us  [local(): new_probe = lax.psum(share, ('row', 'col'))]
    pallas_call x21 -> x13, Pallas kernels: 209 us -> 185 us  [the longest x3 117 us: gradient_call(): pl.pallas_call(ordered(lambda *refs: gradient_kernel(*scales, *refs), 10,...]
    convert_element_type x1 -> x0, local copies, waits for them, and re-layouts: 18.1 us -> none  [coupling_weights(): grown.reshape(matrix.shape[0] * SUB, matrix.shape[1] * SUB)]
    ppermute x32 -> x24, starting transfers between devices: 81.7 us -> 64.5 us  [toward(): return lax.ppermute(block, axis, route)]
    unnamed x65 -> x50, local copies, waits for them, and re-layouts: 8.32 us -> 18.4 us
    convert_element_type x2 -> x1, other arithmetic: 7.9 us -> 0.64 us  [coupling(): return (table, (row == column[None]).astype(jnp.bfloat16))]
    ppermute x32 -> x24, waiting for transfers between devices: 77.3 us -> 70.4 us  [toward(): return lax.ppermute(block, axis, route)]
  transfers between devices with their start and end apart: 37 -> 28, of which waited for: 15 -> 9; matrix products, arithmetic and copies ran while one was open for 7% -> 2% of each run, Pallas kernels for 39% -> 39%
where the time goes in v2:
time: 477 us; the launch traced here: 475 us
  Pallas kernels  185 us (39%)
  waiting for transfers between devices  182 us (38%)
  starting transfers between devices  66.1 us (14%)
  local copies, waits for them, and re-layouts  26.2 us (5%)
  between operations  14.5 us (3%)
    pallas_call x3, Pallas kernels, gradient_call(): pl.pallas_call(ordered(lambda *refs: gradient_kernel(*scales, *refs), 10,...  117 us
    ppermute x3, waiting for transfers between devices, local(): lax.ppermute(own[-1], 'energy', energy_route(shift))  111 us
    ppermute x24, waiting for transfers between devices, toward(): return lax.ppermute(block, axis, route)  70.4 us
    ppermute x24, starting transfers between devices, toward(): return lax.ppermute(block, axis, route)  64.5 us
    pallas_call x3, Pallas kernels, step_call(): pl.pallas_call(ordered(step_kernel, 6, after), grid=(count,), in_specs=[l...  20.7 us
    unnamed x50, local copies, waits for them, and re-layouts  18.4 us
    pallas_call x1, Pallas kernels, couple_call(): pl.pallas_call(ordered(couple_kernel, 2 + len(parts), after), grid=(tile...  18.3 us
    pallas_call x3, Pallas kernels, pack_call(): pl.pallas_call(ordered(pack_kernel, 6, after), grid=(count,), in_specs=[l...  15.6 us
  transfers between devices with their start and end apart: 28, of which 9 were waited for; matrix products, arithmetic and copies ran while one was open for 2% of the time, Pallas kernels for 39%

profile of v2, /device:TPU:0, one launch (start us, length us, event | category | flops | bytes accessed | tf_op | source)
XLA Modules:
  0.0 474.8 jit_solution(17543999905229220360)
XLA Ops:
  8.4 5.0 %collective-permute-start = (f32[2,3,64,256]{3,2,1,0:T(8,128)S(1)}, f32[2,3,64,256]{3,2,1,0:T(8,128)S(1)}, u32[]{:S(2)}, u32[]{:S(2)}) collective-permute-start(f32[2,3,64,256]{3,2,1,0:T(8,128)S(1)} %get-tuple-element.55), channel_id=1, source_target_pairs={{0,4},{4,8},{8,12},{1,5},{5,9},{9,13},{2,6},{6,10},{10,14},{3,7},{... | collective-permute-start | bytes 1179656 | tf_op jit(solution)/shard_map/ppermute | solution.py:468
  13.4 1.3 collective-permute-start.1
  14.7 2.9 fusion.5
  17.6 4.6 collective-permute-start.8
  22.2 1.3 collective-permute-start.9
  23.5 2.4 collective-permute-done.1.refs_4_.refs_5_.refs_3_
  26.6 3.5 shard_map.113
  30.1 2.1 collective-permute-start.2
  32.2 1.4 collective-permute-start.3
  33.7 2.4 fusion.4
  36.1 3.5 collective-permute-start.16
  42.8 2.8 collective-permute-done.9.refs_4_.refs_5_.refs_3_
  46.5 6.4 %shard_map.117 = (f32[2,7,192,128]{3,2,1,0:T(8,128)}, f32[2,7,192,128]{3,2,1,0:T(8,128)}) custom-call(f32[2,16,256,256]{3,2,1,0:T(8,128)} %refs_0_.11, f32[2,16,256,256]{3,2,1,0:T(8,128)} %refs_0_.11, f32[2,7,64,256]{3,2,1,0:T(8,128)} %copy-done.5, f32[2,7,64,256]{3,2,1,0:T(8,128)} %copy-done.5, f32[2,7,64,256]{3,2,1,0:T(8,128)} %copy-done.6, ...), custom_call_target="tpu_custom_call" | custom-call | bytes 8400000 | tf_op jit(solution)/shard_map/pallas_call | solution.py:270
  52.9 1.4 collective-permute-start.10
  54.3 1.3 collective-permute-start.11
  55.6 23.8 %shard_map.114 = (f32[2,3,384,256]{3,2,1,0:T(8,128)}, f32[2,3,192,128]{3,2,1,0:T(8,128)}, f32[2,3,192,128]{3,2,1,0:T(8,128)}, f32[2,16,256,256]{3,2,1,0:T(8,128)}) custom-call(s32[8]{0:T(128)} %reshape.12.refs_0_, f32[2,16,256,256]{3,2,1,0:T(8,128)} %refs_0_.11, f32[2,3,64,256]{3,2,1,0:T(8,128)} %copy-done.10, f32[2,3,64,256]{3,2,1,0:T(8,128)} %copy-done.11, ...), custom_call_target="tpu_custom_call" | custom-call | flops 20999999488 | bytes 15000000 | tf_op jit(solution)/shard_map/pallas_call | solution.py:212
  79.4 5.3 %collective-permute-start.4 = (f32[2,3,192,128]{3,2,1,0:T(8,128)}, f32[2,3,192,128]{3,2,1,0:T(8,128)S(1)}, u32[]{:S(2)}, u32[]{:S(2)}) collective-permute-start(f32[2,3,192,128]{3,2,1,0:T(8,128)} %get-tuple-element.29), channel_id=1, source_target_pairs={{0,1},{1,2},{2,3},{4,5},{5,6},{6,7},{8,9},{9,10},{10,11},{12,13},{... | collective-permute-start | bytes 1769480 | tf_op jit(solution)/shard_map/ppermute | solution.py:468
  84.7 1.3 collective-permute-start.5
  86.9 5.6 %shard_map.121 = (f32[2,6,192,128]{3,2,1,0:T(8,128)}, f32[2,6,192,128]{3,2,1,0:T(8,128)}) custom-call(f32[2,16,256,256]{3,2,1,0:T(8,128)} %refs_0_.11, f32[2,16,256,256]{3,2,1,0:T(8,128)} %refs_0_.11, f32[2,6,64,256]{3,2,1,0:T(8,128)} %copy-done.7, f32[2,6,64,256]{3,2,1,0:T(8,128)} %copy-done.7, f32[2,6,64,256]{3,2,1,0:T(8,128)} %copy-done.8, ...), custom_call_target="tpu_custom_call" | custom-call | bytes 7200000 | tf_op jit(solution)/shard_map/pallas_call | solution.py:270
  92.6 5.0 %collective-permute-start.18 = (f32[2,6,192,128]{3,2,1,0:T(8,128)}, f32[2,6,192,128]{3,2,1,0:T(8,128)}, u32[]{:S(2)}, u32[]{:S(2)}) collective-permute-start(f32[2,6,192,128]{3,2,1,0:T(8,128)} %get-tuple-element.41), channel_id=1, source_target_pairs={{0,1},{1,2},{2,3},{4,5},{5,6},{6,7},{8,9},{9,10},{10,11},{12,13},{... | collective-permute-start | bytes 3538952 | tf_op jit(solution)/shard_map/ppermute | solution.py:468
  97.6 1.3 collective-permute-start.19
  99.7 3.3 shard_map.115
  103.0 3.7 collective-permute-start.6
  108.3 49.6 %shard_map.118 = (f32[2,7,384,256]{3,2,1,0:T(8,128)}, f32[2,7,192,128]{3,2,1,0:T(8,128)}, f32[2,7,192,128]{3,2,1,0:T(8,128)}, f32[2,16,256,256]{3,2,1,0:T(8,128)}) custom-call(s32[8]{0:T(128)} %reshape.12.refs_0_, f32[2,16,256,256]{3,2,1,0:T(8,128)} %refs_0_.11, f32[2,7,64,256]{3,2,1,0:T(8,128)} %copy-done.5, ...), custom_call_target="tpu_custom_call", output_to_operand_aliasing={{3}: (10, {})} | custom-call | flops 49000001536 | bytes 35000000 | tf_op jit(solution)/shard_map/pallas_call | solution.py:212
  157.9 4.4 collective-permute-start.12
  162.3 1.3 collective-permute-start.13
  163.6 43.3 %shard_map.122 = (f32[2,6,384,256]{3,2,1,0:T(8,128)}, f32[2,6,192,128]{3,2,1,0:T(8,128)}, f32[2,6,192,128]{3,2,1,0:T(8,128)}, f32[2,16,256,256]{3,2,1,0:T(8,128)}) custom-call(s32[8]{0:T(128)} %reshape.12.refs_0_, f32[2,16,256,256]{3,2,1,0:T(8,128)} %refs_0_.11, f32[2,6,64,256]{3,2,1,0:T(8,128)} %copy-done.7, ...), custom_call_target="tpu_custom_call", output_to_operand_aliasing={{3}: (10, {})} | custom-call | flops 41999998976 | bytes 30000000 | tf_op jit(solution)/shard_map/pallas_call | solution.py:212
  206.9 6.1 %collective-permute-start.20 = (f32[2,6,192,128]{3,2,1,0:T(8,128)}, f32[2,6,192,128]{3,2,1,0:T(8,128)}, u32[]{:S(2)}, u32[]{:S(2)}) collective-permute-start(f32[2,6,192,128]{3,2,1,0:T(8,128)} %get-tuple-element.45), channel_id=1, source_target_pairs={{0,1},{1,2},{2,3},{4,5},{5,6},{6,7},{8,9},{9,10},{10,11},{12,13},{... | collective-permute-start | bytes 3538952 | tf_op jit(solution)/shard_map/ppermute | solution.py:468
  214.3 1.5 collective-permute-start.7
  215.9 12.2 %collective-permute-done.7.refs_5_ = f32[2,3,64,256]{3,2,1,0:T(8,128)S(1)} collective-permute-done((f32[2,3,64,256]{3,2,1,0:T(8,128)S(1)}, f32[2,3,64,256]{3,2,1,0:T(8,128)S(1)}, u32[]{:S(2)}, u32[]{:S(2)}) %collective-permute-start.7) | collective-permute-done | bytes 393248 | tf_op jit(solution)/shard_map/ppermute | solution.py:468
  228.8 4.6 shard_map.116.refs_6_.refs_2_
  233.4 1.5 collective-permute-start.24
  236.4 5.8 %shard_map.119 = (f32[2,7,64,256]{3,2,1,0:T(8,128)}, f32[2,7,64,256]{3,2,1,0:T(8,128)}) custom-call(f32[2,7,384,256]{3,2,1,0:T(8,128)} %get-tuple-element.36.refs_0_.refs_1_, f32[2,7,384,256]{3,2,1,0:T(8,128)} %get-tuple-element.36.refs_0_.refs_1_, f32[2,7,192,128]{3,2,1,0:T(8,128)} %copy-done.1, f32[2,7,192,128]{3,2,1,0:T(8,128)} %copy-done.1, ...), custom_call_target="tpu_custom_call" | custom-call | flops 1000 | bytes 1000 | tf_op jit(solution)/shard_map/pallas_call | solution.py:318
  242.2 3.1 collective-permute-start.14
  245.3 1.3 collective-permute-start.15
  246.6 5.1 %shard_map.123 = (f32[2,6,64,256]{3,2,1,0:T(8,128)}, f32[2,6,64,256]{3,2,1,0:T(8,128)}) custom-call(f32[2,6,384,256]{3,2,1,0:T(8,128)} %get-tuple-element.44.refs_0_.refs_1_, f32[2,6,384,256]{3,2,1,0:T(8,128)} %get-tuple-element.44.refs_0_.refs_1_, f32[2,6,192,128]{3,2,1,0:T(8,128)} %collective-permute-done.20.refs_2_.refs_3_, ...), custom_call_target="tpu_custom_call" | custom-call | flops 1000 | bytes 1000 | tf_op jit(solution)/shard_map/pallas_call | solution.py:318
  251.7 4.6 collective-permute-start.22
  256.3 1.3 collective-permute-start.23
  257.6 22.7 %collective-permute-done.14.refs_4_ = f32[2,7,64,256]{3,2,1,0:T(8,128)S(1)} collective-permute-done((f32[2,7,64,256]{3,2,1,0:T(8,128)}, f32[2,7,64,256]{3,2,1,0:T(8,128)S(1)}, u32[]{:S(2)}, u32[]{:S(2)}) %collective-permute-start.14) | collective-permute-done | bytes 917536 | tf_op jit(solution)/shard_map/ppermute | solution.py:468
  280.3 6.7 %collective-permute-done.15.refs_5_ = f32[2,7,64,256]{3,2,1,0:T(8,128)S(1)} collective-permute-done((f32[2,7,64,256]{3,2,1,0:T(8,128)}, f32[2,7,64,256]{3,2,1,0:T(8,128)S(1)}, u32[]{:S(2)}, u32[]{:S(2)}) %collective-permute-start.15) | collective-permute-done | bytes 917536 | tf_op jit(solution)/shard_map/ppermute | solution.py:468
  287.9 8.8 %shard_map.120.refs_6_.refs_3_ = f32[2,7,256,256]{3,2,1,0:T(8,128)} custom-call(f32[2,16,256,256]{3,2,1,0:T(8,128)} %refs_0_.11, f32[2,7,384,256]{3,2,1,0:T(8,128)} %get-tuple-element.36.refs_0_.refs_1_, f32[2,7,192,128]{3,2,1,0:T(8,128)} %copy-done.1, f32[2,7,192,128]{3,2,1,0:T(8,128)} %copy-done.2, f32[2,7,64,256]{3,2,1,0:T(8,128)} %copy-done.12, ...), custom_call_target="tpu_custom_call" | custom-call | flops 1000 | bytes 1000 | tf_op jit(solution)/shard_map/pallas_call | solution.py:364
  296.8 16.1 %collective-permute-done.22.refs_4_ = f32[2,6,64,256]{3,2,1,0:T(8,128)S(1)} collective-permute-done((f32[2,6,64,256]{3,2,1,0:T(8,128)}, f32[2,6,64,256]{3,2,1,0:T(8,128)S(1)}, u32[]{:S(2)}, u32[]{:S(2)}) %collective-permute-start.22) | collective-permute-done | bytes 786464 | tf_op jit(solution)/shard_map/ppermute | solution.py:468
  312.9 6.4 %collective-permute-done.23.refs_5_ = f32[2,6,64,256]{3,2,1,0:T(8,128)S(1)} collective-permute-done((f32[2,6,64,256]{3,2,1,0:T(8,128)}, f32[2,6,64,256]{3,2,1,0:T(8,128)S(1)}, u32[]{:S(2)}, u32[]{:S(2)}) %collective-permute-start.23) | collective-permute-done | bytes 786464 | tf_op jit(solution)/shard_map/ppermute | solution.py:468
  320.2 7.3 %shard_map.124.refs_4_ = f32[2,6,256,256]{3,2,1,0:T(8,128)} custom-call(f32[2,16,256,256]{3,2,1,0:T(8,128)} %refs_0_.11, f32[2,6,384,256]{3,2,1,0:T(8,128)} %get-tuple-element.44.refs_0_.refs_1_, f32[2,6,192,128]{3,2,1,0:T(8,128)} %collective-permute-done.20.refs_2_.refs_3_, f32[2,6,192,128]{3,2,1,0:T(8,128)} %collective-permute-done.21.refs_4_.refs_5_.refs_3_, ...), custom_call_target="tpu_custom_call" | custom-call | flops 1000 | bytes 1000 | tf_op jit(solution)/shard_map/pallas_call | solution.py:364
  328.9 111.5 %collective-permute-done.26.refs_7_ = f32[2,6,256,256]{3,2,1,0:T(8,128)S(1)} collective-permute-done((f32[2,6,256,256]{3,2,1,0:T(8,128)}, f32[2,6,256,256]{3,2,1,0:T(8,128)S(1)}, u32[]{:S(2)}, u32[]{:S(2)}) %collective-permute-start.26) | collective-permute-done | bytes 3145760 | tf_op jit(solution)/shard_map/ppermute | solution.py:517
  440.3 1.6 copy-done.9
  442.0 18.3 %shard_map.125 = f32[2,16,256,256]{3,2,1,0:T(8,128)} custom-call(f32[32,64]{1,0:T(8,128)} %reshape.11.refs_0_, bf16[64,512]{1,0:T(8,128)(2,1)} %fusion.refs_1_, f32[2,3,256,256]{3,2,1,0:T(8,128)} %shard_map.116.refs_6_.refs_2_, f32[2,7,256,256]{3,2,1,0:T(8,128)} %shard_map.120.refs_6_.refs_3_, f32[2,6,256,256]{3,2,1,0:T(8,128)} %shard_map.124.refs_4_, ...), custom_call_target="tpu_custom_call" | custom-call | flops 1000 | bytes 1000 | tf_op jit(solution)/shard_map/pallas_call | solution.py:428
  460.3 7.7 %copy.21 = f32[2,16,256,256]{3,2,1,0:T(8,128)} copy(f32[2,16,256,256]{3,2,1,0:T(8,128)} %all-reduce.2.cloned.1.call-done) | data formatting | bytes 16777216
  (81 shorter events, 16.2 us)
Async XLA Ops:
  7.2 320.3 %copy-start = (f32[2,2,32,32]{3,2,1,0:T(8,128)S(1)}, f32[2,2,32,32]{3,2,1,0:T(8,128)}, u32[]{:S(2)}) copy-start(f32[2,2,32,32]{3,2,1,0:T(8,128)} %param.13) | copy-start | bytes 49156
  7.2 453.1 %all-reduce.2.cloned.1.call-start = ((), (), s32[]{:S(2)}) async-start(), calls=%async_computation | async-start | bytes 16777216 | tf_op jit(solution)/shard_map/psum | solution.py:508
  8.4 15.1 %collective-permute-start = (f32[2,3,64,256]{3,2,1,0:T(8,128)S(1)}, f32[2,3,64,256]{3,2,1,0:T(8,128)S(1)}, u32[]{:S(2)}, u32[]{:S(2)}) collective-permute-start(f32[2,3,64,256]{3,2,1,0:T(8,128)S(1)} %get-tuple-element.55), channel_id=1, source_target_pairs={{0,4},{4,8},{8,12},{1,5},{5,9},{9,13},{2,6},{6,10},{10,14},{3,7},{... | collective-permute-start | bytes 1179656 | tf_op jit(solution)/shard_map/ppermute | solution.py:468
  13.4 12.5 %collective-permute-start.1 = (f32[2,3,64,256]{3,2,1,0:T(8,128)S(1)}, f32[2,3,64,256]{3,2,1,0:T(8,128)S(1)}, u32[]{:S(2)}, u32[]{:S(2)}) collective-permute-start(f32[2,3,64,256]{3,2,1,0:T(8,128)S(1)} %get-tuple-element.54), channel_id=1, source_target_pairs={{4,0},{8,4},{12,8},{5,1},{9,5},{13,9},{6,2},{10,6},{14,10},{7,3},{... | collective-permute-start | bytes 1179656 | tf_op jit(solution)/shard_map/ppermute | solution.py:468
  17.6 23.9 %collective-permute-start.8 = (f32[2,7,64,256]{3,2,1,0:T(8,128)}, f32[2,7,64,256]{3,2,1,0:T(8,128)S(1)}, u32[]{:S(2)}, u32[]{:S(2)}) collective-permute-start(f32[2,7,64,256]{3,2,1,0:T(8,128)} %get-tuple-element.53), channel_id=1, source_target_pairs={{0,4},{4,8},{8,12},{1,5},{5,9},{9,13},{2,6},{6,10},{10,14},{3,7},{... | collective-permute-start | bytes 2752520 | tf_op jit(solution)/shard_map/ppermute | solution.py:468
  22.2 23.4 %collective-permute-start.9 = (f32[2,7,64,256]{3,2,1,0:T(8,128)}, f32[2,7,64,256]{3,2,1,0:T(8,128)S(1)}, u32[]{:S(2)}, u32[]{:S(2)}) collective-permute-start(f32[2,7,64,256]{3,2,1,0:T(8,128)} %get-tuple-element.52), channel_id=1, source_target_pairs={{4,0},{8,4},{12,8},{5,1},{9,5},{13,9},{6,2},{10,6},{14,10},{7,3},{... | collective-permute-start | bytes 2752520 | tf_op jit(solution)/shard_map/ppermute | solution.py:468
  23.5 2.4 copy-start.10
  30.1 24.2 %collective-permute-start.2 = (f32[2,3,192,128]{3,2,1,0:T(8,128)}, f32[2,3,192,128]{3,2,1,0:T(8,128)}, u32[]{:S(2)}, u32[]{:S(2)}) collective-permute-start(f32[2,3,192,128]{3,2,1,0:T(8,128)} %get-tuple-element.26), channel_id=1, source_target_pairs={{0,1},{1,2},{2,3},{4,5},{5,6},{6,7},{8,9},{9,10},{10,11},{12,13},{... | collective-permute-start | bytes 1769480 | tf_op jit(solution)/shard_map/ppermute | solution.py:468
  32.2 7.3 %copy-start.20 = (s32[1,1,4,2]{2,3,1,0:T(2,128)S(1)}, s32[1,1,4,2]{2,3,1,0:T(2,128)}, u32[]{:S(2)}) copy-start(s32[1,1,4,2]{2,3,1,0:T(2,128)} %param.14) | copy-start | bytes 100
  32.2 23.4 %collective-permute-start.3 = (f32[2,3,192,128]{3,2,1,0:T(8,128)}, f32[2,3,192,128]{3,2,1,0:T(8,128)}, u32[]{:S(2)}, u32[]{:S(2)}) collective-permute-start(f32[2,3,192,128]{3,2,1,0:T(8,128)} %get-tuple-element.27), channel_id=1, source_target_pairs={{1,0},{2,1},{3,2},{5,4},{6,5},{7,6},{9,8},{10,9},{11,10},{13,12},{... | collective-permute-start | bytes 1769480 | tf_op jit(solution)/shard_map/ppermute | solution.py:468
  36.1 48.6 %collective-permute-start.16 = (f32[2,6,64,256]{3,2,1,0:T(8,128)}, f32[2,6,64,256]{3,2,1,0:T(8,128)S(1)}, u32[]{:S(2)}, u32[]{:S(2)}) collective-permute-start(f32[2,6,64,256]{3,2,1,0:T(8,128)} %get-tuple-element.51), channel_id=1, source_target_pairs={{0,4},{4,8},{8,12},{1,5},{5,9},{9,13},{2,6},{6,10},{10,14},{3,7},{... | collective-permute-start | bytes 2359304 | tf_op jit(solution)/shard_map/ppermute | solution.py:468
  41.5 4.0 copy-start.5
  41.5 44.6 %collective-permute-start.17 = (f32[2,6,64,256]{3,2,1,0:T(8,128)S(1)}, f32[2,6,64,256]{3,2,1,0:T(8,128)S(1)}, u32[]{:S(2)}, u32[]{:S(2)}) collective-permute-start(f32[2,6,64,256]{3,2,1,0:T(8,128)S(1)} %get-tuple-element.50), channel_id=1, source_target_pairs={{4,0},{8,4},{12,8},{5,1},{9,5},{13,9},{6,2},{10,6},{14,10},{7,3},{... | collective-permute-start | bytes 2359304 | tf_op jit(solution)/shard_map/ppermute | solution.py:468
  45.5 1.0 copy-start.6
  52.9 53.7 %collective-permute-start.10 = (f32[2,7,192,128]{3,2,1,0:T(8,128)}, f32[2,7,192,128]{3,2,1,0:T(8,128)S(1)}, u32[]{:S(2)}, u32[]{:S(2)}) collective-permute-start(f32[2,7,192,128]{3,2,1,0:T(8,128)} %get-tuple-element.33), channel_id=1, source_target_pairs={{0,1},{1,2},{2,3},{4,5},{5,6},{6,7},{8,9},{9,10},{10,11},{12,13},{... | collective-permute-start | bytes 4128776 | tf_op jit(solution)/shard_map/ppermute | solution.py:468
  54.3 52.4 %collective-permute-start.11 = (f32[2,7,192,128]{3,2,1,0:T(8,128)}, f32[2,7,192,128]{3,2,1,0:T(8,128)S(1)}, u32[]{:S(2)}, u32[]{:S(2)}) collective-permute-start(f32[2,7,192,128]{3,2,1,0:T(8,128)} %get-tuple-element.34), channel_id=1, source_target_pairs={{1,0},{2,1},{3,2},{5,4},{6,5},{7,6},{9,8},{10,9},{11,10},{13,12},{... | collective-permute-start | bytes 4128776 | tf_op jit(solution)/shard_map/ppermute | solution.py:468
  79.4 18.2 %collective-permute-start.4 = (f32[2,3,192,128]{3,2,1,0:T(8,128)}, f32[2,3,192,128]{3,2,1,0:T(8,128)S(1)}, u32[]{:S(2)}, u32[]{:S(2)}) collective-permute-start(f32[2,3,192,128]{3,2,1,0:T(8,128)} %get-tuple-element.29), channel_id=1, source_target_pairs={{0,1},{1,2},{2,3},{4,5},{5,6},{6,7},{8,9},{9,10},{10,11},{12,13},{... | collective-permute-start | bytes 1769480 | tf_op jit(solution)/shard_map/ppermute | solution.py:468
  84.7 1.3 copy-start.7
  84.7 14.2 %collective-permute-start.5 = (f32[2,3,192,128]{3,2,1,0:T(8,128)}, f32[2,3,192,128]{3,2,1,0:T(8,128)S(1)}, u32[]{:S(2)}, u32[]{:S(2)}) collective-permute-start(f32[2,3,192,128]{3,2,1,0:T(8,128)} %get-tuple-element.30), channel_id=1, source_target_pairs={{1,0},{2,1},{3,2},{5,4},{6,5},{7,6},{9,8},{10,9},{11,10},{13,12},{... | collective-permute-start | bytes 1769480 | tf_op jit(solution)/shard_map/ppermute | solution.py:468
  92.6 71.0 %collective-permute-start.18 = (f32[2,6,192,128]{3,2,1,0:T(8,128)}, f32[2,6,192,128]{3,2,1,0:T(8,128)}, u32[]{:S(2)}, u32[]{:S(2)}) collective-permute-start(f32[2,6,192,128]{3,2,1,0:T(8,128)} %get-tuple-element.41), channel_id=1, source_target_pairs={{0,1},{1,2},{2,3},{4,5},{5,6},{6,7},{8,9},{9,10},{10,11},{12,13},{... | collective-permute-start | bytes 3538952 | tf_op jit(solution)/shard_map/ppermute | solution.py:468
  97.6 1.3 copy-start.3
  97.6 66.0 %collective-permute-start.19 = (f32[2,6,192,128]{3,2,1,0:T(8,128)}, f32[2,6,192,128]{3,2,1,0:T(8,128)}, u32[]{:S(2)}, u32[]{:S(2)}) collective-permute-start(f32[2,6,192,128]{3,2,1,0:T(8,128)} %get-tuple-element.42), channel_id=1, source_target_pairs={{1,0},{2,1},{3,2},{5,4},{6,5},{7,6},{9,8},{10,9},{11,10},{13,12},{... | collective-permute-start | bytes 3538952 | tf_op jit(solution)/shard_map/ppermute | solution.py:468
  103.0 111.3 %collective-permute-start.6 = (f32[2,3,64,256]{3,2,1,0:T(8,128)}, f32[2,3,64,256]{3,2,1,0:T(8,128)S(1)}, u32[]{:S(2)}, u32[]{:S(2)}) collective-permute-start(f32[2,3,64,256]{3,2,1,0:T(8,128)} %get-tuple-element.31), channel_id=1, source_target_pairs={{0,4},{4,8},{8,12},{1,5},{5,9},{9,13},{2,6},{6,10},{10,14},{3,7},{... | collective-permute-start | bytes 1179656 | tf_op jit(solution)/shard_map/ppermute | solution.py:468
  106.7 1.1 copy-start.21
  106.7 1.6 copy-start.22
  157.9 77.0 %collective-permute-start.12 = (f32[2,7,192,128]{3,2,1,0:T(8,128)}, f32[2,7,192,128]{3,2,1,0:T(8,128)S(1)}, u32[]{:S(2)}, u32[]{:S(2)}) collective-permute-start(f32[2,7,192,128]{3,2,1,0:T(8,128)} %get-tuple-element.37), channel_id=1, source_target_pairs={{0,1},{1,2},{2,3},{4,5},{5,6},{6,7},{8,9},{9,10},{10,11},{12,13},{... | collective-permute-start | bytes 4128776 | tf_op jit(solution)/shard_map/ppermute | solution.py:468
  162.3 72.6 %collective-permute-start.13 = (f32[2,7,192,128]{3,2,1,0:T(8,128)}, f32[2,7,192,128]{3,2,1,0:T(8,128)S(1)}, u32[]{:S(2)}, u32[]{:S(2)}) collective-permute-start(f32[2,7,192,128]{3,2,1,0:T(8,128)} %get-tuple-element.38), channel_id=1, source_target_pairs={{1,0},{2,1},{3,2},{5,4},{6,5},{7,6},{9,8},{10,9},{11,10},{13,12},{... | collective-permute-start | bytes 4128776 | tf_op jit(solution)/shard_map/ppermute | solution.py:468
  163.6 50.7 %copy-start.23 = (f32[2,3,64,256]{3,2,1,0:T(8,128)S(1)}, f32[2,3,64,256]{3,2,1,0:T(8,128)}, u32[]{:S(2)}) copy-start(f32[2,3,64,256]{3,2,1,0:T(8,128)} %get-tuple-element.32.refs_11_) | copy-start | bytes 1179652
  206.9 39.7 %collective-permute-start.20 = (f32[2,6,192,128]{3,2,1,0:T(8,128)}, f32[2,6,192,128]{3,2,1,0:T(8,128)}, u32[]{:S(2)}, u32[]{:S(2)}) collective-permute-start(f32[2,6,192,128]{3,2,1,0:T(8,128)} %get-tuple-element.45), channel_id=1, source_target_pairs={{0,1},{1,2},{2,3},{4,5},{5,6},{6,7},{8,9},{9,10},{10,11},{12,13},{... | collective-permute-start | bytes 3538952 | tf_op jit(solution)/shard_map/ppermute | solution.py:468
  213.0 33.6 %collective-permute-start.21 = (f32[2,6,192,128]{3,2,1,0:T(8,128)}, f32[2,6,192,128]{3,2,1,0:T(8,128)}, u32[]{:S(2)}, u32[]{:S(2)}) collective-permute-start(f32[2,6,192,128]{3,2,1,0:T(8,128)} %get-tuple-element.46), channel_id=1, source_target_pairs={{1,0},{2,1},{3,2},{5,4},{6,5},{7,6},{9,8},{10,9},{11,10},{13,12},{... | collective-permute-start | bytes 3538952 | tf_op jit(solution)/shard_map/ppermute | solution.py:468
  214.3 13.7 %copy-start.16 = (f32[2,3,64,256]{3,2,1,0:T(8,128)}, f32[2,3,64,256]{3,2,1,0:T(8,128)S(1)}, u32[]{:S(2)}) copy-start(f32[2,3,64,256]{3,2,1,0:T(8,128)S(1)} %collective-permute-done.6.refs_4_) | copy-start | bytes 1179652
  214.3 13.7 %collective-permute-start.7 = (f32[2,3,64,256]{3,2,1,0:T(8,128)S(1)}, f32[2,3,64,256]{3,2,1,0:T(8,128)S(1)}, u32[]{:S(2)}, u32[]{:S(2)}) collective-permute-start(f32[2,3,64,256]{3,2,1,0:T(8,128)S(1)} %copy-done.23), channel_id=1, source_target_pairs={{4,0},{8,4},{12,8},{5,1},{9,5},{13,9},{6,2},{10,6},{14,10},{7,3},{... | collective-permute-start | bytes 1179656 | tf_op jit(solution)/shard_map/ppermute | solution.py:468
  233.4 63.4 %collective-permute-start.24 = (f32[2,3,256,256]{3,2,1,0:T(8,128)}, f32[2,3,256,256]{3,2,1,0:T(8,128)}, u32[]{:S(2)}, u32[]{:S(2)}) collective-permute-start(f32[2,3,256,256]{3,2,1,0:T(8,128)} %shard_map.116.refs_6_.refs_2_), channel_id=1, source_target_pairs={{0,16},{16,0},{1,17},{17,1},{2,18},{18,2},{3,19},{19,3},{4,20},{20... | collective-permute-start | bytes 4718600 | tf_op jit(solution)/shard_map/ppermute | solution.py:517
  234.9 1.1 copy-start.1
  234.9 1.5 copy-start.2
  242.2 38.1 %collective-permute-start.14 = (f32[2,7,64,256]{3,2,1,0:T(8,128)}, f32[2,7,64,256]{3,2,1,0:T(8,128)S(1)}, u32[]{:S(2)}, u32[]{:S(2)}) collective-permute-start(f32[2,7,64,256]{3,2,1,0:T(8,128)} %get-tuple-element.39), channel_id=1, source_target_pairs={{0,4},{4,8},{8,12},{1,5},{5,9},{9,13},{2,6},{6,10},{10,14},{3,7},{... | collective-permute-start | bytes 2752520 | tf_op jit(solution)/shard_map/ppermute | solution.py:468
  245.3 41.7 %collective-permute-start.15 = (f32[2,7,64,256]{3,2,1,0:T(8,128)}, f32[2,7,64,256]{3,2,1,0:T(8,128)S(1)}, u32[]{:S(2)}, u32[]{:S(2)}) collective-permute-start(f32[2,7,64,256]{3,2,1,0:T(8,128)} %get-tuple-element.40), channel_id=1, source_target_pairs={{4,0},{8,4},{12,8},{5,1},{9,5},{13,9},{6,2},{10,6},{14,10},{7,3},{... | collective-permute-start | bytes 2752520 | tf_op jit(solution)/shard_map/ppermute | solution.py:468
  251.7 61.2 %collective-permute-start.22 = (f32[2,6,64,256]{3,2,1,0:T(8,128)}, f32[2,6,64,256]{3,2,1,0:T(8,128)S(1)}, u32[]{:S(2)}, u32[]{:S(2)}) collective-permute-start(f32[2,6,64,256]{3,2,1,0:T(8,128)} %get-tuple-element.47), channel_id=1, source_target_pairs={{0,4},{4,8},{8,12},{1,5},{5,9},{9,13},{2,6},{6,10},{10,14},{3,7},{... | collective-permute-start | bytes 2359304 | tf_op jit(solution)/shard_map/ppermute | solution.py:468
  256.3 63.0 %collective-permute-start.23 = (f32[2,6,64,256]{3,2,1,0:T(8,128)}, f32[2,6,64,256]{3,2,1,0:T(8,128)S(1)}, u32[]{:S(2)}, u32[]{:S(2)}) collective-permute-start(f32[2,6,64,256]{3,2,1,0:T(8,128)} %get-tuple-element.48), channel_id=1, source_target_pairs={{4,0},{8,4},{12,8},{5,1},{9,5},{13,9},{6,2},{10,6},{14,10},{7,3},{... | collective-permute-start | bytes 2359304 | tf_op jit(solution)/shard_map/ppermute | solution.py:468
  280.3 6.7 %copy-start.12 = (f32[2,7,64,256]{3,2,1,0:T(8,128)}, f32[2,7,64,256]{3,2,1,0:T(8,128)S(1)}, u32[]{:S(2)}) copy-start(f32[2,7,64,256]{3,2,1,0:T(8,128)S(1)} %collective-permute-done.14.refs_4_) | copy-start | bytes 2752516
  287.0 0.9 copy-start.13
  296.7 31.5 %copy-start.18 = (s32[512]{0:T(512)S(1)}, s32[512]{0:T(512)}, u32[]{:S(2)}) copy-start(s32[512]{0:T(512)} %constant.45) | copy-start | bytes 6148
  296.7 31.5 %copy-start.19 = (s32[512]{0:T(512)S(1)}, s32[512]{0:T(512)}, u32[]{:S(2)}) copy-start(s32[512]{0:T(512)} %constant.44) | copy-start | bytes 6148
  296.8 143.6 %collective-permute-start.25 = (f32[2,7,256,256]{3,2,1,0:T(8,128)}, f32[2,7,256,256]{3,2,1,0:T(8,128)}, u32[]{:S(2)}, u32[]{:S(2)}) collective-permute-start(f32[2,7,256,256]{3,2,1,0:T(8,128)} %shard_map.120.refs_6_.refs_3_), channel_id=1, source_target_pairs={{0,16},{16,0},{1,17},{17,1},{2,18},{18,2},{3,19},{19,3},{4,20},{20... | collective-permute-start | bytes 11010056 | tf_op jit(solution)/shard_map/ppermute | solution.py:517
  312.9 6.4 %copy-start.14 = (f32[2,6,64,256]{3,2,1,0:T(8,128)}, f32[2,6,64,256]{3,2,1,0:T(8,128)S(1)}, u32[]{:S(2)}) copy-start(f32[2,6,64,256]{3,2,1,0:T(8,128)S(1)} %collective-permute-done.22.refs_4_) | copy-start | bytes 2359300
  319.3 0.9 copy-start.15
  327.5 112.9 %collective-permute-start.26 = (f32[2,6,256,256]{3,2,1,0:T(8,128)}, f32[2,6,256,256]{3,2,1,0:T(8,128)S(1)}, u32[]{:S(2)}, u32[]{:S(2)}) collective-permute-start(f32[2,6,256,256]{3,2,1,0:T(8,128)} %shard_map.124.refs_4_), channel_id=1, source_target_pairs={{0,16},{16,0},{1,17},{17,1},{2,18},{18,2},{3,19},{19,3},{4,20},{20... | collective-permute-start | bytes 9437192 | tf_op jit(solution)/shard_map/ppermute | solution.py:517
  440.3 1.6 copy-start.9
  (4 other events, 3.2 us)
Sparse Core Ops, SparseCore 0:
  246.7 198.5 all-reduce.1

commit v3 on v2

--- a/solution.py
+++ b/solution.py
@@ -15,7 +15,7 @@
 STEP = 0.25
 PROBE_STEP = 0.5
 FLOOR = 0.25
-PARTS = (3, 7, 6)
+PARTS = (5, 6, 5)
 VMEM = 56 * 2**20
 
 
@@ -175,7 +175,7 @@
 
 
 def cost(flops, moved):
-    return pl.CostEstimate(flops=int(flops), bytes_accessed=int(moved), transcendentals=0)
+    return pl.CostEstimate(flops=1000, bytes_accessed=1000, transcendentals=0)
 
 
 def anywhere(arrays):

time: 477 us -> 469 us (0.983)
  waiting for transfers between devices: 182 us -> 168 us
    ppermute x3, waiting for transfers between devices: 111 us -> 96.8 us  [local(): lax.ppermute(own[-1], 'energy', energy_route(shift))]
    unnamed x50 -> x56, local copies, waits for them, and re-layouts: 18.4 us -> 20.9 us
  transfers between devices with their start and end apart: 28 -> 28, of which waited for: 9 -> 11; matrix products, arithmetic and copies ran while one was open for 2% -> 1% of each run, Pallas kernels for 39% -> 39%
where the time goes in v3:
time: 469 us; the launch traced here: 466 us
  Pallas kernels  186 us (40%)
  waiting for transfers between devices  168 us (36%)
  starting transfers between devices  69.6 us (15%)
  local copies, waits for them, and re-layouts  27.8 us (6%)
  between operations  14.5 us (3%)
    pallas_call x3, Pallas kernels, gradient_call(): pl.pallas_call(ordered(lambda *refs: gradient_kernel(*scales, *refs), 10,...  117 us
    ppermute x3, waiting for transfers between devices, local(): lax.ppermute(own[-1], 'energy', energy_route(shift))  96.8 us
    ppermute x24, waiting for transfers between devices, toward(): return lax.ppermute(block, axis, route)  70.6 us
    ppermute x24, starting transfers between devices, toward(): return lax.ppermute(block, axis, route)  67 us
    unnamed x56, local copies, waits for them, and re-layouts  20.9 us
    pallas_call x3, Pallas kernels, step_call(): pl.pallas_call(ordered(step_kernel, 6, after), grid=(count,), in_specs=[l...  20.8 us
    pallas_call x1, Pallas kernels, couple_call(): pl.pallas_call(ordered(couple_kernel, 2 + len(parts), after), grid=(tile...  18.4 us
    pallas_call x3, Pallas kernels, pack_call(): pl.pallas_call(ordered(pack_kernel, 6, after), grid=(count,), in_specs=[l...  15.6 us
  transfers between devices with their start and end apart: 28, of which 11 were waited for; matrix products, arithmetic and copies ran while one was open for 1% of the time, Pallas kernels for 39%

profile of v3, /device:TPU:0, one launch (start us, length us, event | category | flops | bytes accessed | tf_op | source)
XLA Modules:
  0.0 466.2 jit_solution(8255662037809088958)
XLA Ops:
  7.2 3.1 fusion.4
  10.3 5.0 %collective-permute-start = (f32[2,5,64,256]{3,2,1,0:T(8,128)S(1)}, f32[2,5,64,256]{3,2,1,0:T(8,128)S(1)}, u32[]{:S(2)}, u32[]{:S(2)}) collective-permute-start(f32[2,5,64,256]{3,2,1,0:T(8,128)S(1)} %get-tuple-element.53), channel_id=1, source_target_pairs={{0,4},{4,8},{8,12},{1,5},{5,9},{9,13},{2,6},{6,10},{10,14},{3,7},{... | collective-permute-start | bytes 1966088 | tf_op jit(solution)/shard_map/ppermute | solution.py:468
  15.3 1.3 collective-permute-start.1
  16.6 12.6 %collective-permute-done.refs_2_.refs_3_ = f32[2,5,64,256]{3,2,1,0:T(8,128)S(1)} collective-permute-done((f32[2,5,64,256]{3,2,1,0:T(8,128)S(1)}, f32[2,5,64,256]{3,2,1,0:T(8,128)S(1)}, u32[]{:S(2)}, u32[]{:S(2)}) %collective-permute-start) | collective-permute-done | bytes 655392 | tf_op jit(solution)/shard_map/ppermute | solution.py:468
  29.2 4.2 collective-permute-done.1.refs_4_.refs_5_.refs_3_
  34.2 5.0 %shard_map.113 = (f32[2,5,192,128]{3,2,1,0:T(8,128)}, f32[2,5,192,128]{3,2,1,0:T(8,128)}) custom-call(f32[2,16,256,256]{3,2,1,0:T(8,128)} %refs_0_.11, f32[2,16,256,256]{3,2,1,0:T(8,128)} %refs_0_.11, f32[2,5,64,256]{3,2,1,0:T(8,128)} %copy-done.10, f32[2,5,64,256]{3,2,1,0:T(8,128)} %copy-done.10, f32[2,5,64,256]{3,2,1,0:T(8,128)} %copy-done.11, ...), custom_call_target="tpu_custom_call" | custom-call | flops 1000 | bytes 1000 | tf_op jit(solution)/shard_map/pallas_call | solution.py:270
  39.2 1.5 collective-permute-start.2
  40.7 1.3 collective-permute-start.3
  42.0 2.4 fusion.5
  44.4 3.5 collective-permute-start.8
  47.9 1.3 collective-permute-start.9
  51.0 36.8 %shard_map.114 = (f32[2,5,384,256]{3,2,1,0:T(8,128)}, f32[2,5,192,128]{3,2,1,0:T(8,128)}, f32[2,5,192,128]{3,2,1,0:T(8,128)}, f32[2,16,256,256]{3,2,1,0:T(8,128)}) custom-call(s32[8]{0:T(128)} %reshape.12.refs_0_, f32[2,16,256,256]{3,2,1,0:T(8,128)} %refs_0_.11, f32[2,5,64,256]{3,2,1,0:T(8,128)} %copy-done.10, f32[2,5,64,256]{3,2,1,0:T(8,128)} %copy-done.11, ...), custom_call_target="tpu_custom_call" | custom-call | flops 1000 | bytes 1000 | tf_op jit(solution)/shard_map/pallas_call | solution.py:212
  87.8 10.1 %collective-permute-start.4 = (f32[2,5,192,128]{3,2,1,0:T(8,128)}, f32[2,5,192,128]{3,2,1,0:T(8,128)S(1)}, u32[]{:S(2)}, u32[]{:S(2)}) collective-permute-start(f32[2,5,192,128]{3,2,1,0:T(8,128)} %get-tuple-element.29), channel_id=1, source_target_pairs={{0,1},{1,2},{2,3},{4,5},{5,6},{6,7},{8,9},{9,10},{10,11},{12,13},{... | collective-permute-start | bytes 2949128 | tf_op jit(solution)/shard_map/ppermute | solution.py:468
  97.9 1.3 collective-permute-start.5
  99.2 3.4 collective-permute-start.16
  104.4 5.6 %shard_map.117 = (f32[2,6,192,128]{3,2,1,0:T(8,128)}, f32[2,6,192,128]{3,2,1,0:T(8,128)}) custom-call(f32[2,16,256,256]{3,2,1,0:T(8,128)} %refs_0_.11, f32[2,16,256,256]{3,2,1,0:T(8,128)} %refs_0_.11, f32[2,6,64,256]{3,2,1,0:T(8,128)} %copy-done.6, f32[2,6,64,256]{3,2,1,0:T(8,128)} %copy-done.6, f32[2,6,64,256]{3,2,1,0:T(8,128)} %copy-done.7, ...), custom_call_target="tpu_custom_call" | custom-call | flops 1000 | bytes 1000 | tf_op jit(solution)/shard_map/pallas_call | solution.py:270
  110.0 2.8 collective-permute-start.10
  114.2 1.3 collective-permute-start.17
  116.5 4.5 shard_map.115
  121.0 4.6 collective-permute-start.6
  126.9 5.9 %collective-permute-done.17.refs_4_.refs_5_.refs_3_ = f32[2,5,64,256]{3,2,1,0:T(8,128)S(1)} collective-permute-done((f32[2,5,64,256]{3,2,1,0:T(8,128)}, f32[2,5,64,256]{3,2,1,0:T(8,128)S(1)}, u32[]{:S(2)}, u32[]{:S(2)}) %collective-permute-start.17) | collective-permute-done | bytes 655392 | tf_op jit(solution)/shard_map/ppermute | solution.py:468
  133.7 5.0 %shard_map.121 = (f32[2,5,192,128]{3,2,1,0:T(8,128)}, f32[2,5,192,128]{3,2,1,0:T(8,128)}) custom-call(f32[2,16,256,256]{3,2,1,0:T(8,128)} %refs_0_.11, f32[2,16,256,256]{3,2,1,0:T(8,128)} %refs_0_.11, f32[2,5,64,256]{3,2,1,0:T(8,128)} %copy-done.8, f32[2,5,64,256]{3,2,1,0:T(8,128)} %copy-done.8, f32[2,5,64,256]{3,2,1,0:T(8,128)} %copy-done.9, ...), custom_call_target="tpu_custom_call" | custom-call | flops 1000 | bytes 1000 | tf_op jit(solution)/shard_map/pallas_call | solution.py:270
  138.7 4.2 collective-permute-start.18
  142.9 1.5 collective-permute-start.19
  144.4 2.5 collective-permute-done.7.refs_5_
  147.7 6.7 %shard_map.116.refs_6_.refs_2_ = f32[2,5,256,256]{3,2,1,0:T(8,128)} custom-call(f32[2,16,256,256]{3,2,1,0:T(8,128)} %refs_0_.11, f32[2,5,384,256]{3,2,1,0:T(8,128)} %get-tuple-element.28.refs_0_.refs_1_, f32[2,5,192,128]{3,2,1,0:T(8,128)} %copy-done.4, f32[2,5,192,128]{3,2,1,0:T(8,128)} %copy-done.5, f32[2,5,64,256]{3,2,1,0:T(8,128)} %copy-done.21, ...), custom_call_target="tpu_custom_call" | custom-call | flops 1000 | bytes 1000 | tf_op jit(solution)/shard_map/pallas_call | solution.py:364
  154.4 1.5 collective-permute-start.24
  157.3 43.4 %shard_map.118 = (f32[2,6,384,256]{3,2,1,0:T(8,128)}, f32[2,6,192,128]{3,2,1,0:T(8,128)}, f32[2,6,192,128]{3,2,1,0:T(8,128)}, f32[2,16,256,256]{3,2,1,0:T(8,128)}) custom-call(s32[8]{0:T(128)} %reshape.12.refs_0_, f32[2,16,256,256]{3,2,1,0:T(8,128)} %refs_0_.11, f32[2,6,64,256]{3,2,1,0:T(8,128)} %copy-done.6, ...), custom_call_target="tpu_custom_call", output_to_operand_aliasing={{3}: (10, {})} | custom-call | flops 1000 | bytes 1000 | tf_op jit(solution)/shard_map/pallas_call | solution.py:212
  200.7 2.9 collective-permute-start.12
  203.6 1.3 collective-permute-start.13
  206.2 36.9 %shard_map.122 = (f32[2,5,384,256]{3,2,1,0:T(8,128)}, f32[2,5,192,128]{3,2,1,0:T(8,128)}, f32[2,5,192,128]{3,2,1,0:T(8,128)}, f32[2,16,256,256]{3,2,1,0:T(8,128)}) custom-call(s32[8]{0:T(128)} %reshape.12.refs_0_, f32[2,16,256,256]{3,2,1,0:T(8,128)} %refs_0_.11, f32[2,5,64,256]{3,2,1,0:T(8,128)} %copy-done.8, ...), custom_call_target="tpu_custom_call", output_to_operand_aliasing={{3}: (10, {})} | custom-call | flops 1000 | bytes 1000 | tf_op jit(solution)/shard_map/pallas_call | solution.py:212
  243.1 5.2 %collective-permute-start.20 = (f32[2,5,192,128]{3,2,1,0:T(8,128)}, f32[2,5,192,128]{3,2,1,0:T(8,128)S(1)}, u32[]{:S(2)}, u32[]{:S(2)}) collective-permute-start(f32[2,5,192,128]{3,2,1,0:T(8,128)} %get-tuple-element.45), channel_id=1, source_target_pairs={{0,1},{1,2},{2,3},{4,5},{5,6},{6,7},{8,9},{9,10},{10,11},{12,13},{... | collective-permute-start | bytes 2949128 | tf_op jit(solution)/shard_map/ppermute | solution.py:468
  248.3 1.5 collective-permute-start.21
  251.3 5.1 %shard_map.119 = (f32[2,6,64,256]{3,2,1,0:T(8,128)}, f32[2,6,64,256]{3,2,1,0:T(8,128)}) custom-call(f32[2,6,384,256]{3,2,1,0:T(8,128)} %get-tuple-element.36.refs_0_.refs_1_, f32[2,6,384,256]{3,2,1,0:T(8,128)} %get-tuple-element.36.refs_0_.refs_1_, f32[2,6,192,128]{3,2,1,0:T(8,128)} %copy-done.1, f32[2,6,192,128]{3,2,1,0:T(8,128)} %copy-done.1, ...), custom_call_target="tpu_custom_call" | custom-call | flops 1000 | bytes 1000 | tf_op jit(solution)/shard_map/pallas_call | solution.py:318
  256.4 3.4 collective-permute-start.14
  262.1 4.5 shard_map.123
  266.7 4.6 collective-permute-start.22
  271.2 1.3 collective-permute-start.23
  272.5 21.7 %collective-permute-done.14.refs_4_ = f32[2,6,64,256]{3,2,1,0:T(8,128)S(1)} collective-permute-done((f32[2,6,64,256]{3,2,1,0:T(8,128)}, f32[2,6,64,256]{3,2,1,0:T(8,128)S(1)}, u32[]{:S(2)}, u32[]{:S(2)}) %collective-permute-start.14) | collective-permute-done | bytes 786464 | tf_op jit(solution)/shard_map/ppermute | solution.py:468
  294.3 4.4 collective-permute-done.15.refs_5_
  299.5 7.3 %shard_map.120.refs_6_.refs_3_ = f32[2,6,256,256]{3,2,1,0:T(8,128)} custom-call(f32[2,16,256,256]{3,2,1,0:T(8,128)} %refs_0_.11, f32[2,6,384,256]{3,2,1,0:T(8,128)} %get-tuple-element.36.refs_0_.refs_1_, f32[2,6,192,128]{3,2,1,0:T(8,128)} %copy-done.1, f32[2,6,192,128]{3,2,1,0:T(8,128)} %copy-done.2, f32[2,6,64,256]{3,2,1,0:T(8,128)} %copy-done.18, ...), custom_call_target="tpu_custom_call" | custom-call | flops 1000 | bytes 1000 | tf_op jit(solution)/shard_map/pallas_call | solution.py:364
  307.4 14.9 %collective-permute-done.22.refs_4_ = f32[2,5,64,256]{3,2,1,0:T(8,128)S(1)} collective-permute-done((f32[2,5,64,256]{3,2,1,0:T(8,128)}, f32[2,5,64,256]{3,2,1,0:T(8,128)S(1)}, u32[]{:S(2)}, u32[]{:S(2)}) %collective-permute-start.22) | collective-permute-done | bytes 655392 | tf_op jit(solution)/shard_map/ppermute | solution.py:468
  322.3 4.4 collective-permute-done.23.refs_5_
  327.6 6.8 %shard_map.124.refs_4_ = f32[2,5,256,256]{3,2,1,0:T(8,128)} custom-call(f32[2,16,256,256]{3,2,1,0:T(8,128)} %refs_0_.11, f32[2,5,384,256]{3,2,1,0:T(8,128)} %get-tuple-element.44.refs_0_.refs_1_, f32[2,5,192,128]{3,2,1,0:T(8,128)} %copy-done.3, f32[2,5,192,128]{3,2,1,0:T(8,128)} %collective-permute-done.21.refs_4_.refs_5_.refs_3_, ...), custom_call_target="tpu_custom_call" | custom-call | flops 1000 | bytes 1000 | tf_op jit(solution)/shard_map/pallas_call | solution.py:364
  336.2 40.5 %collective-permute-done.25.refs_6_ = f32[2,6,256,256]{3,2,1,0:T(8,128)S(1)} collective-permute-done((f32[2,6,256,256]{3,2,1,0:T(8,128)}, f32[2,6,256,256]{3,2,1,0:T(8,128)S(1)}, u32[]{:S(2)}, u32[]{:S(2)}) %collective-permute-start.25) | collective-permute-done | bytes 3145760 | tf_op jit(solution)/shard_map/ppermute | solution.py:517
  376.7 56.3 %collective-permute-done.26.refs_7_ = f32[2,5,256,256]{3,2,1,0:T(8,128)} collective-permute-done((f32[2,5,256,256]{3,2,1,0:T(8,128)}, f32[2,5,256,256]{3,2,1,0:T(8,128)}, u32[]{:S(2)}, u32[]{:S(2)}) %collective-permute-start.26) | collective-permute-done | bytes 2621472 | tf_op jit(solution)/shard_map/ppermute | solution.py:517
  433.0 18.4 %shard_map.125 = f32[2,16,256,256]{3,2,1,0:T(8,128)} custom-call(f32[32,64]{1,0:T(8,128)} %reshape.11.refs_0_, bf16[64,512]{1,0:T(8,128)(2,1)} %fusion.refs_1_, f32[2,5,256,256]{3,2,1,0:T(8,128)} %shard_map.116.refs_6_.refs_2_, f32[2,6,256,256]{3,2,1,0:T(8,128)} %shard_map.120.refs_6_.refs_3_, f32[2,5,256,256]{3,2,1,0:T(8,128)} %shard_map.124.refs_4_, ...), custom_call_target="tpu_custom_call" | custom-call | flops 1000 | bytes 1000 | tf_op jit(solution)/shard_map/pallas_call | solution.py:428
  451.7 7.7 %copy.21 = f32[2,16,256,256]{3,2,1,0:T(8,128)} copy(f32[2,16,256,256]{3,2,1,0:T(8,128)} %all-reduce.2.cloned.1.call-done) | data formatting | bytes 16777216
  (86 shorter events, 20.5 us)
Async XLA Ops:
  7.2 327.6 %copy-start = (f32[2,2,32,32]{3,2,1,0:T(8,128)S(1)}, f32[2,2,32,32]{3,2,1,0:T(8,128)}, u32[]{:S(2)}) copy-start(f32[2,2,32,32]{3,2,1,0:T(8,128)} %param.13) | copy-start | bytes 49156
  7.2 444.5 %all-reduce.2.cloned.1.call-start = ((), (), s32[]{:S(2)}) async-start(), calls=%async_computation | async-start | bytes 16777216 | tf_op jit(solution)/shard_map/psum | solution.py:508
  10.3 18.9 %collective-permute-start = (f32[2,5,64,256]{3,2,1,0:T(8,128)S(1)}, f32[2,5,64,256]{3,2,1,0:T(8,128)S(1)}, u32[]{:S(2)}, u32[]{:S(2)}) collective-permute-start(f32[2,5,64,256]{3,2,1,0:T(8,128)S(1)} %get-tuple-element.53), channel_id=1, source_target_pairs={{0,4},{4,8},{8,12},{1,5},{5,9},{9,13},{2,6},{6,10},{10,14},{3,7},{... | collective-permute-start | bytes 1966088 | tf_op jit(solution)/shard_map/ppermute | solution.py:468
  15.3 18.1 %collective-permute-start.1 = (f32[2,5,64,256]{3,2,1,0:T(8,128)S(1)}, f32[2,5,64,256]{3,2,1,0:T(8,128)S(1)}, u32[]{:S(2)}, u32[]{:S(2)}) collective-permute-start(f32[2,5,64,256]{3,2,1,0:T(8,128)S(1)} %get-tuple-element.52), channel_id=1, source_target_pairs={{4,0},{8,4},{12,8},{5,1},{9,5},{13,9},{6,2},{10,6},{14,10},{7,3},{... | collective-permute-start | bytes 1966088 | tf_op jit(solution)/shard_map/ppermute | solution.py:468
  29.2 4.2 copy-start.10
  39.2 10.0 %copy-start.26 = (s32[1,1,4,2]{2,3,1,0:T(2,128)S(1)}, s32[1,1,4,2]{2,3,1,0:T(2,128)}, u32[]{:S(2)}) copy-start(s32[1,1,4,2]{2,3,1,0:T(2,128)} %param.14) | copy-start | bytes 100
  39.2 10.8 %collective-permute-start.2 = (f32[2,5,192,128]{3,2,1,0:T(8,128)}, f32[2,5,192,128]{3,2,1,0:T(8,128)S(1)}, u32[]{:S(2)}, u32[]{:S(2)}) collective-permute-start(f32[2,5,192,128]{3,2,1,0:T(8,128)} %get-tuple-element.26), channel_id=1, source_target_pairs={{0,1},{1,2},{2,3},{4,5},{5,6},{6,7},{8,9},{9,10},{10,11},{12,13},{... | collective-permute-start | bytes 2949128 | tf_op jit(solution)/shard_map/ppermute | solution.py:468
  40.7 9.3 %collective-permute-start.3 = (f32[2,5,192,128]{3,2,1,0:T(8,128)}, f32[2,5,192,128]{3,2,1,0:T(8,128)}, u32[]{:S(2)}, u32[]{:S(2)}) collective-permute-start(f32[2,5,192,128]{3,2,1,0:T(8,128)} %get-tuple-element.27), channel_id=1, source_target_pairs={{1,0},{2,1},{3,2},{5,4},{6,5},{7,6},{9,8},{10,9},{11,10},{13,12},{... | collective-permute-start | bytes 2949128 | tf_op jit(solution)/shard_map/ppermute | solution.py:468
  44.4 58.2 %collective-permute-start.8 = (f32[2,6,64,256]{3,2,1,0:T(8,128)}, f32[2,6,64,256]{3,2,1,0:T(8,128)S(1)}, u32[]{:S(2)}, u32[]{:S(2)}) collective-permute-start(f32[2,6,64,256]{3,2,1,0:T(8,128)} %get-tuple-element.55), channel_id=1, source_target_pairs={{0,4},{4,8},{8,12},{1,5},{5,9},{9,13},{2,6},{6,10},{10,14},{3,7},{... | collective-permute-start | bytes 2359304 | tf_op jit(solution)/shard_map/ppermute | solution.py:468
  47.9 54.7 %collective-permute-start.9 = (f32[2,6,64,256]{3,2,1,0:T(8,128)S(1)}, f32[2,6,64,256]{3,2,1,0:T(8,128)S(1)}, u32[]{:S(2)}, u32[]{:S(2)}) collective-permute-start(f32[2,6,64,256]{3,2,1,0:T(8,128)S(1)} %get-tuple-element.54), channel_id=1, source_target_pairs={{4,0},{8,4},{12,8},{5,1},{9,5},{13,9},{6,2},{10,6},{14,10},{7,3},{... | collective-permute-start | bytes 2359304 | tf_op jit(solution)/shard_map/ppermute | solution.py:468
  50.0 1.0 copy-start.17
  87.8 26.4 %collective-permute-start.4 = (f32[2,5,192,128]{3,2,1,0:T(8,128)}, f32[2,5,192,128]{3,2,1,0:T(8,128)S(1)}, u32[]{:S(2)}, u32[]{:S(2)}) collective-permute-start(f32[2,5,192,128]{3,2,1,0:T(8,128)} %get-tuple-element.29), channel_id=1, source_target_pairs={{0,1},{1,2},{2,3},{4,5},{5,6},{6,7},{8,9},{9,10},{10,11},{12,13},{... | collective-permute-start | bytes 2949128 | tf_op jit(solution)/shard_map/ppermute | solution.py:468
  97.9 17.6 %collective-permute-start.5 = (f32[2,5,192,128]{3,2,1,0:T(8,128)}, f32[2,5,192,128]{3,2,1,0:T(8,128)S(1)}, u32[]{:S(2)}, u32[]{:S(2)}) collective-permute-start(f32[2,5,192,128]{3,2,1,0:T(8,128)} %get-tuple-element.30), channel_id=1, source_target_pairs={{1,0},{2,1},{3,2},{5,4},{6,5},{7,6},{9,8},{10,9},{11,10},{13,12},{... | collective-permute-start | bytes 2949128 | tf_op jit(solution)/shard_map/ppermute | solution.py:468
  99.2 26.4 %collective-permute-start.16 = (f32[2,5,64,256]{3,2,1,0:T(8,128)}, f32[2,5,64,256]{3,2,1,0:T(8,128)S(1)}, u32[]{:S(2)}, u32[]{:S(2)}) collective-permute-start(f32[2,5,64,256]{3,2,1,0:T(8,128)} %get-tuple-element.51), channel_id=1, source_target_pairs={{0,4},{4,8},{8,12},{1,5},{5,9},{9,13},{2,6},{6,10},{10,14},{3,7},{... | collective-permute-start | bytes 1966088 | tf_op jit(solution)/shard_map/ppermute | solution.py:468
  110.0 45.9 %collective-permute-start.10 = (f32[2,6,192,128]{3,2,1,0:T(8,128)}, f32[2,6,192,128]{3,2,1,0:T(8,128)S(1)}, u32[]{:S(2)}, u32[]{:S(2)}) collective-permute-start(f32[2,6,192,128]{3,2,1,0:T(8,128)} %get-tuple-element.33), channel_id=1, source_target_pairs={{0,1},{1,2},{2,3},{4,5},{5,6},{6,7},{8,9},{9,10},{10,11},{12,13},{... | collective-permute-start | bytes 3538952 | tf_op jit(solution)/shard_map/ppermute | solution.py:468
  112.9 43.0 %collective-permute-start.11 = (f32[2,6,192,128]{3,2,1,0:T(8,128)}, f32[2,6,192,128]{3,2,1,0:T(8,128)S(1)}, u32[]{:S(2)}, u32[]{:S(2)}) collective-permute-start(f32[2,6,192,128]{3,2,1,0:T(8,128)} %get-tuple-element.34), channel_id=1, source_target_pairs={{1,0},{2,1},{3,2},{5,4},{6,5},{7,6},{9,8},{10,9},{11,10},{13,12},{... | collective-permute-start | bytes 3538952 | tf_op jit(solution)/shard_map/ppermute | solution.py:468
  114.2 1.3 copy-start.4
  114.2 18.6 %collective-permute-start.17 = (f32[2,5,64,256]{3,2,1,0:T(8,128)}, f32[2,5,64,256]{3,2,1,0:T(8,128)S(1)}, u32[]{:S(2)}, u32[]{:S(2)}) collective-permute-start(f32[2,5,64,256]{3,2,1,0:T(8,128)} %get-tuple-element.50), channel_id=1, source_target_pairs={{4,0},{8,4},{12,8},{5,1},{9,5},{13,9},{6,2},{10,6},{14,10},{7,3},{... | collective-permute-start | bytes 1966088 | tf_op jit(solution)/shard_map/ppermute | solution.py:468
  115.5 1.0 copy-start.5
  121.0 21.9 %collective-permute-start.6 = (f32[2,5,64,256]{3,2,1,0:T(8,128)}, f32[2,5,64,256]{3,2,1,0:T(8,128)S(1)}, u32[]{:S(2)}, u32[]{:S(2)}) collective-permute-start(f32[2,5,64,256]{3,2,1,0:T(8,128)} %get-tuple-element.31), channel_id=1, source_target_pairs={{0,4},{4,8},{8,12},{1,5},{5,9},{9,13},{2,6},{6,10},{10,14},{3,7},{... | collective-permute-start | bytes 1966088 | tf_op jit(solution)/shard_map/ppermute | solution.py:468
  125.6 7.2 %copy-start.8 = (f32[2,5,64,256]{3,2,1,0:T(8,128)}, f32[2,5,64,256]{3,2,1,0:T(8,128)S(1)}, u32[]{:S(2)}) copy-start(f32[2,5,64,256]{3,2,1,0:T(8,128)S(1)} %collective-permute-done.16.refs_2_.refs_3_) | copy-start | bytes 1966084
  125.6 21.3 %collective-permute-start.7 = (f32[2,5,64,256]{3,2,1,0:T(8,128)}, f32[2,5,64,256]{3,2,1,0:T(8,128)S(1)}, u32[]{:S(2)}, u32[]{:S(2)}) collective-permute-start(f32[2,5,64,256]{3,2,1,0:T(8,128)} %get-tuple-element.32.refs_11_), channel_id=1, source_target_pairs={{4,0},{8,4},{12,8},{5,1},{9,5},{13,9},{6,2},{10,6},{14,10},{7,3},{... | collective-permute-start | bytes 1966088 | tf_op jit(solution)/shard_map/ppermute | solution.py:468
  138.7 66.3 %collective-permute-start.18 = (f32[2,5,192,128]{3,2,1,0:T(8,128)}, f32[2,5,192,128]{3,2,1,0:T(8,128)S(1)}, u32[]{:S(2)}, u32[]{:S(2)}) collective-permute-start(f32[2,5,192,128]{3,2,1,0:T(8,128)} %get-tuple-element.41), channel_id=1, source_target_pairs={{0,1},{1,2},{2,3},{4,5},{5,6},{6,7},{8,9},{9,10},{10,11},{12,13},{... | collective-permute-start | bytes 2949128 | tf_op jit(solution)/shard_map/ppermute | solution.py:468
  142.9 4.0 copy-start.21
  142.9 62.1 %collective-permute-start.19 = (f32[2,5,192,128]{3,2,1,0:T(8,128)}, f32[2,5,192,128]{3,2,1,0:T(8,128)S(1)}, u32[]{:S(2)}, u32[]{:S(2)}) collective-permute-start(f32[2,5,192,128]{3,2,1,0:T(8,128)} %get-tuple-element.42), channel_id=1, source_target_pairs={{1,0},{2,1},{3,2},{5,4},{6,5},{7,6},{9,8},{10,9},{11,10},{13,12},{... | collective-permute-start | bytes 2949128 | tf_op jit(solution)/shard_map/ppermute | solution.py:468
  154.4 172.3 %collective-permute-start.24 = (f32[2,5,256,256]{3,2,1,0:T(8,128)}, f32[2,5,256,256]{3,2,1,0:T(8,128)}, u32[]{:S(2)}, u32[]{:S(2)}) collective-permute-start(f32[2,5,256,256]{3,2,1,0:T(8,128)} %shard_map.116.refs_6_.refs_2_), channel_id=1, source_target_pairs={{0,16},{16,0},{1,17},{17,1},{2,18},{18,2},{3,19},{19,3},{4,20},{20... | collective-permute-start | bytes 7864328 | tf_op jit(solution)/shard_map/ppermute | solution.py:517
  155.9 1.0 copy-start.13
  155.9 1.4 copy-start.14
  200.7 49.1 %collective-permute-start.12 = (f32[2,6,192,128]{3,2,1,0:T(8,128)}, f32[2,6,192,128]{3,2,1,0:T(8,128)S(1)}, u32[]{:S(2)}, u32[]{:S(2)}) collective-permute-start(f32[2,6,192,128]{3,2,1,0:T(8,128)} %get-tuple-element.37), channel_id=1, source_target_pairs={{0,1},{1,2},{2,3},{4,5},{5,6},{6,7},{8,9},{9,10},{10,11},{12,13},{... | collective-permute-start | bytes 3538952 | tf_op jit(solution)/shard_map/ppermute | solution.py:468
  203.6 46.2 %collective-permute-start.13 = (f32[2,6,192,128]{3,2,1,0:T(8,128)}, f32[2,6,192,128]{3,2,1,0:T(8,128)S(1)}, u32[]{:S(2)}, u32[]{:S(2)}) collective-permute-start(f32[2,6,192,128]{3,2,1,0:T(8,128)} %get-tuple-element.38), channel_id=1, source_target_pairs={{1,0},{2,1},{3,2},{5,4},{6,5},{7,6},{9,8},{10,9},{11,10},{13,12},{... | collective-permute-start | bytes 3538952 | tf_op jit(solution)/shard_map/ppermute | solution.py:468
  205.0 1.0 copy-start.15
  205.0 1.3 copy-start.16
  243.1 18.0 %collective-permute-start.20 = (f32[2,5,192,128]{3,2,1,0:T(8,128)}, f32[2,5,192,128]{3,2,1,0:T(8,128)S(1)}, u32[]{:S(2)}, u32[]{:S(2)}) collective-permute-start(f32[2,5,192,128]{3,2,1,0:T(8,128)} %get-tuple-element.45), channel_id=1, source_target_pairs={{0,1},{1,2},{2,3},{4,5},{5,6},{6,7},{8,9},{9,10},{10,11},{12,13},{... | collective-permute-start | bytes 2949128 | tf_op jit(solution)/shard_map/ppermute | solution.py:468
  248.3 12.8 %collective-permute-start.21 = (f32[2,5,192,128]{3,2,1,0:T(8,128)}, f32[2,5,192,128]{3,2,1,0:T(8,128)}, u32[]{:S(2)}, u32[]{:S(2)}) collective-permute-start(f32[2,5,192,128]{3,2,1,0:T(8,128)} %get-tuple-element.46), channel_id=1, source_target_pairs={{1,0},{2,1},{3,2},{5,4},{6,5},{7,6},{9,8},{10,9},{11,10},{13,12},{... | collective-permute-start | bytes 2949128 | tf_op jit(solution)/shard_map/ppermute | solution.py:468
  249.9 1.0 copy-start.1
  249.9 1.4 copy-start.2
  256.4 37.9 %collective-permute-start.14 = (f32[2,6,64,256]{3,2,1,0:T(8,128)}, f32[2,6,64,256]{3,2,1,0:T(8,128)S(1)}, u32[]{:S(2)}, u32[]{:S(2)}) collective-permute-start(f32[2,6,64,256]{3,2,1,0:T(8,128)} %get-tuple-element.39), channel_id=1, source_target_pairs={{0,4},{4,8},{8,12},{1,5},{5,9},{9,13},{2,6},{6,10},{10,14},{3,7},{... | collective-permute-start | bytes 2359304 | tf_op jit(solution)/shard_map/ppermute | solution.py:468
  259.8 38.8 %collective-permute-start.15 = (f32[2,6,64,256]{3,2,1,0:T(8,128)}, f32[2,6,64,256]{3,2,1,0:T(8,128)S(1)}, u32[]{:S(2)}, u32[]{:S(2)}) collective-permute-start(f32[2,6,64,256]{3,2,1,0:T(8,128)} %get-tuple-element.40), channel_id=1, source_target_pairs={{4,0},{8,4},{12,8},{5,1},{9,5},{13,9},{6,2},{10,6},{14,10},{7,3},{... | collective-permute-start | bytes 2359304 | tf_op jit(solution)/shard_map/ppermute | solution.py:468
  261.1 1.0 copy-start.3
  266.7 55.7 %collective-permute-start.22 = (f32[2,5,64,256]{3,2,1,0:T(8,128)}, f32[2,5,64,256]{3,2,1,0:T(8,128)S(1)}, u32[]{:S(2)}, u32[]{:S(2)}) collective-permute-start(f32[2,5,64,256]{3,2,1,0:T(8,128)} %get-tuple-element.47), channel_id=1, source_target_pairs={{0,4},{4,8},{8,12},{1,5},{5,9},{9,13},{2,6},{6,10},{10,14},{3,7},{... | collective-permute-start | bytes 1966088 | tf_op jit(solution)/shard_map/ppermute | solution.py:468
  271.2 55.5 %collective-permute-start.23 = (f32[2,5,64,256]{3,2,1,0:T(8,128)}, f32[2,5,64,256]{3,2,1,0:T(8,128)S(1)}, u32[]{:S(2)}, u32[]{:S(2)}) collective-permute-start(f32[2,5,64,256]{3,2,1,0:T(8,128)} %get-tuple-element.48), channel_id=1, source_target_pairs={{4,0},{8,4},{12,8},{5,1},{9,5},{13,9},{6,2},{10,6},{14,10},{7,3},{... | collective-permute-start | bytes 1966088 | tf_op jit(solution)/shard_map/ppermute | solution.py:468
  294.3 4.4 copy-start.18
  306.8 28.7 %copy-start.24 = (s32[512]{0:T(512)S(1)}, s32[512]{0:T(512)}, u32[]{:S(2)}) copy-start(s32[512]{0:T(512)} %constant.45) | copy-start | bytes 6148
  306.8 28.7 %copy-start.25 = (s32[512]{0:T(512)S(1)}, s32[512]{0:T(512)}, u32[]{:S(2)}) copy-start(s32[512]{0:T(512)} %constant.44) | copy-start | bytes 6148
  306.8 69.9 %collective-permute-start.25 = (f32[2,6,256,256]{3,2,1,0:T(8,128)}, f32[2,6,256,256]{3,2,1,0:T(8,128)S(1)}, u32[]{:S(2)}, u32[]{:S(2)}) collective-permute-start(f32[2,6,256,256]{3,2,1,0:T(8,128)} %shard_map.120.refs_6_.refs_3_), channel_id=1, source_target_pairs={{0,16},{16,0},{1,17},{17,1},{2,18},{18,2},{3,19},{19,3},{4,20},{20... | collective-permute-start | bytes 9437192 | tf_op jit(solution)/shard_map/ppermute | solution.py:517
  322.3 4.4 copy-start.20
  334.4 98.6 %collective-permute-start.26 = (f32[2,5,256,256]{3,2,1,0:T(8,128)}, f32[2,5,256,256]{3,2,1,0:T(8,128)}, u32[]{:S(2)}, u32[]{:S(2)}) collective-permute-start(f32[2,5,256,256]{3,2,1,0:T(8,128)} %shard_map.124.refs_4_), channel_id=1, source_target_pairs={{0,16},{16,0},{1,17},{17,1},{2,18},{18,2},{3,19},{19,3},{4,20},{20... | collective-permute-start | bytes 7864328 | tf_op jit(solution)/shard_map/ppermute | solution.py:517
  376.7 56.3 %copy-start.12 = (f32[2,6,256,256]{3,2,1,0:T(8,128)}, f32[2,6,256,256]{3,2,1,0:T(8,128)S(1)}, u32[]{:S(2)}) copy-start(f32[2,6,256,256]{3,2,1,0:T(8,128)S(1)} %collective-permute-done.25.refs_6_) | copy-start | bytes 9437188
  (7 other events, 6.1 us)
Sparse Core Ops, SparseCore 0:
  250.0 201.6 all-reduce.1

commit v4 on v3

--- a/solution.py
+++ b/solution.py
@@ -509,7 +509,7 @@
     for i, (first, count) in enumerate(spans):
         if i >= len(rims):
             trim(i)
-        after = own[-1:]
+        after = own[-1:] or [x[1] for x in grads[1:2]]
         if i == len(spans) - 1:
             after = after + [group[0] for group in other]
         own.append(step_call(object_field, *rims[i], first, after))

time: 469 us -> 469 us (level)
  transfers between devices with their start and end apart: 28 -> 28, of which waited for: 11 -> 10; matrix products, arithmetic and copies ran while one was open for 1% -> 1% of each run, Pallas kernels for 39% -> 39%
where the time goes in v4:
time: 469 us; the launch traced here: 466 us
  Pallas kernels  185 us (39%)
  waiting for transfers between devices  165 us (35%)
  starting transfers between devices  73.3 us (16%)
  local copies, waits for them, and re-layouts  27.4 us (6%)
  between operations  14.5 us (3%)
    pallas_call x3, Pallas kernels, gradient_call(): pl.pallas_call(ordered(lambda *refs: gradient_kernel(*scales, *refs), 10,...  116 us
    ppermute x3, waiting for transfers between devices, local(): lax.ppermute(own[-1], 'energy', energy_route(shift))  96.6 us
    ppermute x24, starting transfers between devices, toward(): return lax.ppermute(block, axis, route)  70.8 us
    ppermute x24, waiting for transfers between devices, toward(): return lax.ppermute(block, axis, route)  68 us
    pallas_call x3, Pallas kernels, step_call(): pl.pallas_call(ordered(step_kernel, 6, after), grid=(count,), in_specs=[l...  20.9 us
    unnamed x56, local copies, waits for them, and re-layouts  20.6 us
    pallas_call x1, Pallas kernels, couple_call(): pl.pallas_call(ordered(couple_kernel, 2 + len(parts), after), grid=(tile...  18.4 us
    pallas_call x3, Pallas kernels, pack_call(): pl.pallas_call(ordered(pack_kernel, 6, after), grid=(count,), in_specs=[l...  15.6 us
  transfers between devices with their start and end apart: 28, of which 10 were waited for; matrix products, arithmetic and copies ran while one was open for 1% of the time, Pallas kernels for 39%

profile of v4, /device:TPU:0, one launch (start us, length us, event | category | flops | bytes accessed | tf_op | source)
XLA Modules:
  0.0 465.8 jit_solution(10517169357397715381)
XLA Ops:
  7.2 3.1 fusion.4
  10.3 5.0 %collective-permute-start = (f32[2,5,64,256]{3,2,1,0:T(8,128)S(1)}, f32[2,5,64,256]{3,2,1,0:T(8,128)S(1)}, u32[]{:S(2)}, u32[]{:S(2)}) collective-permute-start(f32[2,5,64,256]{3,2,1,0:T(8,128)S(1)} %get-tuple-element.53), channel_id=1, source_target_pairs={{0,4},{4,8},{8,12},{1,5},{5,9},{9,13},{2,6},{6,10},{10,14},{3,7},{... | collective-permute-start | bytes 1966088 | tf_op jit(solution)/shard_map/ppermute | solution.py:468
  15.2 1.3 collective-permute-start.1
  16.5 12.6 %collective-permute-done.refs_2_.refs_3_ = f32[2,5,64,256]{3,2,1,0:T(8,128)S(1)} collective-permute-done((f32[2,5,64,256]{3,2,1,0:T(8,128)S(1)}, f32[2,5,64,256]{3,2,1,0:T(8,128)S(1)}, u32[]{:S(2)}, u32[]{:S(2)}) %collective-permute-start) | collective-permute-done | bytes 655392 | tf_op jit(solution)/shard_map/ppermute | solution.py:468
  29.2 4.2 collective-permute-done.1.refs_4_.refs_5_.refs_3_
  34.2 5.0 %shard_map.113 = (f32[2,5,192,128]{3,2,1,0:T(8,128)}, f32[2,5,192,128]{3,2,1,0:T(8,128)}) custom-call(f32[2,16,256,256]{3,2,1,0:T(8,128)} %refs_0_.11, f32[2,16,256,256]{3,2,1,0:T(8,128)} %refs_0_.11, f32[2,5,64,256]{3,2,1,0:T(8,128)} %copy-done.10, f32[2,5,64,256]{3,2,1,0:T(8,128)} %copy-done.10, f32[2,5,64,256]{3,2,1,0:T(8,128)} %copy-done.11, ...), custom_call_target="tpu_custom_call" | custom-call | flops 1000 | bytes 1000 | tf_op jit(solution)/shard_map/pallas_call | solution.py:270
  39.2 1.5 collective-permute-start.2
  40.6 1.3 collective-permute-start.3
  41.9 2.4 fusion.5
  44.4 3.5 collective-permute-start.8
  47.9 1.3 collective-permute-start.9
  50.9 36.4 %shard_map.114 = (f32[2,5,384,256]{3,2,1,0:T(8,128)}, f32[2,5,192,128]{3,2,1,0:T(8,128)}, f32[2,5,192,128]{3,2,1,0:T(8,128)}, f32[2,16,256,256]{3,2,1,0:T(8,128)}) custom-call(s32[8]{0:T(128)} %reshape.12.refs_0_, f32[2,16,256,256]{3,2,1,0:T(8,128)} %refs_0_.11, f32[2,5,64,256]{3,2,1,0:T(8,128)} %copy-done.10, f32[2,5,64,256]{3,2,1,0:T(8,128)} %copy-done.11, ...), custom_call_target="tpu_custom_call" | custom-call | flops 1000 | bytes 1000 | tf_op jit(solution)/shard_map/pallas_call | solution.py:212
  87.3 10.8 %collective-permute-start.4 = (f32[2,5,192,128]{3,2,1,0:T(8,128)}, f32[2,5,192,128]{3,2,1,0:T(8,128)S(1)}, u32[]{:S(2)}, u32[]{:S(2)}) collective-permute-start(f32[2,5,192,128]{3,2,1,0:T(8,128)} %get-tuple-element.29), channel_id=1, source_target_pairs={{0,1},{1,2},{2,3},{4,5},{5,6},{6,7},{8,9},{9,10},{10,11},{12,13},{... | collective-permute-start | bytes 2949128 | tf_op jit(solution)/shard_map/ppermute | solution.py:468
  98.0 1.3 collective-permute-start.5
  99.3 3.1 collective-permute-start.16
  104.2 5.6 %shard_map.116 = (f32[2,6,192,128]{3,2,1,0:T(8,128)}, f32[2,6,192,128]{3,2,1,0:T(8,128)}) custom-call(f32[2,16,256,256]{3,2,1,0:T(8,128)} %refs_0_.11, f32[2,16,256,256]{3,2,1,0:T(8,128)} %refs_0_.11, f32[2,6,64,256]{3,2,1,0:T(8,128)} %copy-done.6, f32[2,6,64,256]{3,2,1,0:T(8,128)} %copy-done.6, f32[2,6,64,256]{3,2,1,0:T(8,128)} %copy-done.7, ...), custom_call_target="tpu_custom_call" | custom-call | flops 1000 | bytes 1000 | tf_op jit(solution)/shard_map/pallas_call | solution.py:270
  109.8 2.8 collective-permute-start.10
  112.6 1.3 collective-permute-start.11
  113.9 1.3 collective-permute-start.17
  116.2 4.5 shard_map.115
  120.8 4.6 collective-permute-start.6
  125.4 1.3 collective-permute-start.7
  126.7 5.8 %collective-permute-done.17.refs_4_.refs_5_.refs_3_ = f32[2,5,64,256]{3,2,1,0:T(8,128)S(1)} collective-permute-done((f32[2,5,64,256]{3,2,1,0:T(8,128)}, f32[2,5,64,256]{3,2,1,0:T(8,128)S(1)}, u32[]{:S(2)}, u32[]{:S(2)}) %collective-permute-start.17) | collective-permute-done | bytes 655392 | tf_op jit(solution)/shard_map/ppermute | solution.py:468
  133.3 5.0 %shard_map.121 = (f32[2,5,192,128]{3,2,1,0:T(8,128)}, f32[2,5,192,128]{3,2,1,0:T(8,128)}) custom-call(f32[2,16,256,256]{3,2,1,0:T(8,128)} %refs_0_.11, f32[2,16,256,256]{3,2,1,0:T(8,128)} %refs_0_.11, f32[2,5,64,256]{3,2,1,0:T(8,128)} %copy-done.8, f32[2,5,64,256]{3,2,1,0:T(8,128)} %copy-done.8, f32[2,5,64,256]{3,2,1,0:T(8,128)} %copy-done.9, ...), custom_call_target="tpu_custom_call" | custom-call | flops 1000 | bytes 1000 | tf_op jit(solution)/shard_map/pallas_call | solution.py:270
  138.3 4.5 collective-permute-start.18
  142.7 1.5 collective-permute-start.19
  145.3 42.9 %shard_map.117 = (f32[2,6,384,256]{3,2,1,0:T(8,128)}, f32[2,6,192,128]{3,2,1,0:T(8,128)}, f32[2,6,192,128]{3,2,1,0:T(8,128)}, f32[2,16,256,256]{3,2,1,0:T(8,128)}) custom-call(s32[8]{0:T(128)} %reshape.12.refs_0_, f32[2,16,256,256]{3,2,1,0:T(8,128)} %refs_0_.11, f32[2,6,64,256]{3,2,1,0:T(8,128)} %copy-done.6, ...), custom_call_target="tpu_custom_call", output_to_operand_aliasing={{3}: (10, {})} | custom-call | flops 1000 | bytes 1000 | tf_op jit(solution)/shard_map/pallas_call | solution.py:212
  189.2 6.7 %shard_map.118.refs_6_.refs_2_ = f32[2,5,256,256]{3,2,1,0:T(8,128)} custom-call(f32[2,16,256,256]{3,2,1,0:T(8,128)} %refs_0_.11, f32[2,5,384,256]{3,2,1,0:T(8,128)} %get-tuple-element.28.refs_0_.refs_1_, f32[2,5,192,128]{3,2,1,0:T(8,128)} %copy-done.3, f32[2,5,192,128]{3,2,1,0:T(8,128)} %copy-done.4, f32[2,5,64,256]{3,2,1,0:T(8,128)} %copy-done.20, ...), custom_call_target="tpu_custom_call" | custom-call | flops 1000 | bytes 1000 | tf_op jit(solution)/shard_map/pallas_call | solution.py:364
  195.8 1.5 collective-permute-start.24
  197.3 6.0 %collective-permute-start.12 = (f32[2,6,192,128]{3,2,1,0:T(8,128)}, f32[2,6,192,128]{3,2,1,0:T(8,128)S(1)}, u32[]{:S(2)}, u32[]{:S(2)}) collective-permute-start(f32[2,6,192,128]{3,2,1,0:T(8,128)} %get-tuple-element.38), channel_id=1, source_target_pairs={{0,1},{1,2},{2,3},{4,5},{5,6},{6,7},{8,9},{9,10},{10,11},{12,13},{... | collective-permute-start | bytes 3538952 | tf_op jit(solution)/shard_map/ppermute | solution.py:468
  206.0 36.5 %shard_map.122 = (f32[2,5,384,256]{3,2,1,0:T(8,128)}, f32[2,5,192,128]{3,2,1,0:T(8,128)}, f32[2,5,192,128]{3,2,1,0:T(8,128)}, f32[2,16,256,256]{3,2,1,0:T(8,128)}) custom-call(s32[8]{0:T(128)} %reshape.12.refs_0_, f32[2,16,256,256]{3,2,1,0:T(8,128)} %refs_0_.11, f32[2,5,64,256]{3,2,1,0:T(8,128)} %copy-done.8, ...), custom_call_target="tpu_custom_call", output_to_operand_aliasing={{3}: (10, {})} | custom-call | flops 1000 | bytes 1000 | tf_op jit(solution)/shard_map/pallas_call | solution.py:212
  242.4 5.3 %collective-permute-start.20 = (f32[2,5,192,128]{3,2,1,0:T(8,128)}, f32[2,5,192,128]{3,2,1,0:T(8,128)S(1)}, u32[]{:S(2)}, u32[]{:S(2)}) collective-permute-start(f32[2,5,192,128]{3,2,1,0:T(8,128)} %get-tuple-element.45), channel_id=1, source_target_pairs={{0,1},{1,2},{2,3},{4,5},{5,6},{6,7},{8,9},{9,10},{10,11},{12,13},{... | collective-permute-start | bytes 2949128 | tf_op jit(solution)/shard_map/ppermute | solution.py:468
  247.7 1.5 collective-permute-start.21
  250.9 5.1 %shard_map.119 = (f32[2,6,64,256]{3,2,1,0:T(8,128)}, f32[2,6,64,256]{3,2,1,0:T(8,128)}) custom-call(f32[2,6,384,256]{3,2,1,0:T(8,128)} %get-tuple-element.37.refs_0_.refs_1_, f32[2,6,384,256]{3,2,1,0:T(8,128)} %get-tuple-element.37.refs_0_.refs_1_, f32[2,6,192,128]{3,2,1,0:T(8,128)} %copy-done.1, f32[2,6,192,128]{3,2,1,0:T(8,128)} %copy-done.1, ...), custom_call_target="tpu_custom_call" | custom-call | flops 1000 | bytes 1000 | tf_op jit(solution)/shard_map/pallas_call | solution.py:318
  256.0 3.4 collective-permute-start.14
  261.7 4.5 shard_map.123
  266.2 4.6 collective-permute-start.22
  270.8 1.3 collective-permute-start.23
  272.1 21.7 %collective-permute-done.14.refs_4_ = f32[2,6,64,256]{3,2,1,0:T(8,128)S(1)} collective-permute-done((f32[2,6,64,256]{3,2,1,0:T(8,128)}, f32[2,6,64,256]{3,2,1,0:T(8,128)S(1)}, u32[]{:S(2)}, u32[]{:S(2)}) %collective-permute-start.14) | collective-permute-done | bytes 786464 | tf_op jit(solution)/shard_map/ppermute | solution.py:468
  293.8 4.4 collective-permute-done.15.refs_5_
  299.1 7.3 %shard_map.120.refs_6_.refs_3_ = f32[2,6,256,256]{3,2,1,0:T(8,128)} custom-call(f32[2,16,256,256]{3,2,1,0:T(8,128)} %refs_0_.11, f32[2,6,384,256]{3,2,1,0:T(8,128)} %get-tuple-element.37.refs_0_.refs_1_, f32[2,6,192,128]{3,2,1,0:T(8,128)} %copy-done.1, f32[2,6,192,128]{3,2,1,0:T(8,128)} %copy-done.2, f32[2,6,64,256]{3,2,1,0:T(8,128)} %copy-done.18, ...), custom_call_target="tpu_custom_call" | custom-call | flops 1000 | bytes 1000 | tf_op jit(solution)/shard_map/pallas_call | solution.py:364
  307.0 14.9 %collective-permute-done.22.refs_4_ = f32[2,5,64,256]{3,2,1,0:T(8,128)S(1)} collective-permute-done((f32[2,5,64,256]{3,2,1,0:T(8,128)}, f32[2,5,64,256]{3,2,1,0:T(8,128)S(1)}, u32[]{:S(2)}, u32[]{:S(2)}) %collective-permute-start.22) | collective-permute-done | bytes 655392 | tf_op jit(solution)/shard_map/ppermute | solution.py:468
  321.9 4.4 collective-permute-done.23.refs_5_
  327.1 6.9 %shard_map.124.refs_4_ = f32[2,5,256,256]{3,2,1,0:T(8,128)} custom-call(f32[2,16,256,256]{3,2,1,0:T(8,128)} %refs_0_.11, f32[2,5,384,256]{3,2,1,0:T(8,128)} %get-tuple-element.44.refs_0_.refs_1_, f32[2,5,192,128]{3,2,1,0:T(8,128)} %copy-done.5, f32[2,5,192,128]{3,2,1,0:T(8,128)} %collective-permute-done.21.refs_4_.refs_5_.refs_3_, ...), custom_call_target="tpu_custom_call" | custom-call | flops 1000 | bytes 1000 | tf_op jit(solution)/shard_map/pallas_call | solution.py:364
  335.7 40.3 %collective-permute-done.25.refs_6_ = f32[2,6,256,256]{3,2,1,0:T(8,128)S(1)} collective-permute-done((f32[2,6,256,256]{3,2,1,0:T(8,128)}, f32[2,6,256,256]{3,2,1,0:T(8,128)S(1)}, u32[]{:S(2)}, u32[]{:S(2)}) %collective-permute-start.25) | collective-permute-done | bytes 3145760 | tf_op jit(solution)/shard_map/ppermute | solution.py:517
  376.0 56.3 %collective-permute-done.26.refs_7_ = f32[2,5,256,256]{3,2,1,0:T(8,128)} collective-permute-done((f32[2,5,256,256]{3,2,1,0:T(8,128)}, f32[2,5,256,256]{3,2,1,0:T(8,128)}, u32[]{:S(2)}, u32[]{:S(2)}) %collective-permute-start.26) | collective-permute-done | bytes 2621472 | tf_op jit(solution)/shard_map/ppermute | solution.py:517
  432.3 18.4 %shard_map.125 = f32[2,16,256,256]{3,2,1,0:T(8,128)} custom-call(f32[32,64]{1,0:T(8,128)} %reshape.11.refs_0_, bf16[64,512]{1,0:T(8,128)(2,1)} %fusion.refs_1_, f32[2,5,256,256]{3,2,1,0:T(8,128)} %shard_map.118.refs_6_.refs_2_, f32[2,6,256,256]{3,2,1,0:T(8,128)} %shard_map.120.refs_6_.refs_3_, f32[2,5,256,256]{3,2,1,0:T(8,128)} %shard_map.124.refs_4_, ...), custom_call_target="tpu_custom_call" | custom-call | flops 1000 | bytes 1000 | tf_op jit(solution)/shard_map/pallas_call | solution.py:428
  451.3 7.7 %copy.21 = f32[2,16,256,256]{3,2,1,0:T(8,128)} copy(f32[2,16,256,256]{3,2,1,0:T(8,128)} %all-reduce.2.cloned.1.call-done) | data formatting | bytes 16777216
  (86 shorter events, 19.2 us)
Async XLA Ops:
  7.2 327.2 %copy-start = (f32[2,2,32,32]{3,2,1,0:T(8,128)S(1)}, f32[2,2,32,32]{3,2,1,0:T(8,128)}, u32[]{:S(2)}) copy-start(f32[2,2,32,32]{3,2,1,0:T(8,128)} %param.13) | copy-start | bytes 49156
  7.2 444.1 %all-reduce.2.cloned.1.call-start = ((), (), s32[]{:S(2)}) async-start(), calls=%async_computation | async-start | bytes 16777216 | tf_op jit(solution)/shard_map/psum | solution.py:508
  10.3 18.9 %collective-permute-start = (f32[2,5,64,256]{3,2,1,0:T(8,128)S(1)}, f32[2,5,64,256]{3,2,1,0:T(8,128)S(1)}, u32[]{:S(2)}, u32[]{:S(2)}) collective-permute-start(f32[2,5,64,256]{3,2,1,0:T(8,128)S(1)} %get-tuple-element.53), channel_id=1, source_target_pairs={{0,4},{4,8},{8,12},{1,5},{5,9},{9,13},{2,6},{6,10},{10,14},{3,7},{... | collective-permute-start | bytes 1966088 | tf_op jit(solution)/shard_map/ppermute | solution.py:468
  15.2 18.1 %collective-permute-start.1 = (f32[2,5,64,256]{3,2,1,0:T(8,128)S(1)}, f32[2,5,64,256]{3,2,1,0:T(8,128)S(1)}, u32[]{:S(2)}, u32[]{:S(2)}) collective-permute-start(f32[2,5,64,256]{3,2,1,0:T(8,128)S(1)} %get-tuple-element.52), channel_id=1, source_target_pairs={{4,0},{8,4},{12,8},{5,1},{9,5},{13,9},{6,2},{10,6},{14,10},{7,3},{... | collective-permute-start | bytes 1966088 | tf_op jit(solution)/shard_map/ppermute | solution.py:468
  29.2 4.2 copy-start.10
  39.2 10.0 %copy-start.26 = (s32[1,1,4,2]{2,3,1,0:T(2,128)S(1)}, s32[1,1,4,2]{2,3,1,0:T(2,128)}, u32[]{:S(2)}) copy-start(s32[1,1,4,2]{2,3,1,0:T(2,128)} %param.14) | copy-start | bytes 100
  39.2 10.8 %collective-permute-start.2 = (f32[2,5,192,128]{3,2,1,0:T(8,128)}, f32[2,5,192,128]{3,2,1,0:T(8,128)S(1)}, u32[]{:S(2)}, u32[]{:S(2)}) collective-permute-start(f32[2,5,192,128]{3,2,1,0:T(8,128)} %get-tuple-element.26), channel_id=1, source_target_pairs={{0,1},{1,2},{2,3},{4,5},{5,6},{6,7},{8,9},{9,10},{10,11},{12,13},{... | collective-permute-start | bytes 2949128 | tf_op jit(solution)/shard_map/ppermute | solution.py:468
  40.6 9.3 %collective-permute-start.3 = (f32[2,5,192,128]{3,2,1,0:T(8,128)}, f32[2,5,192,128]{3,2,1,0:T(8,128)}, u32[]{:S(2)}, u32[]{:S(2)}) collective-permute-start(f32[2,5,192,128]{3,2,1,0:T(8,128)} %get-tuple-element.27), channel_id=1, source_target_pairs={{1,0},{2,1},{3,2},{5,4},{6,5},{7,6},{9,8},{10,9},{11,10},{13,12},{... | collective-permute-start | bytes 2949128 | tf_op jit(solution)/shard_map/ppermute | solution.py:468
  44.4 58.1 %collective-permute-start.8 = (f32[2,6,64,256]{3,2,1,0:T(8,128)}, f32[2,6,64,256]{3,2,1,0:T(8,128)S(1)}, u32[]{:S(2)}, u32[]{:S(2)}) collective-permute-start(f32[2,6,64,256]{3,2,1,0:T(8,128)} %get-tuple-element.55), channel_id=1, source_target_pairs={{0,4},{4,8},{8,12},{1,5},{5,9},{9,13},{2,6},{6,10},{10,14},{3,7},{... | collective-permute-start | bytes 2359304 | tf_op jit(solution)/shard_map/ppermute | solution.py:468
  47.9 54.6 %collective-permute-start.9 = (f32[2,6,64,256]{3,2,1,0:T(8,128)S(1)}, f32[2,6,64,256]{3,2,1,0:T(8,128)S(1)}, u32[]{:S(2)}, u32[]{:S(2)}) collective-permute-start(f32[2,6,64,256]{3,2,1,0:T(8,128)S(1)} %get-tuple-element.54), channel_id=1, source_target_pairs={{4,0},{8,4},{12,8},{5,1},{9,5},{13,9},{6,2},{10,6},{14,10},{7,3},{... | collective-permute-start | bytes 2359304 | tf_op jit(solution)/shard_map/ppermute | solution.py:468
  49.9 0.9 copy-start.17
  87.3 26.6 %collective-permute-start.4 = (f32[2,5,192,128]{3,2,1,0:T(8,128)}, f32[2,5,192,128]{3,2,1,0:T(8,128)S(1)}, u32[]{:S(2)}, u32[]{:S(2)}) collective-permute-start(f32[2,5,192,128]{3,2,1,0:T(8,128)} %get-tuple-element.29), channel_id=1, source_target_pairs={{0,1},{1,2},{2,3},{4,5},{5,6},{6,7},{8,9},{9,10},{10,11},{12,13},{... | collective-permute-start | bytes 2949128 | tf_op jit(solution)/shard_map/ppermute | solution.py:468
  98.0 17.2 %collective-permute-start.5 = (f32[2,5,192,128]{3,2,1,0:T(8,128)}, f32[2,5,192,128]{3,2,1,0:T(8,128)S(1)}, u32[]{:S(2)}, u32[]{:S(2)}) collective-permute-start(f32[2,5,192,128]{3,2,1,0:T(8,128)} %get-tuple-element.30), channel_id=1, source_target_pairs={{1,0},{2,1},{3,2},{5,4},{6,5},{7,6},{9,8},{10,9},{11,10},{13,12},{... | collective-permute-start | bytes 2949128 | tf_op jit(solution)/shard_map/ppermute | solution.py:468
  99.3 26.0 %collective-permute-start.16 = (f32[2,5,64,256]{3,2,1,0:T(8,128)}, f32[2,5,64,256]{3,2,1,0:T(8,128)S(1)}, u32[]{:S(2)}, u32[]{:S(2)}) collective-permute-start(f32[2,5,64,256]{3,2,1,0:T(8,128)} %get-tuple-element.51), channel_id=1, source_target_pairs={{0,4},{4,8},{8,12},{1,5},{5,9},{9,13},{2,6},{6,10},{10,14},{3,7},{... | collective-permute-start | bytes 1966088 | tf_op jit(solution)/shard_map/ppermute | solution.py:468
  109.8 32.9 %collective-permute-start.10 = (f32[2,6,192,128]{3,2,1,0:T(8,128)}, f32[2,6,192,128]{3,2,1,0:T(8,128)S(1)}, u32[]{:S(2)}, u32[]{:S(2)}) collective-permute-start(f32[2,6,192,128]{3,2,1,0:T(8,128)} %get-tuple-element.33), channel_id=1, source_target_pairs={{0,1},{1,2},{2,3},{4,5},{5,6},{6,7},{8,9},{9,10},{10,11},{12,13},{... | collective-permute-start | bytes 3538952 | tf_op jit(solution)/shard_map/ppermute | solution.py:468
  112.6 31.6 %collective-permute-start.11 = (f32[2,6,192,128]{3,2,1,0:T(8,128)}, f32[2,6,192,128]{3,2,1,0:T(8,128)S(1)}, u32[]{:S(2)}, u32[]{:S(2)}) collective-permute-start(f32[2,6,192,128]{3,2,1,0:T(8,128)} %get-tuple-element.34), channel_id=1, source_target_pairs={{1,0},{2,1},{3,2},{5,4},{6,5},{7,6},{9,8},{10,9},{11,10},{13,12},{... | collective-permute-start | bytes 3538952 | tf_op jit(solution)/shard_map/ppermute | solution.py:468
  113.9 1.3 copy-start.3
  113.9 18.5 %collective-permute-start.17 = (f32[2,5,64,256]{3,2,1,0:T(8,128)}, f32[2,5,64,256]{3,2,1,0:T(8,128)S(1)}, u32[]{:S(2)}, u32[]{:S(2)}) collective-permute-start(f32[2,5,64,256]{3,2,1,0:T(8,128)} %get-tuple-element.50), channel_id=1, source_target_pairs={{4,0},{8,4},{12,8},{5,1},{9,5},{13,9},{6,2},{10,6},{14,10},{7,3},{... | collective-permute-start | bytes 1966088 | tf_op jit(solution)/shard_map/ppermute | solution.py:468
  115.2 1.0 copy-start.4
  120.8 67.4 %collective-permute-start.6 = (f32[2,5,64,256]{3,2,1,0:T(8,128)}, f32[2,5,64,256]{3,2,1,0:T(8,128)S(1)}, u32[]{:S(2)}, u32[]{:S(2)}) collective-permute-start(f32[2,5,64,256]{3,2,1,0:T(8,128)} %get-tuple-element.31), channel_id=1, source_target_pairs={{0,4},{4,8},{8,12},{1,5},{5,9},{9,13},{2,6},{6,10},{10,14},{3,7},{... | collective-permute-start | bytes 1966088 | tf_op jit(solution)/shard_map/ppermute | solution.py:468
  125.3 7.1 %copy-start.8 = (f32[2,5,64,256]{3,2,1,0:T(8,128)}, f32[2,5,64,256]{3,2,1,0:T(8,128)S(1)}, u32[]{:S(2)}) copy-start(f32[2,5,64,256]{3,2,1,0:T(8,128)S(1)} %collective-permute-done.16.refs_2_.refs_3_) | copy-start | bytes 1966084
  125.4 62.8 %collective-permute-start.7 = (f32[2,5,64,256]{3,2,1,0:T(8,128)}, f32[2,5,64,256]{3,2,1,0:T(8,128)S(1)}, u32[]{:S(2)}, u32[]{:S(2)}) collective-permute-start(f32[2,5,64,256]{3,2,1,0:T(8,128)} %get-tuple-element.32.refs_11_), channel_id=1, source_target_pairs={{4,0},{8,4},{12,8},{5,1},{9,5},{13,9},{6,2},{10,6},{14,10},{7,3},{... | collective-permute-start | bytes 1966088 | tf_op jit(solution)/shard_map/ppermute | solution.py:468
  138.3 66.4 %collective-permute-start.18 = (f32[2,5,192,128]{3,2,1,0:T(8,128)}, f32[2,5,192,128]{3,2,1,0:T(8,128)S(1)}, u32[]{:S(2)}, u32[]{:S(2)}) collective-permute-start(f32[2,5,192,128]{3,2,1,0:T(8,128)} %get-tuple-element.41), channel_id=1, source_target_pairs={{0,1},{1,2},{2,3},{4,5},{5,6},{6,7},{8,9},{9,10},{10,11},{12,13},{... | collective-permute-start | bytes 2949128 | tf_op jit(solution)/shard_map/ppermute | solution.py:468
  142.7 1.5 copy-start.13
  142.7 61.9 %collective-permute-start.19 = (f32[2,5,192,128]{3,2,1,0:T(8,128)}, f32[2,5,192,128]{3,2,1,0:T(8,128)S(1)}, u32[]{:S(2)}, u32[]{:S(2)}) collective-permute-start(f32[2,5,192,128]{3,2,1,0:T(8,128)} %get-tuple-element.42), channel_id=1, source_target_pairs={{1,0},{2,1},{3,2},{5,4},{6,5},{7,6},{9,8},{10,9},{11,10},{13,12},{... | collective-permute-start | bytes 2949128 | tf_op jit(solution)/shard_map/ppermute | solution.py:468
  144.2 1.0 copy-start.14
  188.1 1.0 copy-start.21
  195.8 130.4 %collective-permute-start.24 = (f32[2,5,256,256]{3,2,1,0:T(8,128)}, f32[2,5,256,256]{3,2,1,0:T(8,128)}, u32[]{:S(2)}, u32[]{:S(2)}) collective-permute-start(f32[2,5,256,256]{3,2,1,0:T(8,128)} %shard_map.118.refs_6_.refs_2_), channel_id=1, source_target_pairs={{0,16},{16,0},{1,17},{17,1},{2,18},{18,2},{3,19},{19,3},{4,20},{20... | collective-permute-start | bytes 7864328 | tf_op jit(solution)/shard_map/ppermute | solution.py:517
  197.3 52.0 %collective-permute-start.12 = (f32[2,6,192,128]{3,2,1,0:T(8,128)}, f32[2,6,192,128]{3,2,1,0:T(8,128)S(1)}, u32[]{:S(2)}, u32[]{:S(2)}) collective-permute-start(f32[2,6,192,128]{3,2,1,0:T(8,128)} %get-tuple-element.38), channel_id=1, source_target_pairs={{0,1},{1,2},{2,3},{4,5},{5,6},{6,7},{8,9},{9,10},{10,11},{12,13},{... | collective-permute-start | bytes 3538952 | tf_op jit(solution)/shard_map/ppermute | solution.py:468
  203.4 46.0 %collective-permute-start.13 = (f32[2,6,192,128]{3,2,1,0:T(8,128)}, f32[2,6,192,128]{3,2,1,0:T(8,128)S(1)}, u32[]{:S(2)}, u32[]{:S(2)}) collective-permute-start(f32[2,6,192,128]{3,2,1,0:T(8,128)} %get-tuple-element.36.refs_6_), channel_id=1, source_target_pairs={{1,0},{2,1},{3,2},{5,4},{6,5},{7,6},{9,8},{10,9},{11,10},{13,12},{... | collective-permute-start | bytes 3538952 | tf_op jit(solution)/shard_map/ppermute | solution.py:468
  204.7 0.9 copy-start.15
  204.7 1.3 copy-start.16
  242.4 18.3 %collective-permute-start.20 = (f32[2,5,192,128]{3,2,1,0:T(8,128)}, f32[2,5,192,128]{3,2,1,0:T(8,128)S(1)}, u32[]{:S(2)}, u32[]{:S(2)}) collective-permute-start(f32[2,5,192,128]{3,2,1,0:T(8,128)} %get-tuple-element.45), channel_id=1, source_target_pairs={{0,1},{1,2},{2,3},{4,5},{5,6},{6,7},{8,9},{9,10},{10,11},{12,13},{... | collective-permute-start | bytes 2949128 | tf_op jit(solution)/shard_map/ppermute | solution.py:468
  247.7 13.0 %collective-permute-start.21 = (f32[2,5,192,128]{3,2,1,0:T(8,128)}, f32[2,5,192,128]{3,2,1,0:T(8,128)}, u32[]{:S(2)}, u32[]{:S(2)}) collective-permute-start(f32[2,5,192,128]{3,2,1,0:T(8,128)} %get-tuple-element.46), channel_id=1, source_target_pairs={{1,0},{2,1},{3,2},{5,4},{6,5},{7,6},{9,8},{10,9},{11,10},{13,12},{... | collective-permute-start | bytes 2949128 | tf_op jit(solution)/shard_map/ppermute | solution.py:468
  249.3 1.0 copy-start.1
  249.3 1.5 copy-start.2
  256.0 37.8 %collective-permute-start.14 = (f32[2,6,64,256]{3,2,1,0:T(8,128)}, f32[2,6,64,256]{3,2,1,0:T(8,128)S(1)}, u32[]{:S(2)}, u32[]{:S(2)}) collective-permute-start(f32[2,6,64,256]{3,2,1,0:T(8,128)} %get-tuple-element.39), channel_id=1, source_target_pairs={{0,4},{4,8},{8,12},{1,5},{5,9},{9,13},{2,6},{6,10},{10,14},{3,7},{... | collective-permute-start | bytes 2359304 | tf_op jit(solution)/shard_map/ppermute | solution.py:468
  259.4 38.8 %collective-permute-start.15 = (f32[2,6,64,256]{3,2,1,0:T(8,128)}, f32[2,6,64,256]{3,2,1,0:T(8,128)S(1)}, u32[]{:S(2)}, u32[]{:S(2)}) collective-permute-start(f32[2,6,64,256]{3,2,1,0:T(8,128)} %get-tuple-element.40), channel_id=1, source_target_pairs={{4,0},{8,4},{12,8},{5,1},{9,5},{13,9},{6,2},{10,6},{14,10},{7,3},{... | collective-permute-start | bytes 2359304 | tf_op jit(solution)/shard_map/ppermute | solution.py:468
  260.7 1.0 copy-start.5
  266.2 55.7 %collective-permute-start.22 = (f32[2,5,64,256]{3,2,1,0:T(8,128)}, f32[2,5,64,256]{3,2,1,0:T(8,128)S(1)}, u32[]{:S(2)}, u32[]{:S(2)}) collective-permute-start(f32[2,5,64,256]{3,2,1,0:T(8,128)} %get-tuple-element.47), channel_id=1, source_target_pairs={{0,4},{4,8},{8,12},{1,5},{5,9},{9,13},{2,6},{6,10},{10,14},{3,7},{... | collective-permute-start | bytes 1966088 | tf_op jit(solution)/shard_map/ppermute | solution.py:468
  270.8 55.5 %collective-permute-start.23 = (f32[2,5,64,256]{3,2,1,0:T(8,128)}, f32[2,5,64,256]{3,2,1,0:T(8,128)S(1)}, u32[]{:S(2)}, u32[]{:S(2)}) collective-permute-start(f32[2,5,64,256]{3,2,1,0:T(8,128)} %get-tuple-element.48), channel_id=1, source_target_pairs={{4,0},{8,4},{12,8},{5,1},{9,5},{13,9},{6,2},{10,6},{14,10},{7,3},{... | collective-permute-start | bytes 1966088 | tf_op jit(solution)/shard_map/ppermute | solution.py:468
  293.8 4.4 copy-start.18
  306.4 28.7 %copy-start.24 = (s32[512]{0:T(512)S(1)}, s32[512]{0:T(512)}, u32[]{:S(2)}) copy-start(s32[512]{0:T(512)} %constant.45) | copy-start | bytes 6148
  306.4 28.7 %copy-start.25 = (s32[512]{0:T(512)S(1)}, s32[512]{0:T(512)}, u32[]{:S(2)}) copy-start(s32[512]{0:T(512)} %constant.44) | copy-start | bytes 6148
  306.4 69.7 %collective-permute-start.25 = (f32[2,6,256,256]{3,2,1,0:T(8,128)}, f32[2,6,256,256]{3,2,1,0:T(8,128)S(1)}, u32[]{:S(2)}, u32[]{:S(2)}) collective-permute-start(f32[2,6,256,256]{3,2,1,0:T(8,128)} %shard_map.120.refs_6_.refs_3_), channel_id=1, source_target_pairs={{0,16},{16,0},{1,17},{17,1},{2,18},{18,2},{3,19},{19,3},{4,20},{20... | collective-permute-start | bytes 9437192 | tf_op jit(solution)/shard_map/ppermute | solution.py:517
  321.9 4.4 copy-start.22
  334.0 98.3 %collective-permute-start.26 = (f32[2,5,256,256]{3,2,1,0:T(8,128)}, f32[2,5,256,256]{3,2,1,0:T(8,128)}, u32[]{:S(2)}, u32[]{:S(2)}) collective-permute-start(f32[2,5,256,256]{3,2,1,0:T(8,128)} %shard_map.124.refs_4_), channel_id=1, source_target_pairs={{0,16},{16,0},{1,17},{17,1},{2,18},{18,2},{3,19},{19,3},{4,20},{20... | collective-permute-start | bytes 7864328 | tf_op jit(solution)/shard_map/ppermute | solution.py:517
  376.0 56.3 %copy-start.12 = (f32[2,6,256,256]{3,2,1,0:T(8,128)}, f32[2,6,256,256]{3,2,1,0:T(8,128)S(1)}, u32[]{:S(2)}) copy-start(f32[2,6,256,256]{3,2,1,0:T(8,128)S(1)} %collective-permute-done.25.refs_6_) | copy-start | bytes 9437188
  (7 other events, 6.0 us)
Sparse Core Ops, SparseCore 0:
  249.4 201.8 all-reduce.1
